TPU v7x, 32 devices: a whole 2x2x4 slice. The times are simulated.
32 devices in a mesh: groups: 2 (over x), tile: 8 (over z, y), pos: 2 (over core).
Axes of the slice: x: 2, y: 2, z: 4, core: 2. Of those that a mesh axis runs over, the one named last changes fastest.
Arguments:
- object_field: float32 [4, 4096, 1024], P('groups', 'tile'), parts along dimension 0, may hold values from -6 to 6
- probe: float32 [8, 2, 128, 128], P('groups'), parts along dimension 0, may hold values from -3 to 3
- patterns: bfloat16 [1024, 128, 128], P(('groups', 'tile', 'pos')), parts along dimension 0, may hold values from 0.5 to 3.5
- scan_tile: int32 [1024, 1], P(('groups', 'tile', 'pos')), parts along dimension 0, may hold values from 0 to 7; in each aligned block of 32 rows (0 to 31, 32 to 63, ...) at most 8 rows name the same one
- scan_row: int32 [1024], P(('groups', 'tile', 'pos')), parts along dimension 0, may hold values from 0 to 384
- scan_col: int32 [1024], P(('groups', 'tile', 'pos')), parts along dimension 0, may hold values from 0 to 896
Outputs:
- object_step: float32 [4, 4096, 1024], P('groups', 'tile', 'pos'), parts along dimension 0
- probe_step: float32 [8, 2, 128, 128], P('groups'), parts along dimension 0
There are 2 independent parts, one for each index of `groups`. A program takes and returns all parts, laid end to end along the dimension named above; each array names one. Nothing has to cross between parts.
Inputs may be any that keep to these rules, and one draw needn't show every extreme that they name: `scan_tile`: among the 32 positions of one device at most 8 lie in one tile, and some device has exactly 8 in some tile.
All inputs are finite; a program needn't handle non-finite values.
Results may differ from a plain program's by a relative error of at most 0.0035.
The roundings to bfloat16 on the way count: a program that leaves them out, or rounds other values in their place, can miss the bound.
Values may be sent and summed in bfloat16 or wider, within the bound.
No kernel may reach another device: no remote copies, remote signals or barrier semaphores. Data moves between devices by JAX's collectives and lax.ppermute only.
A program may use at most 64 MiB of HBM per device.

v0:
```python
import math

import jax
import jax.numpy as jnp
from jax import lax
from jax.sharding import PartitionSpec as P

AMP_FLOOR = 0.5


def dft_parts(length):
    indices = jnp.arange(length, dtype=jnp.int32)
    products = indices[:, None] * indices[None, :] % length
    angles = products.astype(jnp.float32) * (-2.0 * math.pi / length)
    factor = 1.0 / math.sqrt(length)
    return (jnp.cos(angles) * factor, jnp.sin(angles) * factor)


def chirp_parts(length):
    offsets = jnp.arange(length, dtype=jnp.int32) - length // 2
    squares = offsets * offsets
    phases = (squares[:, None] + squares[None, :]).astype(jnp.float32) * (0.5 * math.pi / length)
    return (jnp.cos(phases), jnp.sin(phases))


def left_matrix(real_part, imag_part):
    upper = jnp.concatenate([real_part, -imag_part], 1)
    lower = jnp.concatenate([imag_part, real_part], 1)
    return jnp.concatenate([upper, lower], 0)


def right_matrix(real_part, imag_part):
    return jnp.concatenate([real_part, imag_part], 1)


def make_tables(length):
    dft_real, dft_imag = dft_parts(length)
    dft_real = dft_real.astype(jnp.bfloat16)
    dft_imag = dft_imag.astype(jnp.bfloat16)
    chirp_real, chirp_imag = chirp_parts(length)
    return (
        left_matrix(dft_real, dft_imag),
        right_matrix(dft_real, dft_imag),
        left_matrix(dft_real, -dft_imag),
        right_matrix(dft_real, -dft_imag),
        chirp_real,
        chirp_imag,
    )


def apply_left(matrix, field):
    batch_size = field.shape[0]
    length = field.shape[-1]
    stacked = field.reshape(batch_size, 2 * length, length)
    result = jnp.einsum("ab,nbc->nac", matrix, stacked, preferred_element_type=jnp.float32)
    return result.reshape(batch_size, 2, length, length)


def apply_right(matrix, field):
    length = field.shape[-1]
    result = jnp.einsum("nspq,qr->nspr", field, matrix, preferred_element_type=jnp.float32)
    real_out = result[:, 0, :, :length] - result[:, 1, :, length:]
    imag_out = result[:, 0, :, length:] + result[:, 1, :, :length]
    return jnp.stack([real_out, imag_out], 1)


def correct_patches(patches, measured, probe, weights, tables):
    forward_left, forward_right, back_left, back_right, chirp_real, chirp_imag = tables
    modes = probe.shape[0]
    number = patches.shape[0]
    length = probe.shape[-1]
    probe_real = probe[:, 0]
    probe_imag = probe[:, 1]
    lit_real = chirp_real * probe_real - chirp_imag * probe_imag
    lit_imag = chirp_real * probe_imag + chirp_imag * probe_real
    object_real = patches[:, 0].astype(jnp.float32)
    object_imag = patches[:, 1].astype(jnp.float32)
    exit_real = lit_real[:, None] * object_real[None] - lit_imag[:, None] * object_imag[None]
    exit_imag = lit_real[:, None] * object_imag[None] + lit_imag[:, None] * object_real[None]
    exit_wave = (
        jnp.stack([exit_real, exit_imag], 2)
        .astype(jnp.bfloat16)
        .reshape(modes * number, 2, length, length)
    )
    first_pass = apply_left(forward_left, exit_wave).astype(jnp.bfloat16)
    far_field = apply_right(forward_right, first_pass).reshape(modes, number, 2, length, length)
    intensity = jnp.sum(far_field * far_field, axis=(0, 2))
    factor = measured.astype(jnp.float32) / jnp.maximum(jnp.sqrt(intensity), AMP_FLOOR) - 1.0
    far_change = (
        (far_field * factor[None, :, None])
        .astype(jnp.bfloat16)
        .reshape(modes * number, 2, length, length)
    )
    back_first = apply_left(back_left, far_change).astype(jnp.bfloat16)
    near_field = apply_right(back_right, back_first).reshape(modes, number, 2, length, length)
    near_real = near_field[:, :, 0]
    near_imag = near_field[:, :, 1]
    weighting = weights[None, :, None, None]
    change_real = (chirp_real * near_real + chirp_imag * near_imag) * weighting
    change_imag = (chirp_real * near_imag - chirp_imag * near_real) * weighting
    step_real = jnp.sum(probe_real[:, None] * change_real + probe_imag[:, None] * change_imag, 0)
    step_imag = jnp.sum(probe_real[:, None] * change_imag - probe_imag[:, None] * change_real, 0)
    patch_steps = jnp.stack([step_real, step_imag], 1).astype(jnp.bfloat16)
    grad_real = jnp.sum(object_real[None] * change_real + object_imag[None] * change_imag, 1)
    grad_imag = jnp.sum(object_real[None] * change_imag - object_imag[None] * change_real, 1)
    return (patch_steps, jnp.stack([grad_real, grad_imag], 1))


def blockwise(patches, measured, probe, weights):
    length = probe.shape[-1]
    tables = make_tables(length)
    number = patches.shape[0]
    block_rows = math.gcd(8, number)
    block_count = number // block_rows

    def handle(pieces):
        return correct_patches(pieces[0], pieces[1], probe, pieces[2], tables)

    outputs = lax.map(
        handle,
        (
            patches.reshape(block_count, block_rows, 2, length, length),
            measured.reshape(block_count, block_rows, length, length),
            weights.reshape(block_count, block_rows),
        ),
    )
    return (outputs[0].reshape(number, 2, length, length), jnp.sum(outputs[1], 0))


def cut_patches(object_field, row_list, col_list, length):

    def extract(row_at, col_at):
        return lax.dynamic_slice(object_field, (0, row_at, col_at), (2, length, length))

    return jax.vmap(extract)(row_list, col_list).astype(jnp.bfloat16)


def add_patches(object_field, steps, row_list, col_list):
    length = steps.shape[-1]
    zero = jnp.int32(0)

    def add_one(index, current):
        row_at = row_list[index]
        col_at = col_list[index]
        window = lax.dynamic_slice(current, (zero, row_at, col_at), (2, length, length))
        window = window + steps[index].astype(jnp.float32)
        return lax.dynamic_update_slice(current, window, (zero, row_at, col_at))

    empty_strip = jnp.zeros(object_field.shape, jnp.float32)
    return lax.fori_loop(0, steps.shape[0], add_one, empty_strip)


def on_device(object_field, probe, patterns, scan_tile, scan_row, scan_col):
    length = probe.shape[-1]
    tile_count = lax.axis_size("tile")
    pos_count = lax.axis_size("pos")
    own_count = scan_row.shape[0]
    capacity = max(2, 2 * own_count // tile_count)
    slot_total = tile_count * capacity
    tile_ids = scan_tile[:, 0]
    positions = jnp.arange(own_count, dtype=jnp.int32)
    same_tile = tile_ids[:, None] == tile_ids[None, :]
    earlier = positions[None, :] < positions[:, None]
    slot_rank = jnp.sum(jnp.logical_and(same_tile, earlier).astype(jnp.int32), axis=1)
    slot_index = tile_ids * capacity + slot_rank
    entries = jnp.stack([scan_row, scan_col, jnp.ones_like(scan_row)], 1)
    requests = (
        jnp.zeros((slot_total, 3), jnp.int32)
        .at[slot_index]
        .set(entries)
        .reshape(tile_count, capacity, 3)
    )
    incoming = lax.all_to_all(requests, "tile", split_axis=0, concat_axis=0, tiled=True).reshape(
        slot_total, 3
    )
    tile_patches = cut_patches(object_field, incoming[:, 0], incoming[:, 1], length)
    arrived = lax.all_to_all(
        tile_patches.reshape(tile_count, capacity, 2, length, length),
        "tile",
        split_axis=0,
        concat_axis=0,
        tiled=True,
    ).reshape(slot_total, 2, length, length)
    own_patches = jnp.take(arrived, slot_index, axis=0)
    own_steps, gradient = blockwise(
        own_patches, patterns, probe, jnp.ones((own_count,), jnp.float32)
    )
    sending = jnp.zeros((slot_total, 2, length, length), jnp.bfloat16).at[slot_index].set(own_steps)
    sending = sending.reshape(tile_count, capacity, 2, length, length)
    strip_steps = lax.all_to_all(sending, "tile", split_axis=0, concat_axis=0, tiled=True).reshape(
        slot_total, 2, length, length
    )
    local_sum = add_patches(object_field, strip_steps, incoming[:, 0], incoming[:, 1])
    object_step = lax.psum_scatter(local_sum, "pos", scatter_dimension=2, tiled=True)
    total_scans = own_count * tile_count * pos_count
    probe_step = lax.psum(gradient, ("tile", "pos")) * (1.0 / math.sqrt(total_scans))
    return (object_step, probe_step)


def solution(mesh):
    placed = (
        P("groups", "tile", None),
        P("groups", None, None, None),
        P(("groups", "tile", "pos"), None, None),
        P(("groups", "tile", "pos"), None),
        P(("groups", "tile", "pos")),
        P(("groups", "tile", "pos")),
    )
    return jax.shard_map(
        on_device,
        mesh=mesh,
        in_specs=placed,
        out_specs=(P("groups", "tile", "pos"), P("groups", None, None, None)),
        check_vma=False,
    )
```

profile of v0, /device:TPU:0, one launch (start us, length us, event | category | flops | bytes accessed | tf_op | source)
XLA Modules:
  0.0 1248.0 jit_solution(13913496927485301370)
XLA Ops:
  11.9 7.3 all-to-all-start
  21.7 4.1 all-to-all-done
  26.5 174.3 %while.32 = (s32[]{:T(128)}, bf16[2,512,1024]{2,1,0:T(8,128)(2,1)S(1)}, s32[64,3]{0,1:T(4,128)S(1)}, bf16[64,2,128,128]{3,2,1,0:T(8,128)(2,1)}, s32[]{:T(128)}) while((s32[]{:T(128)}, bf16[2,512,1024]{2,1,0:T(8,128)(2,1)S(1)}, s32[64,3]{0,1:T(4,128)S(1)}, bf16[64,2,128,128]{3,2,1,0:T(8,128)(2,1)}, s32[]{:T(128)}) %tuple.118), condition=%wide.while_cond, body=%wide.while_body.sunk | while | flops 2 | bytes 132713 | solution.py:133
  200.7 4.7 all-to-all-start.1
  207.7 89.7 %all-to-all-done.1 = bf16[8,8,2,128,128]{4,3,2,1,0:T(8,128)(2,1)} async-done(((bf16[8,8,2,128,128]{4,3,2,1,0:T(8,128)(2,1)}), bf16[8,8,2,128,128]{4,3,2,1,0:T(8,128)(2,1)}, u32[]{:S(2)}, u32[]{:S(2)}) %all-to-all-start.1) | async-done | bytes 4194336 | tf_op jit(solution)/shard_map/all_to_all | solution.py:177
  302.2 230.2 %while.33 = (s32[]{:T(128)}, bf16[4,8,2,128,128]{4,3,2,1,0:T(8,128)(2,1)}, f32[4,4,2,128,128]{4,3,2,1,0:T(8,128)}, f32[4,2,128,128]{2,3,0,1:T(8,128)S(1)}, bf16[...) while((s32[]{:T(128)}, ...), condition=%wide.region_8.9_spmd.clone.clone.clone, body=%wide.region_2.8_spmd.clone.clone.clone.sunk | while | flops 2179776512 | bytes 128190160 | solution.py:119
  304.7 4.4 subtract_convert_fusion.2
  309.2 4.8 pad_maximum_fusion.9
  328.4 3.8 copy.91
  347.0 4.2 fusion.65
  362.3 4.4 subtract_convert_fusion.2
  366.7 4.8 pad_maximum_fusion.9
  386.0 3.8 copy.91
  404.6 4.2 fusion.65
  419.9 4.4 subtract_convert_fusion.2
  424.3 4.8 pad_maximum_fusion.9
  443.6 3.8 copy.91
  462.1 4.2 fusion.65
  477.4 4.4 subtract_convert_fusion.2
  481.8 4.8 pad_maximum_fusion.9
  501.1 3.8 copy.91
  519.7 4.2 fusion.65
  535.4 6.3 scatter_fusion
  541.7 4.7 all-to-all-start.2
  547.5 96.3 %all-to-all-done.2 = bf16[8,8,2,128,128]{4,3,2,1,0:T(8,128)(2,1)} async-done(((bf16[8,8,2,128,128]{4,3,2,1,0:T(8,128)(2,1)}), bf16[8,8,2,128,128]{4,3,2,1,0:T(8,128)(2,1)}, u32[]{:S(2)}, u32[]{:S(2)}) %all-to-all-start.2) | async-done | bytes 4194336 | tf_op jit(solution)/shard_map/all_to_all | solution.py:190
  646.2 568.2 %while.31 = (s32[]{:T(128)}, f32[2,512,1024]{2,1,0:T(8,128)}, s32[64]{0:T(128)S(1)}, s32[64]{0:T(128)S(1)}, bf16[64,2,128,128]{3,2,1,0:T(8,128)(2,1)}, /*index=5*/s32[]{:T(128)}, s32[]{:T(128)}, s32[]{:T(128)}, s32[]{:T(128)}) while((s32[]{:T(128)}, f32[2,512,1024]{2,1,0:T(8,128)}, s32[64]{0:T(128)S(1)}, s32[64]{0:T(128)S(1)}, ...), condition=%wide.region_11.12_spmd, body=%wide.region_10.11_spmd.sunk | while | flops 65544 | bytes 590025 | solution.py:150
  722.8 3.7 dynamic_update_slice.32
  935.8 3.7 dynamic_update_slice.32
  945.0 3.7 dynamic_update_slice.32
  1148.8 3.7 dynamic_update_slice.32
  1158.0 3.7 dynamic_update_slice.32
  1216.3 24.2 %reduce-scatter.2.cloned.1.call-done = f32[2,512,512]{2,1,0:T(8,128)} async-done(((f32[2,512,1024]{2,1,0:T(8,128)}), f32[2,512,512]{2,1,0:T(8,128)}) %reduce-scatter.2.cloned.1.call-update) | async-done | bytes 2097168 | tf_op jit(solution)/shard_map/reduce_scatter | solution.py:194
  (622 shorter events, 695.2 us)
Async XLA Ops:
  9.6 196.2 %copy-start.5 = (s32[32,1]{0,1:T(1,128)}, s32[32,1]{0,1:T(1,128)S(1)}, u32[]{:S(2)}) copy-start(s32[32,1]{0,1:T(1,128)S(1)} %get-tuple-element.468) | copy-start | bytes 388
  11.9 13.9 %all-to-all-start = ((s32[8,8,3]{1,2,0:T(4,128)}), s32[8,8,3]{1,2,0:T(4,128)S(1)}, u32[]{:S(2)}, u32[]{:S(2)}) async-start(s32[8,8,3]{1,2,0:T(4,128)} %copy.68), calls=%async_computation | async-start | bytes 32768 | tf_op jit(solution)/shard_map/all_to_all | solution.py:173
  200.7 4.8 copy-start.4
  200.7 96.7 %all-to-all-start.1 = ((bf16[8,8,2,128,128]{4,3,2,1,0:T(8,128)(2,1)}), bf16[8,8,2,128,128]{4,3,2,1,0:T(8,128)(2,1)}, u32[]{:S(2)}, u32[]{:S(2)}) async-start(bf16[8,8,2,128,128]{4,3,2,1,0:T(8,128)(2,1)} %bitcast.192), calls=%async_computation.1 | async-start | bytes 8388608 | tf_op jit(solution)/shard_map/all_to_all | solution.py:177
  302.2 1.1 copy-start.1
  353.8 1.2 copy-start
  358.0 1.7 copy-start.2
  359.7 1.1 copy-start.1
  411.4 1.2 copy-start
  415.6 1.7 copy-start.2
  417.3 1.1 copy-start.1
  469.0 1.2 copy-start
  473.2 1.7 copy-start.2
  474.9 1.1 copy-start.1
  526.5 1.2 copy-start
  530.7 1.7 copy-start.2
  532.4 3.0 copy-start.6
  541.7 4.7 copy-start.3
  541.7 102.0 %all-to-all-start.2 = ((bf16[8,8,2,128,128]{4,3,2,1,0:T(8,128)(2,1)}), bf16[8,8,2,128,128]{4,3,2,1,0:T(8,128)(2,1)}, u32[]{:S(2)}, u32[]{:S(2)}) async-start(bf16[8,8,2,128,128]{4,3,2,1,0:T(8,128)(2,1)} %bitcast.186), calls=%async_computation.2 | async-start | bytes 8388608 | tf_op jit(solution)/shard_map/all_to_all | solution.py:190
  546.4 668.1 %all-reduce.2.cloned.1.call-start = ((), (), s32[]{:S(2)}) async-start(), calls=%async_computation.5 | async-start | bytes 1048576 | tf_op jit(solution)/shard_map/psum | solution.py:196
  547.4 693.1 %reduce-scatter.2.cloned.1.call-start = ((), (), s32[]{:S(2)}) async-start(), calls=%async_computation.4 | async-start | bytes 6291456 | tf_op jit(solution)/shard_map/reduce_scatter | solution.py:194
  643.7 2.5 copy-start.7
  643.7 2.5 copy-start.8
Sparse Core Ops, SparseCore 0:
  551.6 139.4 all-reduce.1
Sparse Core Ops, SparseCore 1:
  1214.5 26.0 reduce-scatter.1
where the time goes:
time: 1260 us; the launch traced here: 1250 us
  local copies, waits for them, and re-layouts  566 us (45%)
  waiting for transfers between devices  214 us (17%)
  loops' own time  212 us (17%)
  other arithmetic  180 us (14%)
  matrix products  43 us (3%)
  starting transfers between devices  16.7 us (1%)
  between operations  15.6 us (1%)
    dynamic_update_slice x64, local copies, waits for them, and re-layouts, add_one(): return lax.dynamic_update_slice(current, window, (zero, row_at, col_at))  216 us
    another operation x1, loops' own time, add_patches(): return lax.fori_loop(0, steps.shape[0], add_one, empty_strip)  212 us
    gather x192, local copies, waits for them, and re-layouts  174 us
    all_to_all x1, waiting for transfers between devices, on_device(): lax.all_to_all(sending, 'tile', split_axis=0, concat_axis=0, tiled=True)  96.3 us
    all_to_all x1, waiting for transfers between devices, on_device(): lax.all_to_all(tile_patches.reshape(tile_count, capacity, 2, length, leng...  89.7 us
    add x64, other arithmetic, add_one(): window = window + steps[index].astype(jnp.float32)  69.2 us
    dynamic_slice x64, local copies, waits for them, and re-layouts, add_one(): row_at = row_list[index]  35.9 us
    dynamic_slice x64, local copies, waits for them, and re-layouts, add_one(): col_at = col_list[index]  35.5 us
  transfers between devices with their start and end apart: 5, of which 4 were waited for; matrix products, arithmetic and copies ran while one was open for 29% of the time, Pallas kernels for 0%

commit v1 on v0

v1 whole, which is shorter than its diff:
```python
import functools
import math

import jax
import jax.numpy as jnp
import numpy as np
from jax import lax
from jax.experimental import pallas as pl
from jax.experimental.pallas import tpu as pltpu
from jax.sharding import PartitionSpec as P

AMP_FLOOR = 0.5
HEAD = 16
DIGIT = 16
LANES = 128
BAND = 16
MAX_STAGES = 3


def dft_tables(length):
    indices = np.arange(length, dtype=np.int32)
    products = indices[:, None] * indices[None, :] % length
    angles = products.astype(np.float32) * np.float32(-2.0 * math.pi / length)
    factor = np.float32(1.0 / math.sqrt(length))
    real = (np.cos(angles) * factor).astype(jnp.bfloat16)
    imag = (np.sin(angles) * factor).astype(jnp.bfloat16)
    forward = np.block([[real, -imag], [imag, real]])
    backward = np.block([[real, imag], [-imag, real]])
    return np.stack([forward, backward])


def chirp_table(length):
    offsets = np.arange(length, dtype=np.int32) - length // 2
    squares = offsets * offsets
    phases = (squares[:, None] + squares[None, :]).astype(np.float32) * np.float32(
        0.5 * math.pi / length
    )
    return np.stack([np.cos(phases), np.sin(phases)]).astype(np.float32)


def pack_kernel(tile_count, capacity, tile_ref, row_ref, col_ref, pat_ref, *rest):
    blocks, count_ref, source_ref = rest[:tile_count], rest[tile_count], rest[tile_count + 1]
    number, length = pat_ref.shape[0], pat_ref.shape[1]
    me = lax.axis_index("tile")
    for hop in range(tile_count):
        count_ref[hop] = 0

    def place(index, carry):
        hop = tile_ref[index] ^ me
        rank = count_ref[hop]
        count_ref[hop] = rank + 1
        source_ref[hop * capacity + rank] = index
        return carry

    lax.fori_loop(0, number, place, 0)
    lane = lax.broadcasted_iota(jnp.int32, (HEAD, LANES), 1)
    line = lax.broadcasted_iota(jnp.int32, (HEAD, LANES), 0)
    for hop in range(tile_count):
        count = count_ref[hop]
        head = jnp.where(line == 4, count, 0)
        for rank in range(capacity):
            valid = rank < count
            index = jnp.where(valid, source_ref[hop * capacity + rank], 0)
            row, col = row_ref[index], col_ref[index]

            @pl.when(valid)
            def _(hop=hop, rank=rank, index=index):
                blocks[hop][rank * length : (rank + 1) * length, :] = pat_ref[index]

            digits = jnp.where(
                line == 0,
                row // DIGIT,
                jnp.where(
                    line == 1,
                    row % DIGIT,
                    jnp.where(line == 2, col // DIGIT, jnp.where(line == 3, col % DIGIT, 0)),
                ),
            )
            head = head + jnp.where((lane == rank) & valid, digits, 0)
        blocks[hop][capacity * length :, :] = head.astype(jnp.float32).astype(jnp.bfloat16)


def pack(patterns, tile_ids, rows, cols, tile_count, capacity):
    length = patterns.shape[-1]
    block = jax.ShapeDtypeStruct((capacity * length + HEAD, length), jnp.bfloat16)
    smem = pl.BlockSpec(memory_space=pltpu.SMEM)
    vmem = pl.BlockSpec(memory_space=pltpu.VMEM)
    return pl.pallas_call(
        functools.partial(pack_kernel, tile_count, capacity),
        out_shape=[block] * tile_count,
        in_specs=[smem, smem, smem, vmem],
        out_specs=[vmem] * tile_count,
        scratch_shapes=[
            pltpu.SMEM((tile_count,), jnp.int32),
            pltpu.SMEM((tile_count * capacity,), jnp.int32),
        ],
        compiler_params=pltpu.CompilerParams(vmem_limit_bytes=24 * 2**20),
        name="pack_patterns",
    )(tile_ids, rows, cols, patterns)


def step_kernel(block_count, capacity, scale, width, object_hbm, probe_ref, dft_ref, chirp_ref, *rest):
    blocks = rest[:block_count]
    keep_hbm, send_hbm, grad_keep_hbm, grad_send_hbm = rest[block_count : block_count + 4]
    (
        field,
        total,
        pats,
        heads,
        corners,
        list_row,
        list_col,
        list_pat,
        lit,
        grad,
        patch,
        wide,
        tall,
        far,
        in_sem,
        out_sem,
    ) = rest[block_count + 4 :]
    modes, _, length, _ = probe_ref.shape
    rows, columns = object_hbm.shape[1:]
    block_rows = capacity * length + HEAD
    bands = length // BAND
    pos = lax.axis_index("pos")

    column_tiles = columns // LANES
    load_field = [
        pltpu.make_async_copy(
            object_hbm.at[:, :, tile * LANES : (tile + 1) * LANES],
            field.at[:, tile, 0:rows, :],
            in_sem.at[block_count + 1 + tile],
        )
        for tile in range(column_tiles)
    ]
    loads = [
        pltpu.make_async_copy(
            blocks[b], pats.at[b * block_rows : (b + 1) * block_rows], in_sem.at[b]
        )
        for b in range(block_count)
    ]
    for load in loads + load_field:
        load.start()

    def clear(index, carry):
        at = pl.ds(pl.multiple_of(index * 8, 8), 8)
        for plane in range(2):
            for tile in range(column_tiles + 1):
                total[plane, tile, at, :] = jnp.zeros((8, LANES), jnp.float32)
        return carry

    lax.fori_loop(0, total.shape[2] // 8, clear, 0)
    for mode in range(modes):
        for band in range(bands):
            at = pl.ds(band * BAND, BAND)
            cr, ci = chirp_ref[0, at, :], chirp_ref[1, at, :]
            pr, pi = probe_ref[mode, 0, at, :], probe_ref[mode, 1, at, :]
            lit[mode, 0, at, :] = cr * pr - ci * pi
            lit[mode, 1, at, :] = cr * pi + ci * pr
            grad[pl.ds((2 * mode) * length + band * BAND, BAND), :] = jnp.zeros_like(cr)
            grad[pl.ds((2 * mode + 1) * length + band * BAND, BAND), :] = jnp.zeros_like(cr)

    for load in loads:
        load.wait()
    for b in range(block_count):
        heads[b * HEAD : (b + 1) * HEAD, :] = (
            pats[(b + 1) * block_rows - HEAD : (b + 1) * block_rows, :]
            .astype(jnp.float32)
            .astype(jnp.int32)
        )
    fetch = pltpu.make_async_copy(heads, corners, in_sem.at[block_count])
    fetch.start()
    fetch.wait()

    number = jnp.int32(0)
    for b in range(block_count):

        def note(rank, at, b=b):
            first = b * HEAD
            list_row[at] = corners[first, rank] * DIGIT + corners[first + 1, rank]
            list_col[at] = corners[first + 2, rank] * DIGIT + corners[first + 3, rank]
            list_pat[at] = b * block_rows + rank * length
            return at + 1

        number = lax.fori_loop(0, corners[b * HEAD + 4, 0], note, number)
    for load in load_field:
        load.wait()

    lane = lax.broadcasted_iota(jnp.int32, (BAND, LANES), 1)

    def visit(turn, carry):
        items = []
        for u in range(width):
            index = turn * width + u
            valid = index < number
            index = jnp.where(valid, index, turn * width)
            col = list_col[index]
            shift = col % LANES
            items.append(
                (
                    u,
                    list_row[index],
                    col // LANES,
                    shift,
                    pl.multiple_of(list_pat[index], LANES),
                    jnp.where(valid, jnp.float32(1.0), jnp.float32(0.0)),
                )
            )
        for u, row, col, shift, _, _ in items:
            back = (LANES - shift) % LANES
            inside = lane < LANES - shift
            for band in range(bands):
                at = pl.ds(band * BAND, BAND)
                at_field = pl.ds(row + band * BAND, BAND)
                planes = []
                for plane in range(2):
                    left = pltpu.roll(field[plane, col, at_field, :], back, 1)
                    right = pltpu.roll(field[plane, col + 1, at_field, :], back, 1)
                    cell = jnp.where(inside, left, right).astype(jnp.bfloat16).astype(jnp.float32)
                    patch[u, plane, at, :] = cell
                    planes.append(cell)
                pr, pi = planes
                for mode in range(modes):
                    lr, li = lit[mode, 0, at, :], lit[mode, 1, at, :]
                    lanes = pl.ds(mode * length, length)
                    wide[u, pl.ds(band * BAND, BAND), lanes] = (lr * pr - li * pi).astype(
                        jnp.bfloat16
                    )
                    wide[u, pl.ds(length + band * BAND, BAND), lanes] = (
                        lr * pi + li * pr
                    ).astype(jnp.bfloat16)

        def columns_pass(u, table):
            for mode in range(0, modes, 2):
                both = min(2, modes - mode)
                out = jnp.dot(
                    dft_ref[table],
                    wide[u, :, mode * length : (mode + both) * length],
                    preferred_element_type=jnp.float32,
                ).astype(jnp.bfloat16)
                for q in range(both):
                    at = pl.ds((mode + q) * length, length)
                    tall[u, at, 0:length] = out[0:length, q * length : (q + 1) * length]
                    tall[u, at, length : 2 * length] = out[
                        length : 2 * length, q * length : (q + 1) * length
                    ]

        def rows_pass(u, table):
            far[u] = jnp.dot(tall[u], dft_ref[table], preferred_element_type=jnp.float32)

        for item in items:
            columns_pass(item[0], 0)
        for item in items:
            rows_pass(item[0], 1)
        for u, _, _, _, source, weight in items:
            for band in range(bands):
                waves = []
                bright = None
                for mode in range(modes):
                    at = pl.ds(mode * length + band * BAND, BAND)
                    fr, fi = far[u, at, 0:length], far[u, at, length : 2 * length]
                    waves.append((fr, fi))
                    power = fr * fr + fi * fi
                    bright = power if bright is None else bright + power
                measured = pats[pl.ds(source + band * BAND, BAND), :].astype(jnp.float32)
                inverse = jnp.minimum(lax.rsqrt(bright), 1.0 / AMP_FLOOR)
                factor = (measured * inverse - 1.0) * weight
                for mode in range(modes):
                    fr, fi = waves[mode]
                    lanes = pl.ds(mode * length, length)
                    wide[u, pl.ds(band * BAND, BAND), lanes] = (fr * factor).astype(jnp.bfloat16)
                    wide[u, pl.ds(length + band * BAND, BAND), lanes] = (fi * factor).astype(
                        jnp.bfloat16
                    )
        for item in items:
            columns_pass(item[0], 1)
        for item in items:
            rows_pass(item[0], 0)
        for band in range(bands):
            at = pl.ds(band * BAND, BAND)
            steps = [[None, None] for _ in items]
            for mode in range(modes):
                at_far = pl.ds(mode * length + band * BAND, BAND)
                at_gr = pl.ds((2 * mode) * length + band * BAND, BAND)
                at_gi = pl.ds((2 * mode + 1) * length + band * BAND, BAND)
                lr, li = lit[mode, 0, at, :], lit[mode, 1, at, :]
                gr, gi = grad[at_gr, :], grad[at_gi, :]
                for item in items:
                    u = item[0]
                    nr, ni = far[u, at_far, 0:length], far[u, at_far, length : 2 * length]
                    pr, pi = patch[u, 0, at, :], patch[u, 1, at, :]
                    sr, si = lr * nr + li * ni, lr * ni - li * nr
                    if mode:
                        sr, si = steps[u][0] + sr, steps[u][1] + si
                    steps[u] = [sr, si]
                    gr = gr + (pr * nr + pi * ni)
                    gi = gi + (pr * ni - pi * nr)
                grad[at_gr, :] = gr
                grad[at_gi, :] = gi
            for u, row, col, shift, _, _ in items:
                at_field = pl.ds(row + band * BAND, BAND)
                for plane in range(2):
                    step = steps[u][plane].astype(jnp.bfloat16).astype(jnp.float32)
                    moved = pltpu.roll(step, shift, 1)
                    total[plane, col, at_field, :] += jnp.where(lane >= shift, moved, 0.0)
                    total[plane, col + 1, at_field, :] += jnp.where(lane < shift, moved, 0.0)
        return carry

    lax.fori_loop(0, (number + width - 1) // width, visit, 0)

    for mode in range(modes):
        for band in range(bands):
            at = pl.ds(band * BAND, BAND)
            at_gr = pl.ds((2 * mode) * length + band * BAND, BAND)
            at_gi = pl.ds((2 * mode + 1) * length + band * BAND, BAND)
            cr, ci = chirp_ref[0, at, :] * scale, chirp_ref[1, at, :] * scale
            gr, gi = grad[at_gr, :], grad[at_gi, :]
            grad[at_gr, :] = cr * gr + ci * gi
            grad[at_gi, :] = cr * gi - ci * gr
    half = column_tiles // 2
    grad_half = grad.shape[0] // 2
    stores = []
    for grad_out, out, side in (
        (grad_send_hbm, send_hbm, 1 - pos),
        (grad_keep_hbm, keep_hbm, pos),
    ):
        stores.append(
            pltpu.make_async_copy(
                grad.at[pl.ds(pl.multiple_of(side * grad_half, 8), grad_half), :],
                grad_out,
                out_sem.at[len(stores)],
            )
        )
        for tile in range(half):
            stores.append(
                pltpu.make_async_copy(
                    total.at[:, side * half + tile, 0:rows, :],
                    out.at[:, :, tile * LANES : (tile + 1) * LANES],
                    out_sem.at[len(stores)],
                )
            )
    for store in stores:
        store.start()
    for store in stores:
        store.wait()


def step(object_field, probe, blocks, tables, scale, capacity):
    modes, _, length, _ = probe.shape
    rows, columns = object_field.shape[1:]
    count = len(blocks)
    width = 2
    slots = count * capacity
    vmem = pl.BlockSpec(memory_space=pltpu.VMEM)
    hbm = pl.BlockSpec(memory_space=pl.ANY)
    f32, bf16 = jnp.float32, jnp.bfloat16
    padded = (2, columns // LANES + 1, rows + 8, LANES)
    work = slots * modes * 4 * 8 * length**3
    return pl.pallas_call(
        functools.partial(step_kernel, count, capacity, scale, width),
        out_shape=[
            jax.ShapeDtypeStruct((2, rows, columns // 2), f32),
            jax.ShapeDtypeStruct((2, rows, columns // 2), f32),
            jax.ShapeDtypeStruct((modes * length, length), f32),
            jax.ShapeDtypeStruct((modes * length, length), f32),
        ],
        in_specs=[hbm, vmem, vmem, vmem] + [hbm] * count,
        out_specs=[hbm] * 4,
        scratch_shapes=[
            pltpu.VMEM(padded, f32),
            pltpu.VMEM(padded, f32),
            pltpu.VMEM((count * (capacity * length + HEAD), length), bf16),
            pltpu.VMEM((count * HEAD, LANES), jnp.int32),
            pltpu.SMEM((count * HEAD, LANES), jnp.int32),
            pltpu.SMEM((slots,), jnp.int32),
            pltpu.SMEM((slots,), jnp.int32),
            pltpu.SMEM((slots,), jnp.int32),
            pltpu.VMEM((modes, 2, length, length), f32),
            pltpu.VMEM((2 * modes * length, length), f32),
            pltpu.VMEM((width, 2, length, length), f32),
            pltpu.VMEM((width, 2 * length, modes * length), bf16),
            pltpu.VMEM((width, modes * length, 2 * length), bf16),
            pltpu.VMEM((width, modes * length, 2 * length), f32),
            pltpu.SemaphoreType.DMA((count + 1 + columns // LANES,)),
            pltpu.SemaphoreType.DMA((2 + columns // LANES,)),
        ],
        compiler_params=pltpu.CompilerParams(vmem_limit_bytes=40 * 2**20),
        cost_estimate=pl.CostEstimate(
            flops=work, bytes_accessed=16 * 2**20, transcendentals=slots * length**2
        ),
        name="gradient_step",
    )(object_field, probe, *tables, *blocks)


def sum_over_scans(keep, send, tile_count):
    other = [(0, 1), (1, 0)]
    part = keep + lax.ppermute(send, "pos", other)
    rows, length = part.shape
    pieces = part.reshape(tile_count, rows // tile_count, length)
    mine = jnp.sum(lax.all_to_all(pieces, "tile", split_axis=0, concat_axis=0, tiled=True), 0)
    copies = jnp.broadcast_to(mine[None], pieces.shape)
    whole = lax.all_to_all(copies, "tile", split_axis=0, concat_axis=0, tiled=True)
    whole = whole.reshape(rows, length)
    return (whole, lax.ppermute(whole, "pos", other))


def on_device(object_field, probe, patterns, scan_tile, scan_row, scan_col):
    tile_count = lax.axis_size("tile")
    pos_count = lax.axis_size("pos")
    number, length = patterns.shape[0], patterns.shape[-1]
    capacity = max(2, 2 * number // tile_count)
    scale = 1.0 / math.sqrt(number * tile_count * pos_count)
    tables = (jnp.asarray(dft_tables(length)), jnp.asarray(chirp_table(length)))
    blocks = pack(patterns, scan_tile[:, 0], scan_row, scan_col, tile_count, capacity)
    arrived = [blocks[0]]
    for hop in range(1, tile_count):
        arrived.append(
            lax.ppermute(blocks[hop], "tile", [(i, i ^ hop) for i in range(tile_count)])
        )
    cuts = [0, tile_count // 2, tile_count * 3 // 4, tile_count]
    parts = [
        step(object_field, probe, arrived[a:b], tables, scale, capacity)
        for a, b in zip(cuts[:-1], cuts[1:])
    ]
    keep, send, grad_keep, grad_send = [sum(group[1:], group[0]) for group in zip(*parts)]
    mine, theirs = sum_over_scans(grad_keep, grad_send, tile_count)
    first = lax.axis_index("pos") == 0
    grad = jnp.concatenate([jnp.where(first, mine, theirs), jnp.where(first, theirs, mine)])
    object_step = keep + lax.ppermute(send, "pos", [(0, 1), (1, 0)])
    return (object_step, grad.reshape(probe.shape))


def solution(mesh):
    placed = (
        P("groups", "tile", None),
        P("groups", None, None, None),
        P(("groups", "tile", "pos"), None, None),
        P(("groups", "tile", "pos"), None),
        P(("groups", "tile", "pos")),
        P(("groups", "tile", "pos")),
    )
    return jax.shard_map(
        on_device,
        mesh=mesh,
        in_specs=placed,
        out_specs=(P("groups", "tile", "pos"), P("groups", None, None, None)),
        check_vma=False,
    )
```

time: 1260 us -> 142 us (0.11)
  local copies, waits for them, and re-layouts: 566 us -> 9.6 us
  loops' own time: 212 us -> 0 us
  waiting for transfers between devices: 214 us -> 24.7 us
  other arithmetic: 180 us -> 7.65 us
  blocking collectives: 0 us -> 45.8 us
  matrix products: 43 us -> 0 us
  Pallas kernels: 0 us -> 35.7 us
  between operations: 15.6 us -> 0.77 us
    dynamic_update_slice x64 -> x0, local copies, waits for them, and re-layouts: 216 us -> none  [add_one(): return lax.dynamic_update_slice(current, window, (zero, row_at, col_at))]
    another operation x3 -> x0, loops' own time: 212 us -> none  [the longest x1 212 us: add_patches(): return lax.fori_loop(0, steps.shape[0], add_one, empty_strip)]
    all_to_all x3 -> x0, waiting for transfers between devices: 190 us -> none  [the longest x1 96.3 us: on_device(): lax.all_to_all(sending, 'tile', split_axis=0, concat_axis=0, tiled=True)]
    gather x193 -> x0, local copies, waits for them, and re-layouts: 177 us -> none
    add x68 -> x4, other arithmetic: 86.2 us -> 6.76 us  [the longest x1 4.57 us: on_device(): object_step = keep + lax.ppermute(send, 'pos', [(0, 1), (1, 0)])]
    dynamic_slice x136 -> x0, local copies, waits for them, and re-layouts: 76.8 us -> none  [the longest x64 35.9 us: add_one(): row_at = row_list[index]]
    convert_element_type x28 -> x0, local copies, waits for them, and re-layouts: 68.8 us -> none  [the longest x8 27.8 us: correct_patches(): far_change = (far_field * factor[None, :, None]).astype(jnp.bfloat16).res...]
    all_to_all x0 -> x2, blocking collectives: none -> 45.8 us  [the longest x1 33.4 us: sum_over_scans(): lax.all_to_all(pieces, 'tile', split_axis=0, concat_axis=0, tiled=True)]
  transfers between devices with their start and end apart: 5 -> 10, of which waited for: 4 -> 4; matrix products, arithmetic and copies ran while one was open for 29% -> 1% of each run, Pallas kernels for 0% -> 12%
where the time goes in v1:
time: 142 us; the launch traced here: 141 us
  blocking collectives  45.8 us (32%)
  Pallas kernels  35.7 us (25%)
  waiting for transfers between devices  24.7 us (17%)
  starting transfers between devices  16.8 us (12%)
  local copies, waits for them, and re-layouts  9.6 us (7%)
  other arithmetic  7.65 us (5%)
    pallas_call x3, Pallas kernels, step(): pl.pallas_call(functools.partial(step_kernel, count, capacity, scale, wid...  33.6 us
    all_to_all x1, blocking collectives, sum_over_scans(): lax.all_to_all(pieces, 'tile', split_axis=0, concat_axis=0, tiled=True)  33.4 us
    ppermute x7, waiting for transfers between devices, on_device(): lax.ppermute(blocks[hop], 'tile', [(i, i ^ hop) for i in range(tile_count)])  19.2 us
    ppermute x7, starting transfers between devices, on_device(): lax.ppermute(blocks[hop], 'tile', [(i, i ^ hop) for i in range(tile_count)])  14.1 us
    all_to_all x1, blocking collectives, sum_over_scans(): lax.all_to_all(copies, 'tile', split_axis=0, concat_axis=0, tiled=True)  12.4 us
    unnamed x24, local copies, waits for them, and re-layouts  9.58 us
    add x1, other arithmetic, on_device(): object_step = keep + lax.ppermute(send, 'pos', [(0, 1), (1, 0)])  4.57 us
    ppermute x1, waiting for transfers between devices, sum_over_scans(): part = keep + lax.ppermute(send, 'pos', other)  3.91 us
  transfers between devices with their start and end apart: 10, of which 4 were waited for; matrix products, arithmetic and copies ran while one was open for 1% of the time, Pallas kernels for 12%

profile of v1, /device:TPU:0, one launch (start us, length us, event | category | flops | bytes accessed | tf_op | source)
XLA Modules:
  0.0 141.0 jit_solution(12963260149683063180)
XLA Ops:
  0.6 1.2 copy-done.3
  1.9 0.7 copy-done.4
  2.5 0.7 copy-done.5
  3.2 0.7 copy-done.6
  3.8 2.1 %pack_patterns.1 = (bf16[1040,128]{1,0:T(8,128)(2,1)S(1)}, bf16[1040,128]{1,0:T(8,128)(2,1)S(1)}, bf16[1040,128]{1,0:T(8,128)(2,1)S(1)}, bf16[1040,128]{1,0:T(8,...) custom-call(s32[32]{0:T(128)S(1)} %bitcast.6, ...), custom_call_target="tpu_custom_call" | custom-call | tf_op jit(solution)/shard_map/pack_patterns/pallas_call | solution.py:88
  5.9 4.1 %collective-permute-start.3 = (bf16[1040,128]{1,0:T(8,128)(2,1)S(1)}, bf16[1040,128]{1,0:T(8,128)(2,1)S(1)}, u32[]{:S(2)}, u32[]{:S(2)}) collective-permute-start(bf16[1040,128]{1,0:T(8,128)(2,1)S(1)} %get-tuple-element.27), channel_id=1, source_target_pairs={{0,8},{2,10},{4,12},{6,14},{8,0},{10,2},{12,4},{14,6},{1,9},{3,11}... | collective-permute-start | bytes 798728 | tf_op jit(solution)/shard_map/ppermute | solution.py:420
  10.0 1.3 collective-permute-start.4
  11.3 0.2 collective-permute-start
  11.6 1.8 %collective-permute-start.1 = (bf16[1040,128]{1,0:T(8,128)(2,1)S(1)}, bf16[1040,128]{1,0:T(8,128)(2,1)S(1)}, u32[]{:S(2)}, u32[]{:S(2)}) collective-permute-start(bf16[1040,128]{1,0:T(8,128)(2,1)S(1)} %get-tuple-element.24), channel_id=1, source_target_pairs={{0,4},{2,6},{4,0},{6,2},{8,12},{10,14},{12,8},{14,10},{1,5},{3,7},... | collective-permute-start | bytes 798728 | tf_op jit(solution)/shard_map/ppermute | solution.py:420
  13.4 1.4 collective-permute-start.2
  14.8 14.0 %collective-permute-done.3.rest_0_ = bf16[1040,128]{1,0:T(8,128)(2,1)S(1)} collective-permute-done((bf16[1040,128]{1,0:T(8,128)(2,1)S(1)}, bf16[1040,128]{1,0:T(8,128)(2,1)S(1)}, u32[]{:S(2)}, u32[]{:S(2)}) %collective-permute-start.3) | collective-permute-done | bytes 266272 | tf_op jit(solution)/shard_map/ppermute | solution.py:420
  28.8 2.8 %collective-permute-start.5 = (bf16[1040,128]{1,0:T(8,128)(2,1)S(1)}, bf16[1040,128]{1,0:T(8,128)(2,1)S(1)}, u32[]{:S(2)}, u32[]{:S(2)}) collective-permute-start(bf16[1040,128]{1,0:T(8,128)(2,1)S(1)} %get-tuple-element.30), channel_id=1, source_target_pairs={{0,12},{2,14},{4,8},{6,10},{8,4},{10,6},{12,0},{14,2},{1,13},{3,15... | collective-permute-start | bytes 798728 | tf_op jit(solution)/shard_map/ppermute | solution.py:420
  31.6 5.3 %collective-permute-done.4.rest_1_ = bf16[1040,128]{1,0:T(8,128)(2,1)S(1)} collective-permute-done((bf16[1040,128]{1,0:T(8,128)(2,1)S(1)}, bf16[1040,128]{1,0:T(8,128)(2,1)S(1)}, u32[]{:S(2)}, u32[]{:S(2)}) %collective-permute-start.4) | collective-permute-done | bytes 266272 | tf_op jit(solution)/shard_map/ppermute | solution.py:420
  36.8 2.4 %collective-permute-start.6 = (bf16[1040,128]{1,0:T(8,128)(2,1)S(1)}, bf16[1040,128]{1,0:T(8,128)(2,1)S(1)}, u32[]{:S(2)}, u32[]{:S(2)}) collective-permute-start(bf16[1040,128]{1,0:T(8,128)(2,1)S(1)} %get-tuple-element.31), channel_id=1, source_target_pairs={{0,14},{2,12},{4,10},{6,8},{8,6},{10,4},{12,2},{14,0},{1,15},{3,13... | collective-permute-start | bytes 798728 | tf_op jit(solution)/shard_map/ppermute | solution.py:420
  39.3 2.2 %copy-done.7 = f32[2,512,1024]{2,1,0:T(8,128)S(1)} copy-done((f32[2,512,1024]{2,1,0:T(8,128)S(1)}, f32[2,512,1024]{2,1,0:T(8,128)}, u32[]{:S(2)}) %copy-start.7) | copy-done | bytes 4194328
  41.5 1.0 copy-done.9
  42.5 0.9 copy-done.10
  43.5 0.9 copy-done.11
  44.4 9.0 %gradient_step.4 = (f32[2,512,512]{2,1,0:T(8,128)S(1)}, f32[2,512,512]{2,1,0:T(8,128)S(1)}, f32[512,128]{1,0:T(8,128)S(1)}, f32[512,128]{1,0:T(8,128)S(1)}) custom-call(f32[2,512,1024]{2,1,0:T(8,128)S(1)} %copy-done.7, f32[4,2,128,128]{3,2,1,0:T(8,128)S(1)} %copy-done.9, bf16[2,256,256]{2,1,0:T(8,128)(2,1)S(1)} %copy-done.10, f32[2,128,128]{2,1,0:T(8,128)S(1)} %copy-done.11, ...), custom_call_target="tpu_custom_call" | custom-call | flops 4294967296 | bytes 16777216 | tf_op jit(solution)/shard_map/gradient_step/pallas_call | solution.py:361
  53.4 0.0 copy-start.8
  53.4 7.5 %gradient_step.5 = (f32[2,512,512]{2,1,0:T(8,128)S(1)}, f32[2,512,512]{2,1,0:T(8,128)S(1)}, f32[512,128]{1,0:T(8,128)S(1)}, f32[512,128]{1,0:T(8,128)S(1)}) custom-call(f32[2,512,1024]{2,1,0:T(8,128)S(1)} %copy-done.7, f32[4,2,128,128]{3,2,1,0:T(8,128)S(1)} %copy-done.9, bf16[2,256,256]{2,1,0:T(8,128)(2,1)S(1)} %copy-done.10, f32[2,128,128]{2,1,0:T(8,128)S(1)} %copy-done.11, ...), custom_call_target="tpu_custom_call" | custom-call | flops 4294967296 | bytes 16777216 | tf_op jit(solution)/shard_map/gradient_step/pallas_call | solution.py:361
  60.9 1.3 copy-done
  62.2 17.1 %gradient_step.3 = (f32[2,512,512]{2,1,0:T(8,128)S(1)}, f32[2,512,512]{2,1,0:T(8,128)S(1)}, f32[512,128]{1,0:T(8,128)S(1)}, f32[512,128]{1,0:T(8,128)S(1)}) custom-call(f32[2,512,1024]{2,1,0:T(8,128)S(1)} %copy-done.8, f32[4,2,128,128]{3,2,1,0:T(8,128)S(1)} %copy-done.9, bf16[2,256,256]{2,1,0:T(8,128)(2,1)S(1)} %copy-done.10, f32[2,128,128]{2,1,0:T(8,128)S(1)} %copy-done.11, ...), custom_call_target="tpu_custom_call" | custom-call | flops 8589934592 | bytes 16777216 | tf_op jit(solution)/shard_map/gradient_step/pallas_call | solution.py:361
  79.4 2.1 %add_add_fusion = f32[2,512,512]{2,1,0:T(8,128)} fusion(f32[2,512,512]{2,1,0:T(8,128)S(1)} %get-tuple-element.35, f32[2,512,512]{2,1,0:T(8,128)S(1)} %get-tuple-element.33, f32[2,512,512]{2,1,0:T(8,128)S(1)} %get-tuple-element.34), kind=kLoop, calls=%fused_computation | loop fusion | flops 1048576 | bytes 8388608 | tf_op jit(solution)/shard_map/add | solution.py:427
  81.5 2.6 %collective-permute-start.7 = (f32[2,512,512]{2,1,0:T(8,128)}, f32[2,512,512]{2,1,0:T(8,128)}, u32[]{:S(2)}, u32[]{:S(2)}) collective-permute-start(f32[2,512,512]{2,1,0:T(8,128)} %add_add_fusion), channel_id=1, source_target_pairs={{0,1},{1,0},{2,3},{3,2},{4,5},{5,4},{6,7},{7,6},{8,9},{9,8},{10,11... | collective-permute-start | bytes 6291464 | tf_op jit(solution)/shard_map/ppermute | solution.py:431
  84.1 0.1 collective-permute-start.8
  84.2 3.9 %collective-permute-done.8 = f32[512,128]{1,0:T(8,128)S(1)} collective-permute-done((f32[512,128]{1,0:T(8,128)S(1)}, f32[512,128]{1,0:T(8,128)S(1)}, u32[]{:S(2)}, u32[]{:S(2)}) %collective-permute-start.8) | collective-permute-done | bytes 262176 | tf_op jit(solution)/shard_map/ppermute | solution.py:399
  88.1 33.4 %all_to_all.10 = f32[8,64,128]{2,1,0:T(8,128)S(1)} all-to-all(f32[8,64,128]{2,1,0:T(8,128)S(1)} %bitcast.7), channel_id=1, replica_groups=mesh['groups'=2,'tile'=8,'pos'=2] {'tile'}, dimensions={0} | all-to-all | bytes 524288 | tf_op jit(solution)/shard_map/all_to_all | solution.py:402
  121.6 12.4 %all_to_all.11 = f32[8,64,128]{2,1,0:T(8,128)S(1)} all-to-all(f32[8,64,128]{2,1,0:T(8,128)S(1)} %broadcast_in_dim.2), channel_id=1, replica_groups=mesh['groups'=2,'tile'=8,'pos'=2] {'tile'}, dimensions={0} | all-to-all | bytes 524288 | tf_op jit(solution)/shard_map/all_to_all | solution.py:404
  134.0 1.5 %collective-permute-done.9 = f32[512,128]{1,0:T(8,128)S(1)} collective-permute-done((f32[512,128]{1,0:T(8,128)S(1)}, f32[512,128]{1,0:T(8,128)S(1)}, u32[]{:S(2)}, u32[]{:S(2)}) %collective-permute-start.9) | collective-permute-done | bytes 262176 | tf_op jit(solution)/shard_map/ppermute | solution.py:406
  135.6 0.8 pad_maximum_fusion
  136.4 4.6 %add_add_fusion.1 = f32[2,512,512]{2,1,0:T(8,128)} fusion(f32[2,512,512]{2,1,0:T(8,128)} %collective-permute-done.7, f32[2,512,512]{2,1,0:T(8,128)S(1)} %copy-done.1, f32[2,512,512]{2,1,0:T(8,128)} %copy-done.2, f32[2,512,512]{2,1,0:T(8,128)S(1)} %get-tuple-element.29), kind=kLoop, calls=%fused_computation.1 | loop fusion | flops 1572864 | bytes 10485760 | tf_op jit(solution)/shard_map/add | solution.py:431
  (26 shorter events, 0.2 us)
Async XLA Ops:
  0.6 1.2 copy-start.3
  1.9 0.7 copy-start.4
  2.5 0.7 copy-start.5
  3.2 0.7 copy-start.6
  5.9 22.8 %collective-permute-start.3 = (bf16[1040,128]{1,0:T(8,128)(2,1)S(1)}, bf16[1040,128]{1,0:T(8,128)(2,1)S(1)}, u32[]{:S(2)}, u32[]{:S(2)}) collective-permute-start(bf16[1040,128]{1,0:T(8,128)(2,1)S(1)} %get-tuple-element.27), channel_id=1, source_target_pairs={{0,8},{2,10},{4,12},{6,14},{8,0},{10,2},{12,4},{14,6},{1,9},{3,11}... | collective-permute-start | bytes 798728 | tf_op jit(solution)/shard_map/ppermute | solution.py:420
  10.0 26.8 %collective-permute-start.4 = (bf16[1040,128]{1,0:T(8,128)(2,1)S(1)}, bf16[1040,128]{1,0:T(8,128)(2,1)S(1)}, u32[]{:S(2)}, u32[]{:S(2)}) collective-permute-start(bf16[1040,128]{1,0:T(8,128)(2,1)S(1)} %get-tuple-element.28), channel_id=1, source_target_pairs={{0,10},{2,8},{4,14},{6,12},{8,2},{10,0},{12,6},{14,4},{1,11},{3,9}... | collective-permute-start | bytes 798728 | tf_op jit(solution)/shard_map/ppermute | solution.py:420
  11.3 50.9 %collective-permute-start = (bf16[1040,128]{1,0:T(8,128)(2,1)S(1)}, bf16[1040,128]{1,0:T(8,128)(2,1)S(1)}, u32[]{:S(2)}, u32[]{:S(2)}) collective-permute-start(bf16[1040,128]{1,0:T(8,128)(2,1)S(1)} %get-tuple-element.23), channel_id=1, source_target_pairs={{0,2},{2,0},{4,6},{6,4},{8,10},{10,8},{12,14},{14,12},{1,3},{3,1},... | collective-permute-start | bytes 798728 | tf_op jit(solution)/shard_map/ppermute | solution.py:420
  11.6 50.6 %collective-permute-start.1 = (bf16[1040,128]{1,0:T(8,128)(2,1)S(1)}, bf16[1040,128]{1,0:T(8,128)(2,1)S(1)}, u32[]{:S(2)}, u32[]{:S(2)}) collective-permute-start(bf16[1040,128]{1,0:T(8,128)(2,1)S(1)} %get-tuple-element.24), channel_id=1, source_target_pairs={{0,4},{2,6},{4,0},{6,2},{8,12},{10,14},{12,8},{14,10},{1,5},{3,7},... | collective-permute-start | bytes 798728 | tf_op jit(solution)/shard_map/ppermute | solution.py:420
  13.4 48.8 %collective-permute-start.2 = (bf16[1040,128]{1,0:T(8,128)(2,1)S(1)}, bf16[1040,128]{1,0:T(8,128)(2,1)S(1)}, u32[]{:S(2)}, u32[]{:S(2)}) collective-permute-start(bf16[1040,128]{1,0:T(8,128)(2,1)S(1)} %get-tuple-element.25), channel_id=1, source_target_pairs={{0,6},{2,4},{4,2},{6,0},{8,14},{10,12},{12,10},{14,8},{1,7},{3,5},... | collective-permute-start | bytes 798728 | tf_op jit(solution)/shard_map/ppermute | solution.py:420
  28.8 24.6 %collective-permute-start.5 = (bf16[1040,128]{1,0:T(8,128)(2,1)S(1)}, bf16[1040,128]{1,0:T(8,128)(2,1)S(1)}, u32[]{:S(2)}, u32[]{:S(2)}) collective-permute-start(bf16[1040,128]{1,0:T(8,128)(2,1)S(1)} %get-tuple-element.30), channel_id=1, source_target_pairs={{0,12},{2,14},{4,8},{6,10},{8,4},{10,6},{12,0},{14,2},{1,13},{3,15... | collective-permute-start | bytes 798728 | tf_op jit(solution)/shard_map/ppermute | solution.py:420
  36.8 16.6 %collective-permute-start.6 = (bf16[1040,128]{1,0:T(8,128)(2,1)S(1)}, bf16[1040,128]{1,0:T(8,128)(2,1)S(1)}, u32[]{:S(2)}, u32[]{:S(2)}) collective-permute-start(bf16[1040,128]{1,0:T(8,128)(2,1)S(1)} %get-tuple-element.31), channel_id=1, source_target_pairs={{0,14},{2,12},{4,10},{6,8},{8,6},{10,4},{12,2},{14,0},{1,15},{3,13... | collective-permute-start | bytes 798728 | tf_op jit(solution)/shard_map/ppermute | solution.py:420
  39.3 2.2 %copy-start.7 = (f32[2,512,1024]{2,1,0:T(8,128)S(1)}, f32[2,512,1024]{2,1,0:T(8,128)}, u32[]{:S(2)}) copy-start(f32[2,512,1024]{2,1,0:T(8,128)} %object_hbm.5) | copy-start | bytes 12582916
  41.5 1.0 copy-start.9
  42.5 0.9 copy-start.10
  43.5 0.9 copy-start.11
  53.4 8.8 %copy-start.8 = (f32[2,512,1024]{2,1,0:T(8,128)S(1)}, f32[2,512,1024]{2,1,0:T(8,128)}, u32[]{:S(2)}) copy-start(f32[2,512,1024]{2,1,0:T(8,128)} %object_hbm.5) | copy-start | bytes 12582916
  60.9 1.3 copy-start
  79.4 2.1 %copy-start.2 = (f32[2,512,512]{2,1,0:T(8,128)}, f32[2,512,512]{2,1,0:T(8,128)S(1)}, u32[]{:S(2)}) copy-start(f32[2,512,512]{2,1,0:T(8,128)S(1)} %get-tuple-element.26) | copy-start | bytes 6291460
  81.5 54.9 %collective-permute-start.7 = (f32[2,512,512]{2,1,0:T(8,128)}, f32[2,512,512]{2,1,0:T(8,128)}, u32[]{:S(2)}, u32[]{:S(2)}) collective-permute-start(f32[2,512,512]{2,1,0:T(8,128)} %add_add_fusion), channel_id=1, source_target_pairs={{0,1},{1,0},{2,3},{3,2},{4,5},{5,4},{6,7},{7,6},{8,9},{9,8},{10,11... | collective-permute-start | bytes 6291464 | tf_op jit(solution)/shard_map/ppermute | solution.py:431
  84.1 4.0 %collective-permute-start.8 = (f32[512,128]{1,0:T(8,128)S(1)}, f32[512,128]{1,0:T(8,128)S(1)}, u32[]{:S(2)}, u32[]{:S(2)}) collective-permute-start(f32[512,128]{1,0:T(8,128)S(1)} %add_add_fusion.2), channel_id=1, source_target_pairs={{0,1},{1,0},{2,3},{3,2},{4,5},{5,4},{6,7},{7,6},{8,9},{9,8},{10,11... | collective-permute-start | bytes 786440 | tf_op jit(solution)/shard_map/ppermute | solution.py:399
  134.0 1.5 %collective-permute-start.9 = (f32[512,128]{1,0:T(8,128)S(1)}, f32[512,128]{1,0:T(8,128)S(1)}, u32[]{:S(2)}, u32[]{:S(2)}) collective-permute-start(f32[512,128]{1,0:T(8,128)S(1)} %bitcast.8), channel_id=1, source_target_pairs={{0,1},{1,0},{2,3},{3,2},{4,5},{5,4},{6,7},{7,6},{8,9},{9,8},{10,11... | collective-permute-start | bytes 786440 | tf_op jit(solution)/shard_map/ppermute | solution.py:406
  134.0 2.4 %copy-start.1 = (f32[2,512,512]{2,1,0:T(8,128)S(1)}, f32[2,512,512]{2,1,0:T(8,128)}, u32[]{:S(2)}) copy-start(f32[2,512,512]{2,1,0:T(8,128)} %copy-done) | copy-start | bytes 6291460

commit v2 on v1

v2 whole, which is shorter than its diff:
```python
import functools
import math

import jax
import jax.numpy as jnp
import numpy as np
from jax import lax
from jax.experimental import pallas as pl
from jax.experimental.pallas import tpu as pltpu
from jax.sharding import PartitionSpec as P

AMP_FLOOR = 0.5
HEAD = 16
DIGIT = 16
LANES = 128
SQUARE = 4
CROSS = jnp.float32
BAND = 16


def dft_tables(length):
    indices = np.arange(length, dtype=np.int32)
    products = indices[:, None] * indices[None, :] % length
    angles = products.astype(np.float32) * np.float32(-2.0 * math.pi / length)
    factor = np.float32(1.0 / math.sqrt(length))
    real = (np.cos(angles) * factor).astype(jnp.bfloat16)
    imag = (np.sin(angles) * factor).astype(jnp.bfloat16)
    forward = np.block([[real, -imag], [imag, real]])
    backward = np.block([[real, imag], [-imag, real]])
    return np.stack([forward, backward])


def chirp_table(length):
    offsets = np.arange(length, dtype=np.int32) - length // 2
    squares = offsets * offsets
    phases = (squares[:, None] + squares[None, :]).astype(np.float32) * np.float32(
        0.5 * math.pi / length
    )
    return np.stack([np.cos(phases), np.sin(phases)]).astype(np.float32)


def pack_kernel(tile_count, capacity, tile_ref, row_ref, col_ref, pat_ref, *rest):
    blocks, count_ref, source_ref = rest[:tile_count], rest[tile_count], rest[tile_count + 1]
    number, length = pat_ref.shape[0], pat_ref.shape[1]
    me = lax.axis_index("tile")
    for hop in range(tile_count):
        count_ref[hop] = 0

    def place(index, carry):
        hop = tile_ref[index] ^ me
        rank = count_ref[hop]
        count_ref[hop] = rank + 1
        source_ref[hop * capacity + rank] = index
        return carry

    lax.fori_loop(0, number, place, 0)
    lane = lax.broadcasted_iota(jnp.int32, (HEAD, LANES), 1)
    line = lax.broadcasted_iota(jnp.int32, (HEAD, LANES), 0)
    for hop in range(tile_count):
        count = count_ref[hop]
        head = jnp.where(line == 4, count, 0)
        for rank in range(capacity):
            valid = rank < count
            index = jnp.where(valid, source_ref[hop * capacity + rank], 0)
            row, col = row_ref[index], col_ref[index]

            @pl.when(valid)
            def _(hop=hop, rank=rank, index=index):
                blocks[hop][rank * length : (rank + 1) * length, :] = pat_ref[index]

            digits = jnp.where(
                line == 0,
                row // DIGIT,
                jnp.where(
                    line == 1,
                    row % DIGIT,
                    jnp.where(line == 2, col // DIGIT, jnp.where(line == 3, col % DIGIT, 0)),
                ),
            )
            head = head + jnp.where((lane == rank) & valid, digits, 0)
        blocks[hop][capacity * length :, :] = head.astype(jnp.float32).astype(jnp.bfloat16)


def pack(patterns, tile_ids, rows, cols, tile_count, capacity):
    length = patterns.shape[-1]
    block = jax.ShapeDtypeStruct((capacity * length + HEAD, length), jnp.bfloat16)
    smem = pl.BlockSpec(memory_space=pltpu.SMEM)
    vmem = pl.BlockSpec(memory_space=pltpu.VMEM)
    return pl.pallas_call(
        functools.partial(pack_kernel, tile_count, capacity),
        out_shape=[block] * tile_count,
        in_specs=[smem, smem, smem, vmem],
        out_specs=[vmem] * tile_count,
        scratch_shapes=[
            pltpu.SMEM((tile_count,), jnp.int32),
            pltpu.SMEM((tile_count * capacity,), jnp.int32),
        ],
        compiler_params=pltpu.CompilerParams(vmem_limit_bytes=56 * 2**20),
        name="pack_patterns",
    )(tile_ids, rows, cols, patterns)


def step_kernel(
    block_count, capacity, scale, first, last, object_hbm, probe_ref, dft_ref, chirp_ref, *rest
):
    blocks = rest[:block_count]
    rest = rest[block_count:]
    if not first:
        before = rest[:SQUARE]
        rest = rest[SQUARE:]
    after = rest[: 2 + SQUARE]
    (
        field,
        total,
        pats,
        heads,
        corners,
        list_row,
        list_col,
        list_pat,
        lit,
        grad,
        patch_even,
        patch_odd,
        wide,
        tall,
        in_sem,
        out_sem,
    ) = rest[2 + SQUARE :]
    modes, _, length, _ = probe_ref.shape
    rows, columns = object_hbm.shape[1:]
    block_rows = capacity * length + HEAD
    bands = length // BAND
    pos = lax.axis_index("pos")

    column_tiles = columns // LANES
    load_field = [
        pltpu.make_async_copy(
            object_hbm.at[:, :, tile * LANES : (tile + 1) * LANES],
            field.at[:, tile, 0:rows, :],
            in_sem.at[block_count + 1 + tile],
        )
        for tile in range(column_tiles)
    ]
    loads = [
        pltpu.make_async_copy(
            blocks[b], pats.at[b * block_rows : (b + 1) * block_rows], in_sem.at[b]
        )
        for b in range(block_count)
    ]
    for load in loads + load_field:
        load.start()

    half = column_tiles // 2
    quarter = grad.shape[0] // SQUARE
    me = lax.axis_index("tile") % (SQUARE // 2) * 2 + pos

    def grad_parts(outsides):
        return [
            (grad.at[pl.ds(pl.multiple_of((me ^ turn) * quarter, 8), quarter), :], outside)
            for turn, outside in enumerate(outsides)
        ]

    def total_parts(keep_out, send_out):
        return [
            (
                total.at[:, side * half + tile, 0:rows, :],
                out.at[:, :, tile * LANES : (tile + 1) * LANES],
            )
            for out, side in ((send_out, 1 - pos), (keep_out, pos))
            for tile in range(half)
        ]

    carried = []
    if first:
        grad[...] = jnp.zeros_like(grad)
    else:
        carried = [
            pltpu.make_async_copy(outside, inside, out_sem.at[n])
            for n, (inside, outside) in enumerate(grad_parts(before))
        ]
    for load in carried:
        load.start()

    def clear(index, carry):
        at = pl.ds(pl.multiple_of(index * 8, 8), 8)
        for plane in range(2):
            for tile in range(column_tiles):
                total[plane, tile, at, :] = jnp.zeros((8, LANES), jnp.float32)
        return carry

    lax.fori_loop(0, rows // 8, clear, 0)
    for mode in range(modes):
        for band in range(bands):
            at = pl.ds(band * BAND, BAND)
            cr, ci = chirp_ref[0, at, :], chirp_ref[1, at, :]
            pr, pi = probe_ref[mode, 0, at, :], probe_ref[mode, 1, at, :]
            lit[mode, 0, at, :] = cr * pr - ci * pi
            lit[mode, 1, at, :] = cr * pi + ci * pr

    for load in loads:
        load.wait()
    for b in range(block_count):
        heads[b * HEAD : (b + 1) * HEAD, :] = (
            pats[(b + 1) * block_rows - HEAD : (b + 1) * block_rows, :]
            .astype(jnp.float32)
            .astype(jnp.int32)
        )
    fetch = pltpu.make_async_copy(heads, corners, in_sem.at[block_count])
    fetch.start()
    fetch.wait()

    number = jnp.int32(0)
    for b in range(block_count):

        def note(rank, at, b=b):
            first = b * HEAD
            list_row[at] = corners[first, rank] * DIGIT + corners[first + 1, rank]
            list_col[at] = corners[first + 2, rank] * DIGIT + corners[first + 3, rank]
            list_pat[at] = b * block_rows + rank * length
            return at + 1

        number = lax.fori_loop(0, corners[b * HEAD + 4, 0], note, number)
    for load in load_field + carried:
        load.wait()

    patch = (patch_even, patch_odd)
    group = max(BAND, LANES // modes)
    groups = length // group
    tall_rows = modes * group

    def item(index):
        index = jnp.clip(index, 0, number - 1)
        row, col = list_row[index], list_col[index]
        shift = col % LANES
        return row, col // LANES, shift, pl.multiple_of(list_pat[index], LANES)

    def exit_chunks(index, side):
        row, col, shift, _ = item(index)
        slot = (index >> 1) & 1
        back = (LANES - shift) % LANES

        def chunk(band):
            at = pl.ds(band * BAND, BAND)
            at_field = pl.ds(row + band * BAND, BAND)
            lane = lax.broadcasted_iota(jnp.int32, (BAND, LANES), 1)
            planes = []
            for plane in range(2):
                left = pltpu.roll(field[plane, col, at_field, :], back, 1)
                right = pltpu.roll(field[plane, col + 1, at_field, :], back, 1)
                cell = jnp.where(lane < LANES - shift, left, right)
                cell = cell.astype(jnp.bfloat16).astype(jnp.float32)
                patch[side][slot, plane, at, :] = cell
                planes.append(cell)
            pr, pi = planes
            for mode in range(modes):
                lr, li = lit[mode, 0, at, :], lit[mode, 1, at, :]
                lanes = pl.ds(mode * length, length)
                wide[side, at, lanes] = (lr * pr - li * pi).astype(jnp.bfloat16)
                wide[side, pl.ds(length + band * BAND, BAND), lanes] = (
                    lr * pi + li * pr
                ).astype(jnp.bfloat16)

        return [functools.partial(chunk, band) for band in range(bands)]

    def column_chunks(source, target, table):
        def chunk(mode):
            both = min(2, modes - mode)
            out = jnp.dot(
                dft_ref[table],
                wide[source, :, mode * length : (mode + both) * length],
                preferred_element_type=jnp.float32,
            ).astype(jnp.bfloat16)
            for q in range(both):
                for g in range(groups):
                    at = pl.ds(g * tall_rows + (mode + q) * group, group)
                    for plane in range(2):
                        tall[target, at, plane * length : (plane + 1) * length] = out[
                            plane * length + g * group : plane * length + (g + 1) * group,
                            q * length : (q + 1) * length,
                        ]

        return [functools.partial(chunk, mode) for mode in range(0, modes, 2)]

    def row_product(source, table, g):
        out = jnp.dot(
            tall[source, g * tall_rows : (g + 1) * tall_rows, :],
            dft_ref[table],
            preferred_element_type=jnp.float32,
        )
        return [
            (
                out[mode * group : (mode + 1) * group, 0:length],
                out[mode * group : (mode + 1) * group, length : 2 * length],
            )
            for mode in range(modes)
        ]

    def far_chunks(index, side):
        _, _, _, source = item(index)
        weight = jnp.where((index >= 0) & (index < number), jnp.float32(1.0), jnp.float32(0.0))

        def chunk(g):
            waves = row_product(side, 1, g)
            bright = None
            for fr, fi in waves:
                power = fr * fr + fi * fi
                bright = power if bright is None else bright + power
            measured = pats[pl.ds(source + g * group, group), :].astype(jnp.float32)
            inverse = jnp.minimum(lax.rsqrt(bright), 1.0 / AMP_FLOOR)
            factor = (measured * inverse - 1.0) * weight
            for mode in range(modes):
                fr, fi = waves[mode]
                lanes = pl.ds(mode * length, length)
                wide[2, pl.ds(g * group, group), lanes] = (fr * factor).astype(jnp.bfloat16)
                wide[2, pl.ds(length + g * group, group), lanes] = (fi * factor).astype(
                    jnp.bfloat16
                )

        return [functools.partial(chunk, g) for g in range(groups)]

    def step_chunks(index, side):
        row, col, shift, _ = item(index)
        slot = (index >> 1) & 1

        def chunk(g):
            at = pl.ds(g * group, group)
            at_field = pl.ds(row + g * group, group)
            lane = lax.broadcasted_iota(jnp.int32, (group, LANES), 1)
            waves = row_product(2 + side, 0, g)
            pr, pi = patch[side][slot, 0, at, :], patch[side][slot, 1, at, :]
            steps = [None, None]
            for mode in range(modes):
                at_gr = pl.ds((2 * mode) * length + g * group, group)
                at_gi = pl.ds((2 * mode + 1) * length + g * group, group)
                lr, li = lit[mode, 0, at, :], lit[mode, 1, at, :]
                nr, ni = waves[mode]
                sr, si = lr * nr + li * ni, lr * ni - li * nr
                steps = [sr, si] if mode == 0 else [steps[0] + sr, steps[1] + si]
                grad[at_gr, :] += pr * nr + pi * ni
                grad[at_gi, :] += pr * ni - pi * nr
            places = [(plane, col + tile) for plane in range(2) for tile in range(2)]
            olds = [total[plane, tile, at_field, :] for plane, tile in places]
            sums = []
            for plane in range(2):
                moved = steps[plane].astype(jnp.bfloat16).astype(jnp.float32)
                moved = pltpu.roll(moved, shift, 1)
                sums.append(olds[2 * plane] + jnp.where(lane >= shift, moved, 0.0))
                sums.append(olds[2 * plane + 1] + jnp.where(lane < shift, moved, 0.0))
            for (plane, tile), value in zip(places, sums):
                total[plane, tile, at_field, :] = value

        return [functools.partial(chunk, g) for g in range(groups)]

    def run(*lists):
        order = []
        for rank, chunks in enumerate(lists):
            order += [((n + 0.5) / len(chunks), rank, chunk) for n, chunk in enumerate(chunks)]
        for _, _, chunk in sorted(order, key=lambda entry: entry[:2]):
            chunk()

    def visit(turn, carry):
        for side in range(2):
            at, other = 2 * turn + side, 1 - side
            run(far_chunks(at, side))
            run(column_chunks(other, other, 0), exit_chunks(at + 2, side))
            run(column_chunks(2, 2 + side, 1), step_chunks(at - 1, other))
        return carry

    @pl.when(number > 0)
    def _():
        tall[3] = jnp.zeros(tall.shape[1:], tall.dtype)
        patch[1][1] = jnp.zeros(patch[1].shape[1:], jnp.float32)
        run(exit_chunks(jnp.int32(0), 0))
        run(column_chunks(0, 0, 0), exit_chunks(jnp.int32(1), 1))
        lax.fori_loop(0, number // 2 + 1, visit, 0)

    for mode in range(modes if last else 0):
        for band in range(bands):
            at = pl.ds(band * BAND, BAND)
            at_gr = pl.ds((2 * mode) * length + band * BAND, BAND)
            at_gi = pl.ds((2 * mode + 1) * length + band * BAND, BAND)
            cr, ci = chirp_ref[0, at, :] * scale, chirp_ref[1, at, :] * scale
            gr, gi = grad[at_gr, :], grad[at_gi, :]
            grad[at_gr, :] = cr * gr + ci * gi
            grad[at_gi, :] = cr * gi - ci * gr
    stores = [
        pltpu.make_async_copy(inside, outside, out_sem.at[n])
        for n, (inside, outside) in enumerate(
            grad_parts(after[2:]) + total_parts(*after[:2])
        )
    ]
    for store in stores:
        store.start()
    for store in stores:
        store.wait()


def step(object_field, probe, blocks, tables, scale, capacity, before=None, last=True):
    modes, _, length, _ = probe.shape
    rows, columns = object_field.shape[1:]
    count = len(blocks)
    slots = count * capacity
    vmem = pl.BlockSpec(memory_space=pltpu.VMEM)
    hbm = pl.BlockSpec(memory_space=pl.ANY)
    f32, bf16 = jnp.float32, jnp.bfloat16
    padded = (2, columns // LANES + 1, rows + 8, LANES)
    work = slots * modes * 4 * 8 * length**3
    return pl.pallas_call(
        functools.partial(
            step_kernel, count, capacity, scale, before is None, last
        ),
        out_shape=[
            jax.ShapeDtypeStruct((2, rows, columns // 2), f32),
            jax.ShapeDtypeStruct((2, rows, columns // 2), f32),
        ]
        + [jax.ShapeDtypeStruct((2 * modes * length // SQUARE, length), f32)] * SQUARE,
        in_specs=[hbm, vmem, vmem, vmem] + [hbm] * (count + len(before or ())),
        out_specs=[hbm] * (2 + SQUARE),
        scratch_shapes=[
            pltpu.VMEM(padded, f32),
            pltpu.VMEM(padded, f32),
            pltpu.VMEM((count * (capacity * length + HEAD), length), bf16),
            pltpu.VMEM((count * HEAD, LANES), jnp.int32),
            pltpu.SMEM((count * HEAD, LANES), jnp.int32),
            pltpu.SMEM((slots,), jnp.int32),
            pltpu.SMEM((slots,), jnp.int32),
            pltpu.SMEM((slots,), jnp.int32),
            pltpu.VMEM((modes, 2, length, length), f32),
            pltpu.VMEM((2 * modes * length, length), f32),
            pltpu.VMEM((2, 2, length, length), f32),
            pltpu.VMEM((2, 2, length, length), f32),
            pltpu.VMEM((3, 2 * length, modes * length), bf16),
            pltpu.VMEM((4, modes * length, 2 * length), bf16),
            pltpu.SemaphoreType.DMA((count + 1 + columns // LANES,)),
            pltpu.SemaphoreType.DMA((SQUARE + columns // LANES,)),
        ],
        compiler_params=pltpu.CompilerParams(vmem_limit_bytes=56 * 2**20),
        cost_estimate=pl.CostEstimate(
            flops=work, bytes_accessed=16 * 2**20, transcendentals=slots * length**2
        ),
        name="gradient_step",
    )(object_field, probe, *tables, *blocks, *(before or ()))


def from_peer(array, turn, devices):
    pairs = [(i, i ^ turn) for i in range(devices)]
    return lax.ppermute(array, ("tile", "pos"), pairs)


def tree_sum(parts):
    while len(parts) > 1:
        parts = [a + b for a, b in zip(parts[::2], parts[1::2])]
    return parts[0]


def on_device(object_field, probe, patterns, scan_tile, scan_row, scan_col):
    tile_count = lax.axis_size("tile")
    pos_count = lax.axis_size("pos")
    number, length = patterns.shape[0], patterns.shape[-1]
    capacity = max(2, 2 * number // tile_count)
    scale = 1.0 / math.sqrt(number * tile_count * pos_count)
    tables = (jnp.asarray(dft_tables(length)), jnp.asarray(chirp_table(length)))
    blocks = pack(patterns, scan_tile[:, 0], scan_row, scan_col, tile_count, capacity)
    late = tile_count * 3 // 4
    order = [*range(late - tile_count // 4), *range(late, tile_count), *range(tile_count // 2, late)]
    arrived = [blocks[0]]
    for hop in order[1:]:
        block = blocks[hop]
        if len(arrived) >= late:
            block = lax.optimization_barrier((block, arrived[1]))[0]
        arrived.append(lax.ppermute(block, "tile", [(i, i ^ hop) for i in range(tile_count)]))
    cuts = [0, tile_count // 2, tile_count * 3 // 4, tile_count]
    grads, keeps, sends = None, [], []
    for a, b in zip(cuts[:-1], cuts[1:]):
        keep, send, *grads = step(
            object_field, probe, arrived[a:b], tables, scale, capacity, grads, b == tile_count
        )
        keeps.append(keep)
        sends.append(send)

    devices = tile_count * pos_count
    inside, across = range(1, SQUARE), range(SQUARE, devices, SQUARE)
    part = tree_sum([grads[0]] + [from_peer(grads[turn], turn, devices) for turn in inside])
    sends[-1], part = lax.optimization_barrier((sends[-1], part))
    other = [(0, 1), (1, 0)]
    object_step = sum(keeps[1:], keeps[0])
    for send in sends:
        object_step = object_step + lax.ppermute(send, "pos", other)
    part = part.astype(CROSS)
    part = tree_sum(
        [part.astype(jnp.float32)]
        + [from_peer(part, turn, devices).astype(jnp.float32) for turn in across]
    )
    part, object_step = lax.optimization_barrier((part, object_step))
    square = [part] + [from_peer(part, turn, devices) for turn in inside]
    me = lax.axis_index(("tile", "pos"))
    for bit in (1, 2):
        swapped = (me & bit) != 0
        square = [jnp.where(swapped, square[q ^ bit], square[q]) for q in range(SQUARE)]
    return (object_step, jnp.concatenate(square).reshape(probe.shape))


def solution(mesh):
    placed = (
        P("groups", "tile", None),
        P("groups", None, None, None),
        P(("groups", "tile", "pos"), None, None),
        P(("groups", "tile", "pos"), None),
        P(("groups", "tile", "pos")),
        P(("groups", "tile", "pos")),
    )
    return jax.shard_map(
        on_device,
        mesh=mesh,
        in_specs=placed,
        out_specs=(P("groups", "tile", "pos"), P("groups", None, None, None)),
        check_vma=False,
    )
```

time: 142 us -> 128 us (0.901)
  blocking collectives: 45.8 us -> 0 us
  starting transfers between devices: 16.8 us -> 44.2 us
  Pallas kernels: 35.7 us -> 56.3 us
  local copies, waits for them, and re-layouts: 9.6 us -> 2.26 us
  waiting for transfers between devices: 24.7 us -> 18.4 us
    all_to_all x2 -> x0, blocking collectives: 45.8 us -> none  [the longest x1 33.4 us: sum_over_scans(): lax.all_to_all(pieces, 'tile', split_axis=0, concat_axis=0, tiled=True)]
    ppermute x10 -> x19, starting transfers between devices: 16.8 us -> 44.2 us  [the longest x9 27.4 us: from_peer(): return lax.ppermute(array, ('tile', 'pos'), pairs)]
    pallas_call x3, Pallas kernels: 33.6 us -> 52.2 us  [step(): pl.pallas_call(functools.partial(step_kernel, count, capacity, scale, bef...]
    unnamed x24 -> x20, local copies, waits for them, and re-layouts: 9.58 us -> 2.26 us
    ppermute x10 -> x19, waiting for transfers between devices: 24.7 us -> 18.4 us  [the longest x9 14.8 us: from_peer(): return lax.ppermute(array, ('tile', 'pos'), pairs)]
    pallas_call x1, Pallas kernels: 2.11 us -> 4.13 us  [pack(): pl.pallas_call(functools.partial(pack_kernel, tile_count, capacity), out_...]
    add x4 -> x3, other arithmetic: 6.76 us -> 5.44 us  [the longest x1 4.47 us: on_device(): object_step = object_step + lax.ppermute(send, 'pos', other)]
  transfers between devices with their start and end apart: 10 -> 19, of which waited for: 4 -> 6; matrix products, arithmetic and copies ran while one was open for 1% -> 1% of each run, Pallas kernels for 12% -> 29%
where the time goes in v2:
time: 128 us
  Pallas kernels  56.3 us (44%)
  starting transfers between devices  44.2 us (35%)
  waiting for transfers between devices  18.4 us (14%)
  other arithmetic  6.31 us (5%)
  local copies, waits for them, and re-layouts  2.26 us (2%)
    pallas_call x3, Pallas kernels, step(): pl.pallas_call(functools.partial(step_kernel, count, capacity, scale, bef...  52.2 us
    ppermute x9, starting transfers between devices, from_peer(): return lax.ppermute(array, ('tile', 'pos'), pairs)  27.4 us
    ppermute x7, starting transfers between devices, on_device(): lax.ppermute(block, 'tile', [(i, i ^ hop) for i in range(tile_count)])  15 us
    ppermute x9, waiting for transfers between devices, from_peer(): return lax.ppermute(array, ('tile', 'pos'), pairs)  14.8 us
    add x1, other arithmetic, on_device(): object_step = object_step + lax.ppermute(send, 'pos', other)  4.47 us
    pallas_call x1, Pallas kernels, pack(): pl.pallas_call(functools.partial(pack_kernel, tile_count, capacity), out_...  4.13 us
    ppermute x7, waiting for transfers between devices, on_device(): lax.ppermute(block, 'tile', [(i, i ^ hop) for i in range(tile_count)])  3.63 us
  transfers between devices with their start and end apart: 19, of which 6 were waited for; matrix products, arithmetic and copies ran while one was open for 1% of the time, Pallas kernels for 29%

profile of v2, /device:TPU:0, one launch (start us, length us, event | category | flops | bytes accessed | tf_op | source)
XLA Modules:
  0.0 128.3 jit_solution(1350709871577251260)
XLA Ops:
  0.6 4.1 %pack_patterns.1 = (bf16[1040,128]{1,0:T(8,128)(2,1)}, bf16[1040,128]{1,0:T(8,128)(2,1)}, bf16[1040,128]{1,0:T(8,128)(2,1)}, bf16[1040,128]{1,0:T(8,128)(2,1)}, ...) custom-call(s32[32]{0:T(128)} %bitcast.3, ...), custom_call_target="tpu_custom_call" | custom-call | tf_op jit(solution)/shard_map/pack_patterns/pallas_call | solution.py:89
  4.8 3.0 %collective-permute-start = (bf16[1040,128]{1,0:T(8,128)(2,1)}, bf16[1040,128]{1,0:T(8,128)(2,1)S(1)}, u32[]{:S(2)}, u32[]{:S(2)}) collective-permute-start(bf16[1040,128]{1,0:T(8,128)(2,1)} %get-tuple-element.35), channel_id=1, source_target_pairs={{0,2},{2,0},{4,6},{6,4},{8,10},{10,8},{12,14},{14,12},{1,3},{3,1},... | collective-permute-start | bytes 798728 | tf_op jit(solution)/shard_map/ppermute | solution.py:472
  7.7 1.6 %collective-permute-start.5 = (bf16[1040,128]{1,0:T(8,128)(2,1)}, bf16[1040,128]{1,0:T(8,128)(2,1)S(1)}, u32[]{:S(2)}, u32[]{:S(2)}) collective-permute-start(bf16[1040,128]{1,0:T(8,128)(2,1)} %get-tuple-element.42), channel_id=1, source_target_pairs={{0,4},{2,6},{4,0},{6,2},{8,12},{10,14},{12,8},{14,10},{1,5},{3,7},... | collective-permute-start | bytes 798728 | tf_op jit(solution)/shard_map/ppermute | solution.py:472
  9.3 4.0 %collective-permute-start.3 = (bf16[1040,128]{1,0:T(8,128)(2,1)}, bf16[1040,128]{1,0:T(8,128)(2,1)S(1)}, u32[]{:S(2)}, u32[]{:S(2)}) collective-permute-start(bf16[1040,128]{1,0:T(8,128)(2,1)} %get-tuple-element.39), channel_id=1, source_target_pairs={{0,12},{2,14},{4,8},{6,10},{8,4},{10,6},{12,0},{14,2},{1,13},{3,15... | collective-permute-start | bytes 798728 | tf_op jit(solution)/shard_map/ppermute | solution.py:472
  13.3 1.2 collective-permute-start.4
  14.5 2.9 %collective-permute-start.1 = (bf16[1040,128]{1,0:T(8,128)(2,1)}, bf16[1040,128]{1,0:T(8,128)(2,1)S(1)}, u32[]{:S(2)}, u32[]{:S(2)}) collective-permute-start(bf16[1040,128]{1,0:T(8,128)(2,1)} %get-tuple-element.36), channel_id=1, source_target_pairs={{0,8},{2,10},{4,12},{6,14},{8,0},{10,2},{12,4},{14,6},{1,9},{3,11}... | collective-permute-start | bytes 798728 | tf_op jit(solution)/shard_map/ppermute | solution.py:472
  17.4 2.4 %collective-permute-start.2 = (bf16[1040,128]{1,0:T(8,128)(2,1)}, bf16[1040,128]{1,0:T(8,128)(2,1)S(1)}, u32[]{:S(2)}, u32[]{:S(2)}) collective-permute-start(bf16[1040,128]{1,0:T(8,128)(2,1)} %get-tuple-element.38), channel_id=1, source_target_pairs={{0,10},{2,8},{4,14},{6,12},{8,2},{10,0},{12,6},{14,4},{1,11},{3,9}... | collective-permute-start | bytes 798728 | tf_op jit(solution)/shard_map/ppermute | solution.py:472
  19.8 3.6 %collective-permute-done.6.rest_3_ = bf16[1040,128]{1,0:T(8,128)(2,1)S(1)} collective-permute-done((bf16[1040,128]{1,0:T(8,128)(2,1)}, bf16[1040,128]{1,0:T(8,128)(2,1)S(1)}, u32[]{:S(2)}, u32[]{:S(2)}) %collective-permute-start.6) | collective-permute-done | bytes 266272 | tf_op jit(solution)/shard_map/ppermute | solution.py:472
  23.4 0.7 copy-done.9
  24.1 21.8 %gradient_step.3 = (f32[2,512,512]{2,1,0:T(8,128)}, f32[2,512,512]{2,1,0:T(8,128)}, f32[256,128]{1,0:T(8,128)}, f32[256,128]{1,0:T(8,128)}, f32[256,128]{1,0:T(8,128)}, /*index=5*/f32[256,128]{1,0:T(8,128)}) custom-call(f32[2,512,1024]{2,1,0:T(8,128)} %object_hbm.5, f32[4,2,128,128]{3,2,1,0:T(8,128)} %probe_ref.5, ...), custom_call_target="tpu_custom_call" | custom-call | flops 8589934592 | bytes 16777216 | tf_op jit(solution)/shard_map/gradient_step/pallas_call | solution.py:409
  46.0 0.7 copy-done.5
  46.7 0.1 copy-done.6
  46.7 15.4 %gradient_step.4 = (f32[2,512,512]{2,1,0:T(8,128)}, f32[2,512,512]{2,1,0:T(8,128)}, f32[256,128]{1,0:T(8,128)}, f32[256,128]{1,0:T(8,128)}, f32[256,128]{1,0:T(8,128)}, /*index=5*/f32[256,128]{1,0:T(8,128)}) custom-call(f32[2,512,1024]{2,1,0:T(8,128)} %object_hbm.5, f32[4,2,128,128]{3,2,1,0:T(8,128)} %probe_ref.5, ...), custom_call_target="tpu_custom_call" | custom-call | flops 4294967296 | bytes 16777216 | tf_op jit(solution)/shard_map/gradient_step/pallas_call | solution.py:409
  62.2 0.7 copy-done.3
  62.9 0.1 copy-done.4
  63.0 15.0 %gradient_step.5 = (f32[2,512,512]{2,1,0:T(8,128)}, f32[2,512,512]{2,1,0:T(8,128)}, f32[256,128]{1,0:T(8,128)}, f32[256,128]{1,0:T(8,128)}, f32[256,128]{1,0:T(8,128)}, /*index=5*/f32[256,128]{1,0:T(8,128)}) custom-call(f32[2,512,1024]{2,1,0:T(8,128)} %object_hbm.5, f32[4,2,128,128]{3,2,1,0:T(8,128)} %probe_ref.5, ...), custom_call_target="tpu_custom_call" | custom-call | flops 4294967296 | bytes 16777216 | tf_op jit(solution)/shard_map/gradient_step/pallas_call | solution.py:409
  78.1 2.1 %collective-permute-start.7 = (f32[256,128]{1,0:T(8,128)}, f32[256,128]{1,0:T(8,128)S(1)}, u32[]{:S(2)}, u32[]{:S(2)}) collective-permute-start(f32[256,128]{1,0:T(8,128)} %get-tuple-element.54), channel_id=1, source_target_pairs={{0,1},{1,0},{2,3},{3,2},{4,5},{5,4},{6,7},{7,6},{8,9},{9,8},{10,11... | collective-permute-start | bytes 393224 | tf_op jit(solution)/shard_map/ppermute | solution.py:448
  80.2 0.5 collective-permute-start.13
  80.7 3.4 %collective-permute-done.8 = f32[256,128]{1,0:T(8,128)S(1)} collective-permute-done((f32[256,128]{1,0:T(8,128)}, f32[256,128]{1,0:T(8,128)S(1)}, u32[]{:S(2)}, u32[]{:S(2)}) %collective-permute-start.8) | collective-permute-done | bytes 131104 | tf_op jit(solution)/shard_map/ppermute | solution.py:448
  84.1 0.9 add_add_fusion.2
  85.1 1.3 %collective-permute-start.15 = (f32[2,512,512]{2,1,0:T(8,128)}, f32[2,512,512]{2,1,0:T(8,128)S(1)}, u32[]{:S(2)}, u32[]{:S(2)}) collective-permute-start(f32[2,512,512]{2,1,0:T(8,128)} %get-tuple-element.63), channel_id=1, source_target_pairs={{0,1},{1,0},{2,3},{3,2},{4,5},{5,4},{6,7},{7,6},{8,9},{9,8},{10,11... | collective-permute-start | bytes 6291464 | tf_op jit(solution)/shard_map/ppermute | solution.py:489
  86.3 0.4 collective-permute-start.11
  86.7 18.0 %collective-permute-start.12 = (f32[256,128]{1,0:T(8,128)S(1)}, f32[256,128]{1,0:T(8,128)S(1)}, u32[]{:S(2)}, u32[]{:S(2)}) collective-permute-start(f32[256,128]{1,0:T(8,128)S(1)} %add_add_fusion.2), channel_id=1, source_target_pairs={{0,12},{1,13},{2,14},{3,15},{4,8},{5,9},{6,10},{7,11},{8,4},{9,5},... | collective-permute-start | bytes 393224 | tf_op jit(solution)/shard_map/ppermute | solution.py:448
  104.8 4.9 %collective-permute-start.10 = (f32[256,128]{1,0:T(8,128)S(1)}, f32[256,128]{1,0:T(8,128)S(1)}, u32[]{:S(2)}, u32[]{:S(2)}) collective-permute-start(f32[256,128]{1,0:T(8,128)S(1)} %add_add_fusion.2), channel_id=1, source_target_pairs={{0,4},{1,5},{2,6},{3,7},{4,0},{5,1},{6,2},{7,3},{8,12},{9,13},{10,... | collective-permute-start | bytes 393224 | tf_op jit(solution)/shard_map/ppermute | solution.py:448
  109.7 2.2 %collective-permute-done.12 = f32[256,128]{1,0:T(8,128)S(1)} collective-permute-done((f32[256,128]{1,0:T(8,128)S(1)}, f32[256,128]{1,0:T(8,128)S(1)}, u32[]{:S(2)}, u32[]{:S(2)}) %collective-permute-start.12) | collective-permute-done | bytes 131104 | tf_op jit(solution)/shard_map/ppermute | solution.py:448
  111.9 2.4 %collective-permute-done.10 = f32[256,128]{1,0:T(8,128)S(1)} collective-permute-done((f32[256,128]{1,0:T(8,128)S(1)}, f32[256,128]{1,0:T(8,128)S(1)}, u32[]{:S(2)}, u32[]{:S(2)}) %collective-permute-start.10) | collective-permute-done | bytes 131104 | tf_op jit(solution)/shard_map/ppermute | solution.py:448
  114.4 4.5 %add_add_fusion = f32[2,512,512]{2,1,0:T(8,128)} fusion(f32[2,512,512]{2,1,0:T(8,128)S(1)} %collective-permute-done.15, f32[2,512,512]{2,1,0:T(8,128)S(1)} %collective-permute-done.14, f32[2,512,512]{2,1,0:T(8,128)S(1)} %collective-permute-done.13, f32[2,512,512]{2,1,0:T(8,128)} %get-tuple-element.60, f32[2,512,512]{2,1,0:T(8,128)S(1)} %copy-done, ...), kind=kLoop, calls=%fused_computation | loop fusion | flops 2621440 | bytes 14680064 | tf_op jit(solution)/shard_map/add | solution.py:489
  118.9 1.6 %collective-permute-start.17 = (f32[256,128]{1,0:T(8,128)S(1)}, f32[256,128]{1,0:T(8,128)S(1)}, u32[]{:S(2)}, u32[]{:S(2)}) collective-permute-start(f32[256,128]{1,0:T(8,128)S(1)} %add_add_fusion.1), channel_id=1, source_target_pairs={{0,2},{1,3},{2,0},{3,1},{4,6},{5,7},{6,4},{7,5},{8,10},{9,11},{10,... | collective-permute-start | bytes 393224 | tf_op jit(solution)/shard_map/ppermute | solution.py:448
  120.5 0.2 collective-permute-start.18
  120.7 3.7 %collective-permute-done.16 = f32[256,128]{1,0:T(8,128)S(1)} collective-permute-done((f32[256,128]{1,0:T(8,128)S(1)}, f32[256,128]{1,0:T(8,128)S(1)}, u32[]{:S(2)}, u32[]{:S(2)}) %collective-permute-start.16) | collective-permute-done | bytes 131104 | tf_op jit(solution)/shard_map/ppermute | solution.py:448
  124.5 3.0 %collective-permute-done.17 = f32[256,128]{1,0:T(8,128)S(1)} collective-permute-done((f32[256,128]{1,0:T(8,128)S(1)}, f32[256,128]{1,0:T(8,128)S(1)}, u32[]{:S(2)}, u32[]{:S(2)}) %collective-permute-start.17) | collective-permute-done | bytes 131104 | tf_op jit(solution)/shard_map/ppermute | solution.py:448
  127.5 0.8 pad_maximum_fusion
  (35 shorter events, 0.3 us)
Async XLA Ops:
  4.8 9.7 %collective-permute-start = (bf16[1040,128]{1,0:T(8,128)(2,1)}, bf16[1040,128]{1,0:T(8,128)(2,1)S(1)}, u32[]{:S(2)}, u32[]{:S(2)}) collective-permute-start(bf16[1040,128]{1,0:T(8,128)(2,1)} %get-tuple-element.35), channel_id=1, source_target_pairs={{0,2},{2,0},{4,6},{6,4},{8,10},{10,8},{12,14},{14,12},{1,3},{3,1},... | collective-permute-start | bytes 798728 | tf_op jit(solution)/shard_map/ppermute | solution.py:472
  7.7 9.7 %collective-permute-start.5 = (bf16[1040,128]{1,0:T(8,128)(2,1)}, bf16[1040,128]{1,0:T(8,128)(2,1)S(1)}, u32[]{:S(2)}, u32[]{:S(2)}) collective-permute-start(bf16[1040,128]{1,0:T(8,128)(2,1)} %get-tuple-element.42), channel_id=1, source_target_pairs={{0,4},{2,6},{4,0},{6,2},{8,12},{10,14},{12,8},{14,10},{1,5},{3,7},... | collective-permute-start | bytes 798728 | tf_op jit(solution)/shard_map/ppermute | solution.py:472
  9.3 14.1 %collective-permute-start.6 = (bf16[1040,128]{1,0:T(8,128)(2,1)}, bf16[1040,128]{1,0:T(8,128)(2,1)S(1)}, u32[]{:S(2)}, u32[]{:S(2)}) collective-permute-start(bf16[1040,128]{1,0:T(8,128)(2,1)} %get-tuple-element.43), channel_id=1, source_target_pairs={{0,6},{2,4},{4,2},{6,0},{8,14},{10,12},{12,10},{14,8},{1,7},{3,5},... | collective-permute-start | bytes 798728 | tf_op jit(solution)/shard_map/ppermute | solution.py:472
  9.3 36.6 %collective-permute-start.3 = (bf16[1040,128]{1,0:T(8,128)(2,1)}, bf16[1040,128]{1,0:T(8,128)(2,1)S(1)}, u32[]{:S(2)}, u32[]{:S(2)}) collective-permute-start(bf16[1040,128]{1,0:T(8,128)(2,1)} %get-tuple-element.39), channel_id=1, source_target_pairs={{0,12},{2,14},{4,8},{6,10},{8,4},{10,6},{12,0},{14,2},{1,13},{3,15... | collective-permute-start | bytes 798728 | tf_op jit(solution)/shard_map/ppermute | solution.py:472
  13.3 32.7 %collective-permute-start.4 = (bf16[1040,128]{1,0:T(8,128)(2,1)}, bf16[1040,128]{1,0:T(8,128)(2,1)S(1)}, u32[]{:S(2)}, u32[]{:S(2)}) collective-permute-start(bf16[1040,128]{1,0:T(8,128)(2,1)} %get-tuple-element.40), channel_id=1, source_target_pairs={{0,14},{2,12},{4,10},{6,8},{8,6},{10,4},{12,2},{14,0},{1,15},{3,13... | collective-permute-start | bytes 798728 | tf_op jit(solution)/shard_map/ppermute | solution.py:472
  14.5 8.9 %copy-start.7 = (bf16[1040,128]{1,0:T(8,128)(2,1)}, bf16[1040,128]{1,0:T(8,128)(2,1)S(1)}, u32[]{:S(2)}) copy-start(bf16[1040,128]{1,0:T(8,128)(2,1)S(1)} %collective-permute-done.rest_1_) | copy-start | bytes 798724
  14.5 47.7 %collective-permute-start.1 = (bf16[1040,128]{1,0:T(8,128)(2,1)}, bf16[1040,128]{1,0:T(8,128)(2,1)S(1)}, u32[]{:S(2)}, u32[]{:S(2)}) collective-permute-start(bf16[1040,128]{1,0:T(8,128)(2,1)} %get-tuple-element.36), channel_id=1, source_target_pairs={{0,8},{2,10},{4,12},{6,14},{8,0},{10,2},{12,4},{14,6},{1,9},{3,11}... | collective-permute-start | bytes 798728 | tf_op jit(solution)/shard_map/ppermute | solution.py:472
  17.4 6.0 %copy-start.8 = (bf16[1040,128]{1,0:T(8,128)(2,1)}, bf16[1040,128]{1,0:T(8,128)(2,1)S(1)}, u32[]{:S(2)}) copy-start(bf16[1040,128]{1,0:T(8,128)(2,1)S(1)} %collective-permute-done.5.rest_2_) | copy-start | bytes 798724
  17.4 44.8 %collective-permute-start.2 = (bf16[1040,128]{1,0:T(8,128)(2,1)}, bf16[1040,128]{1,0:T(8,128)(2,1)S(1)}, u32[]{:S(2)}, u32[]{:S(2)}) collective-permute-start(bf16[1040,128]{1,0:T(8,128)(2,1)} %get-tuple-element.38), channel_id=1, source_target_pairs={{0,10},{2,8},{4,14},{6,12},{8,2},{10,0},{12,6},{14,4},{1,11},{3,9}... | collective-permute-start | bytes 798728 | tf_op jit(solution)/shard_map/ppermute | solution.py:472
  23.4 0.7 copy-start.9
  46.0 0.7 copy-start.5
  46.0 0.8 copy-start.6
  62.2 0.7 copy-start.3
  62.2 0.8 copy-start.4
  63.0 17.2 %copy-start.2 = (f32[2,512,512]{2,1,0:T(8,128)S(1)}, f32[2,512,512]{2,1,0:T(8,128)}, u32[]{:S(2)}) copy-start(f32[2,512,512]{2,1,0:T(8,128)} %get-tuple-element.61) | copy-start | bytes 6291460
  63.0 51.4 %copy-start = (f32[2,512,512]{2,1,0:T(8,128)S(1)}, f32[2,512,512]{2,1,0:T(8,128)}, u32[]{:S(2)}) copy-start(f32[2,512,512]{2,1,0:T(8,128)} %get-tuple-element.58) | copy-start | bytes 6291460
  63.0 51.4 %copy-start.1 = (f32[2,512,512]{2,1,0:T(8,128)S(1)}, f32[2,512,512]{2,1,0:T(8,128)}, u32[]{:S(2)}) copy-start(f32[2,512,512]{2,1,0:T(8,128)} %get-tuple-element.59) | copy-start | bytes 6291460
  78.0 6.2 %collective-permute-start.8 = (f32[256,128]{1,0:T(8,128)}, f32[256,128]{1,0:T(8,128)S(1)}, u32[]{:S(2)}, u32[]{:S(2)}) collective-permute-start(f32[256,128]{1,0:T(8,128)} %get-tuple-element.55), channel_id=1, source_target_pairs={{0,2},{1,3},{2,0},{3,1},{4,6},{5,7},{6,4},{7,5},{8,10},{9,11},{10,... | collective-permute-start | bytes 393224 | tf_op jit(solution)/shard_map/ppermute | solution.py:448
  78.0 6.1 %collective-permute-start.9 = (f32[256,128]{1,0:T(8,128)}, f32[256,128]{1,0:T(8,128)S(1)}, u32[]{:S(2)}, u32[]{:S(2)}) collective-permute-start(f32[256,128]{1,0:T(8,128)} %get-tuple-element.56), channel_id=1, source_target_pairs={{0,3},{1,2},{2,1},{3,0},{4,7},{5,6},{6,5},{7,4},{8,11},{9,10},{10,... | collective-permute-start | bytes 393224 | tf_op jit(solution)/shard_map/ppermute | solution.py:448
  78.1 6.0 %collective-permute-start.7 = (f32[256,128]{1,0:T(8,128)}, f32[256,128]{1,0:T(8,128)S(1)}, u32[]{:S(2)}, u32[]{:S(2)}) collective-permute-start(f32[256,128]{1,0:T(8,128)} %get-tuple-element.54), channel_id=1, source_target_pairs={{0,1},{1,0},{2,3},{3,2},{4,5},{5,4},{6,7},{7,6},{8,9},{9,8},{10,11... | collective-permute-start | bytes 393224 | tf_op jit(solution)/shard_map/ppermute | solution.py:448
  80.2 34.1 %collective-permute-start.14 = (f32[2,512,512]{2,1,0:T(8,128)}, f32[2,512,512]{2,1,0:T(8,128)S(1)}, u32[]{:S(2)}, u32[]{:S(2)}) collective-permute-start(f32[2,512,512]{2,1,0:T(8,128)} %get-tuple-element.62), channel_id=1, source_target_pairs={{0,1},{1,0},{2,3},{3,2},{4,5},{5,4},{6,7},{7,6},{8,9},{9,8},{10,11... | collective-permute-start | bytes 6291464 | tf_op jit(solution)/shard_map/ppermute | solution.py:489
  80.2 34.2 %collective-permute-start.13 = (f32[2,512,512]{2,1,0:T(8,128)S(1)}, f32[2,512,512]{2,1,0:T(8,128)S(1)}, u32[]{:S(2)}, u32[]{:S(2)}) collective-permute-start(f32[2,512,512]{2,1,0:T(8,128)S(1)} %copy-done.2), channel_id=1, source_target_pairs={{0,1},{1,0},{2,3},{3,2},{4,5},{5,4},{6,7},{7,6},{8,9},{9,8},{10,11... | collective-permute-start | bytes 6291464 | tf_op jit(solution)/shard_map/ppermute | solution.py:489
  85.1 29.3 %collective-permute-start.15 = (f32[2,512,512]{2,1,0:T(8,128)}, f32[2,512,512]{2,1,0:T(8,128)S(1)}, u32[]{:S(2)}, u32[]{:S(2)}) collective-permute-start(f32[2,512,512]{2,1,0:T(8,128)} %get-tuple-element.63), channel_id=1, source_target_pairs={{0,1},{1,0},{2,3},{3,2},{4,5},{5,4},{6,7},{7,6},{8,9},{9,8},{10,11... | collective-permute-start | bytes 6291464 | tf_op jit(solution)/shard_map/ppermute | solution.py:489
  86.3 18.4 %collective-permute-start.11 = (f32[256,128]{1,0:T(8,128)S(1)}, f32[256,128]{1,0:T(8,128)S(1)}, u32[]{:S(2)}, u32[]{:S(2)}) collective-permute-start(f32[256,128]{1,0:T(8,128)S(1)} %add_add_fusion.2), channel_id=1, source_target_pairs={{0,8},{1,9},{2,10},{3,11},{4,12},{5,13},{6,14},{7,15},{8,0},{9,1},... | collective-permute-start | bytes 393224 | tf_op jit(solution)/shard_map/ppermute | solution.py:448
  86.7 25.2 %collective-permute-start.12 = (f32[256,128]{1,0:T(8,128)S(1)}, f32[256,128]{1,0:T(8,128)S(1)}, u32[]{:S(2)}, u32[]{:S(2)}) collective-permute-start(f32[256,128]{1,0:T(8,128)S(1)} %add_add_fusion.2), channel_id=1, source_target_pairs={{0,12},{1,13},{2,14},{3,15},{4,8},{5,9},{6,10},{7,11},{8,4},{9,5},... | collective-permute-start | bytes 393224 | tf_op jit(solution)/shard_map/ppermute | solution.py:448
  104.8 9.5 %collective-permute-start.10 = (f32[256,128]{1,0:T(8,128)S(1)}, f32[256,128]{1,0:T(8,128)S(1)}, u32[]{:S(2)}, u32[]{:S(2)}) collective-permute-start(f32[256,128]{1,0:T(8,128)S(1)} %add_add_fusion.2), channel_id=1, source_target_pairs={{0,4},{1,5},{2,6},{3,7},{4,0},{5,1},{6,2},{7,3},{8,12},{9,13},{10,... | collective-permute-start | bytes 393224 | tf_op jit(solution)/shard_map/ppermute | solution.py:448
  118.8 5.6 %collective-permute-start.16 = (f32[256,128]{1,0:T(8,128)S(1)}, f32[256,128]{1,0:T(8,128)S(1)}, u32[]{:S(2)}, u32[]{:S(2)}) collective-permute-start(f32[256,128]{1,0:T(8,128)S(1)} %add_add_fusion.1), channel_id=1, source_target_pairs={{0,3},{1,2},{2,1},{3,0},{4,7},{5,6},{6,5},{7,4},{8,11},{9,10},{10,... | collective-permute-start | bytes 393224 | tf_op jit(solution)/shard_map/ppermute | solution.py:448
  118.9 8.6 %collective-permute-start.17 = (f32[256,128]{1,0:T(8,128)S(1)}, f32[256,128]{1,0:T(8,128)S(1)}, u32[]{:S(2)}, u32[]{:S(2)}) collective-permute-start(f32[256,128]{1,0:T(8,128)S(1)} %add_add_fusion.1), channel_id=1, source_target_pairs={{0,2},{1,3},{2,0},{3,1},{4,6},{5,7},{6,4},{7,5},{8,10},{9,11},{10,... | collective-permute-start | bytes 393224 | tf_op jit(solution)/shard_map/ppermute | solution.py:448
  120.5 7.0 %collective-permute-start.18 = (f32[256,128]{1,0:T(8,128)S(1)}, f32[256,128]{1,0:T(8,128)S(1)}, u32[]{:S(2)}, u32[]{:S(2)}) collective-permute-start(f32[256,128]{1,0:T(8,128)S(1)} %add_add_fusion.1), channel_id=1, source_target_pairs={{0,1},{1,0},{2,3},{3,2},{4,5},{5,4},{6,7},{7,6},{8,9},{9,8},{10,11... | collective-permute-start | bytes 393224 | tf_op jit(solution)/shard_map/ppermute | solution.py:448

commit v3 on v2

--- a/solution.py
+++ b/solution.py
@@ -14,7 +14,7 @@
 DIGIT = 16
 LANES = 128
 SQUARE = 4
-CROSS = jnp.float32
+
 BAND = 16
 
 
@@ -100,103 +100,99 @@
     )(tile_ids, rows, cols, patterns)
 
 
-def step_kernel(
-    block_count, capacity, scale, first, last, object_hbm, probe_ref, dft_ref, chirp_ref, *rest
-):
+def prepare_kernel(object_hbm, probe_ref, chirp_ref, field, lit, sems):
+    rows, columns = object_hbm.shape[1:]
+    modes, _, length, _ = probe_ref.shape
+    loads = [
+        pltpu.make_async_copy(
+            object_hbm.at[:, :, tile * LANES : (tile + 1) * LANES],
+            field.at[:, tile, 0:rows, :],
+            sems.at[tile],
+        )
+        for tile in range(columns // LANES)
+    ]
+    for load in loads:
+        load.start()
+    for mode in range(modes):
+        for band in range(length // BAND):
+            at = pl.ds(band * BAND, BAND)
+            cr, ci = chirp_ref[0, at, :], chirp_ref[1, at, :]
+            pr, pi = probe_ref[mode, 0, at, :], probe_ref[mode, 1, at, :]
+            lit[mode, 0, at, :] = cr * pr - ci * pi
+            lit[mode, 1, at, :] = cr * pi + ci * pr
+    for load in loads:
+        load.wait()
+
+
+def prepare(object_field, probe, chirp):
+    _, rows, columns = object_field.shape
+    vmem = pl.BlockSpec(memory_space=pltpu.VMEM)
+    return pl.pallas_call(
+        prepare_kernel,
+        out_shape=[
+            jax.ShapeDtypeStruct((2, columns // LANES + 1, rows + 8, LANES), jnp.float32),
+            jax.ShapeDtypeStruct(probe.shape, jnp.float32),
+        ],
+        in_specs=[pl.BlockSpec(memory_space=pl.ANY), vmem, vmem],
+        out_specs=[vmem, vmem],
+        scratch_shapes=[pltpu.SemaphoreType.DMA((columns // LANES,))],
+        compiler_params=pltpu.CompilerParams(vmem_limit_bytes=16 * 2**20),
+        name="prepare_strip",
+    )(object_field, probe, chirp)
+
+
+def step_kernel(block_count, capacity, scale, first, last, field, lit, dft_ref, chirp_ref, *rest):
     blocks = rest[:block_count]
     rest = rest[block_count:]
     if not first:
-        before = rest[:SQUARE]
+        total_before, grad_before = rest[:2]
+        rest = rest[2:]
+    total, grad = rest[:2]
+    rest = rest[2:]
+    if last:
+        quarters = rest[:SQUARE]
         rest = rest[SQUARE:]
-    after = rest[: 2 + SQUARE]
     (
-        field,
-        total,
         pats,
         heads,
         corners,
         list_row,
         list_col,
         list_pat,
-        lit,
-        grad,
         patch_even,
         patch_odd,
         wide,
         tall,
         in_sem,
         out_sem,
-    ) = rest[2 + SQUARE :]
-    modes, _, length, _ = probe_ref.shape
-    rows, columns = object_hbm.shape[1:]
+    ) = rest
+    modes, _, length, _ = lit.shape
+    column_tiles, rows = total.shape[1:3]
     block_rows = capacity * length + HEAD
     bands = length // BAND
-    pos = lax.axis_index("pos")
-
-    column_tiles = columns // LANES
-    load_field = [
-        pltpu.make_async_copy(
-            object_hbm.at[:, :, tile * LANES : (tile + 1) * LANES],
-            field.at[:, tile, 0:rows, :],
-            in_sem.at[block_count + 1 + tile],
-        )
-        for tile in range(column_tiles)
-    ]
+
     loads = [
         pltpu.make_async_copy(
             blocks[b], pats.at[b * block_rows : (b + 1) * block_rows], in_sem.at[b]
         )
         for b in range(block_count)
     ]
-    for load in loads + load_field:
+    for load in loads:
         load.start()
 
-    half = column_tiles // 2
-    quarter = grad.shape[0] // SQUARE
-    me = lax.axis_index("tile") % (SQUARE // 2) * 2 + pos
-
-    def grad_parts(outsides):
-        return [
-            (grad.at[pl.ds(pl.multiple_of((me ^ turn) * quarter, 8), quarter), :], outside)
-            for turn, outside in enumerate(outsides)
-        ]
-
-    def total_parts(keep_out, send_out):
-        return [
-            (
-                total.at[:, side * half + tile, 0:rows, :],
-                out.at[:, :, tile * LANES : (tile + 1) * LANES],
-            )
-            for out, side in ((send_out, 1 - pos), (keep_out, pos))
-            for tile in range(half)
-        ]
-
-    carried = []
-    if first:
-        grad[...] = jnp.zeros_like(grad)
-    else:
-        carried = [
-            pltpu.make_async_copy(outside, inside, out_sem.at[n])
-            for n, (inside, outside) in enumerate(grad_parts(before))
-        ]
-    for load in carried:
-        load.start()
-
-    def clear(index, carry):
+    def begin(index, carry):
         at = pl.ds(pl.multiple_of(index * 8, 8), 8)
         for plane in range(2):
             for tile in range(column_tiles):
-                total[plane, tile, at, :] = jnp.zeros((8, LANES), jnp.float32)
+                total[plane, tile, at, :] = (
+                    jnp.zeros((8, LANES), jnp.float32)
+                    if first
+                    else total_before[plane, tile, at, :]
+                )
         return carry
 
-    lax.fori_loop(0, rows // 8, clear, 0)
-    for mode in range(modes):
-        for band in range(bands):
-            at = pl.ds(band * BAND, BAND)
-            cr, ci = chirp_ref[0, at, :], chirp_ref[1, at, :]
-            pr, pi = probe_ref[mode, 0, at, :], probe_ref[mode, 1, at, :]
-            lit[mode, 0, at, :] = cr * pr - ci * pi
-            lit[mode, 1, at, :] = cr * pi + ci * pr
+    lax.fori_loop(0, rows // 8, begin, 0)
+    grad[...] = jnp.zeros_like(grad) if first else grad_before[...]
 
     for load in loads:
         load.wait()
@@ -214,18 +210,17 @@
     for b in range(block_count):
 
         def note(rank, at, b=b):
-            first = b * HEAD
-            list_row[at] = corners[first, rank] * DIGIT + corners[first + 1, rank]
-            list_col[at] = corners[first + 2, rank] * DIGIT + corners[first + 3, rank]
+            first_line = b * HEAD
+            list_row[at] = corners[first_line, rank] * DIGIT + corners[first_line + 1, rank]
+            list_col[at] = corners[first_line + 2, rank] * DIGIT + corners[first_line + 3, rank]
             list_pat[at] = b * block_rows + rank * length
             return at + 1
 
         number = lax.fori_loop(0, corners[b * HEAD + 4, 0], note, number)
-    for load in load_field + carried:
-        load.wait()
 
     patch = (patch_even, patch_odd)
-    group = max(BAND, LANES // modes)
+    group = BAND
+    span = 4
     groups = length // group
     tall_rows = modes * group
 
@@ -284,16 +279,22 @@
 
     def row_product(source, table, g):
         out = jnp.dot(
-            tall[source, g * tall_rows : (g + 1) * tall_rows, :],
+            tall[source, g * tall_rows : (g + span) * tall_rows, :],
             dft_ref[table],
             preferred_element_type=jnp.float32,
         )
         return [
-            (
-                out[mode * group : (mode + 1) * group, 0:length],
-                out[mode * group : (mode + 1) * group, length : 2 * length],
-            )
-            for mode in range(modes)
+            [
+                tuple(
+                    out[
+                        k * tall_rows + mode * group : k * tall_rows + (mode + 1) * group,
+                        plane * length : (plane + 1) * length,
+                    ]
+                    for plane in range(2)
+                )
+                for mode in range(modes)
+            ]
+            for k in range(span)
         ]
 
     def far_chunks(index, side):
@@ -301,7 +302,10 @@
         weight = jnp.where((index >= 0) & (index < number), jnp.float32(1.0), jnp.float32(0.0))
 
         def chunk(g):
-            waves = row_product(side, 1, g)
+            for k, waves in enumerate(row_product(side, 1, g)):
+                amplitude(g + k, waves)
+
+        def amplitude(g, waves):
             bright = None
             for fr, fi in waves:
                 power = fr * fr + fi * fi
@@ -317,17 +321,20 @@
                     jnp.bfloat16
                 )
 
-        return [functools.partial(chunk, g) for g in range(groups)]
+        return [functools.partial(chunk, g) for g in range(0, groups, span)]
 
     def step_chunks(index, side):
         row, col, shift, _ = item(index)
         slot = (index >> 1) & 1
 
         def chunk(g):
+            for k, waves in enumerate(row_product(2 + side, 0, g)):
+                update(g + k, waves)
+
+        def update(g, waves):
             at = pl.ds(g * group, group)
             at_field = pl.ds(row + g * group, group)
             lane = lax.broadcasted_iota(jnp.int32, (group, LANES), 1)
-            waves = row_product(2 + side, 0, g)
             pr, pi = patch[side][slot, 0, at, :], patch[side][slot, 1, at, :]
             steps = [None, None]
             for mode in range(modes):
@@ -350,7 +357,7 @@
             for (plane, tile), value in zip(places, sums):
                 total[plane, tile, at_field, :] = value
 
-        return [functools.partial(chunk, g) for g in range(groups)]
+        return [functools.partial(chunk, g) for g in range(0, groups, span)]
 
     def run(*lists):
         order = []
@@ -375,7 +382,9 @@
         run(column_chunks(0, 0, 0), exit_chunks(jnp.int32(1), 1))
         lax.fori_loop(0, number // 2 + 1, visit, 0)
 
-    for mode in range(modes if last else 0):
+    if not last:
+        return
+    for mode in range(modes):
         for band in range(bands):
             at = pl.ds(band * BAND, BAND)
             at_gr = pl.ds((2 * mode) * length + band * BAND, BAND)
@@ -384,11 +393,16 @@
             gr, gi = grad[at_gr, :], grad[at_gi, :]
             grad[at_gr, :] = cr * gr + ci * gi
             grad[at_gi, :] = cr * gi - ci * gr
+    pos = lax.axis_index("pos")
+    me = lax.axis_index("tile") % (SQUARE // 2) * 2 + pos
+    quarter = grad.shape[0] // SQUARE
+    parts = [
+        (grad.at[pl.ds(pl.multiple_of((me ^ turn) * quarter, 8), quarter), :], outside)
+        for turn, outside in enumerate(quarters)
+    ]
     stores = [
         pltpu.make_async_copy(inside, outside, out_sem.at[n])
-        for n, (inside, outside) in enumerate(
-            grad_parts(after[2:]) + total_parts(*after[:2])
-        )
+        for n, (inside, outside) in enumerate(parts)
     ]
     for store in stores:
         store.start()
@@ -396,51 +410,112 @@
         store.wait()
 
 
-def step(object_field, probe, blocks, tables, scale, capacity, before=None, last=True):
-    modes, _, length, _ = probe.shape
-    rows, columns = object_field.shape[1:]
+def step(field, lit, blocks, tables, scale, capacity, before, last):
+    modes, _, length, _ = lit.shape
+    column_tiles, rows = field.shape[1:3]
     count = len(blocks)
     slots = count * capacity
     vmem = pl.BlockSpec(memory_space=pltpu.VMEM)
     hbm = pl.BlockSpec(memory_space=pl.ANY)
     f32, bf16 = jnp.float32, jnp.bfloat16
-    padded = (2, columns // LANES + 1, rows + 8, LANES)
-    work = slots * modes * 4 * 8 * length**3
+    outs = [
+        jax.ShapeDtypeStruct(field.shape, f32),
+        jax.ShapeDtypeStruct((2 * modes * length, length), f32),
+    ]
+    specs = [vmem, vmem]
+    if last:
+        outs += [jax.ShapeDtypeStruct((2 * modes * length // SQUARE, length), f32)] * SQUARE
+        specs += [hbm] * SQUARE
     return pl.pallas_call(
-        functools.partial(
-            step_kernel, count, capacity, scale, before is None, last
-        ),
-        out_shape=[
-            jax.ShapeDtypeStruct((2, rows, columns // 2), f32),
-            jax.ShapeDtypeStruct((2, rows, columns // 2), f32),
-        ]
-        + [jax.ShapeDtypeStruct((2 * modes * length // SQUARE, length), f32)] * SQUARE,
-        in_specs=[hbm, vmem, vmem, vmem] + [hbm] * (count + len(before or ())),
-        out_specs=[hbm] * (2 + SQUARE),
+        functools.partial(step_kernel, count, capacity, scale, not before, last),
+        out_shape=outs,
+        in_specs=[vmem] * 4 + [hbm] * count + [vmem] * len(before),
+        out_specs=specs,
         scratch_shapes=[
-            pltpu.VMEM(padded, f32),
-            pltpu.VMEM(padded, f32),
             pltpu.VMEM((count * (capacity * length + HEAD), length), bf16),
             pltpu.VMEM((count * HEAD, LANES), jnp.int32),
             pltpu.SMEM((count * HEAD, LANES), jnp.int32),
             pltpu.SMEM((slots,), jnp.int32),
             pltpu.SMEM((slots,), jnp.int32),
             pltpu.SMEM((slots,), jnp.int32),
-            pltpu.VMEM((modes, 2, length, length), f32),
-            pltpu.VMEM((2 * modes * length, length), f32),
             pltpu.VMEM((2, 2, length, length), f32),
             pltpu.VMEM((2, 2, length, length), f32),
             pltpu.VMEM((3, 2 * length, modes * length), bf16),
             pltpu.VMEM((4, modes * length, 2 * length), bf16),
-            pltpu.SemaphoreType.DMA((count + 1 + columns // LANES,)),
-            pltpu.SemaphoreType.DMA((SQUARE + columns // LANES,)),
+            pltpu.SemaphoreType.DMA((count + 1,)),
+            pltpu.SemaphoreType.DMA((SQUARE,)),
         ],
-        compiler_params=pltpu.CompilerParams(vmem_limit_bytes=56 * 2**20),
+        compiler_params=pltpu.CompilerParams(vmem_limit_bytes=26 * 2**20),
         cost_estimate=pl.CostEstimate(
-            flops=work, bytes_accessed=16 * 2**20, transcendentals=slots * length**2
+            flops=slots * modes * 4 * 8 * length**3,
+            bytes_accessed=16 * 2**20,
+            transcendentals=slots * length**2,
         ),
         name="gradient_step",
-    )(object_field, probe, *tables, *blocks, *(before or ()))
+    )(field, lit, *tables, *blocks, *before)
+
+
+def give_kernel(total, send, sems):
+    half = send.shape[2] // LANES
+    side = 1 - lax.axis_index("pos")
+    stores = [
+        pltpu.make_async_copy(
+            total.at[:, side * half + tile, 0 : send.shape[1], :],
+            send.at[:, :, tile * LANES : (tile + 1) * LANES],
+            sems.at[tile],
+        )
+        for tile in range(half)
+    ]
+    for store in stores:
+        store.start()
+    for store in stores:
+        store.wait()
+
+
+def finish_kernel(total, received, out):
+    half = out.shape[2] // LANES
+    side = lax.axis_index("pos")
+
+    def add(index, carry):
+        at = pl.ds(pl.multiple_of(index * 8, 8), 8)
+        for plane in range(2):
+            for tile in range(half):
+                lanes = pl.ds(tile * LANES, LANES)
+                out[plane, at, lanes] = (
+                    total[plane, side * half + tile, at, :] + received[plane, at, lanes]
+                )
+        return carry
+
+    lax.fori_loop(0, out.shape[1] // 8, add, 0)
+
+
+def halves(total, received=None):
+    _, column_tiles, rows, _ = total.shape
+    half = (column_tiles - 1) // 2
+    shape = jax.ShapeDtypeStruct((2, rows - 8, half * LANES), jnp.float32)
+    vmem = pl.BlockSpec(memory_space=pltpu.VMEM)
+    cost = pl.CostEstimate(flops=2**20, bytes_accessed=4 * 2**20, transcendentals=0)
+    limit = pltpu.CompilerParams(vmem_limit_bytes=16 * 2**20)
+    if received is None:
+        return pl.pallas_call(
+            give_kernel,
+            out_shape=shape,
+            in_specs=[vmem],
+            out_specs=pl.BlockSpec(memory_space=pl.ANY),
+            scratch_shapes=[pltpu.SemaphoreType.DMA((half,))],
+            compiler_params=limit,
+            cost_estimate=cost,
+            name="give_half",
+        )(total)
+    return pl.pallas_call(
+        finish_kernel,
+        out_shape=shape,
+        in_specs=[vmem, vmem],
+        out_specs=vmem,
+        compiler_params=limit,
+        cost_estimate=cost,
+        name="add_half",
+    )(total, received)
 
 
 def from_peer(array, turn, devices):
@@ -462,35 +537,29 @@
     scale = 1.0 / math.sqrt(number * tile_count * pos_count)
     tables = (jnp.asarray(dft_tables(length)), jnp.asarray(chirp_table(length)))
     blocks = pack(patterns, scan_tile[:, 0], scan_row, scan_col, tile_count, capacity)
+    field, lit = prepare(object_field, probe, tables[1])
     late = tile_count * 3 // 4
     order = [*range(late - tile_count // 4), *range(late, tile_count), *range(tile_count // 2, late)]
     arrived = [blocks[0]]
     for hop in order[1:]:
         block = blocks[hop]
         if len(arrived) >= late:
-            block = lax.optimization_barrier((block, arrived[1]))[0]
+            block = lax.optimization_barrier((block, arrived[1], lit))[0]
         arrived.append(lax.ppermute(block, "tile", [(i, i ^ hop) for i in range(tile_count)]))
     cuts = [0, tile_count // 2, tile_count * 3 // 4, tile_count]
-    grads, keeps, sends = None, [], []
+    sums = ()
     for a, b in zip(cuts[:-1], cuts[1:]):
-        keep, send, *grads = step(
-            object_field, probe, arrived[a:b], tables, scale, capacity, grads, b == tile_count
-        )
-        keeps.append(keep)
-        sends.append(send)
+        sums = step(field, lit, arrived[a:b], tables, scale, capacity, sums, b == tile_count)
+    total, grads = sums[0], sums[2:]
 
     devices = tile_count * pos_count
     inside, across = range(1, SQUARE), range(SQUARE, devices, SQUARE)
     part = tree_sum([grads[0]] + [from_peer(grads[turn], turn, devices) for turn in inside])
-    sends[-1], part = lax.optimization_barrier((sends[-1], part))
-    other = [(0, 1), (1, 0)]
-    object_step = sum(keeps[1:], keeps[0])
-    for send in sends:
-        object_step = object_step + lax.ppermute(send, "pos", other)
-    part = part.astype(CROSS)
+    send, part = lax.optimization_barrier((halves(total), part))
+    object_step = halves(total, lax.ppermute(send, "pos", [(0, 1), (1, 0)]))
     part = tree_sum(
-        [part.astype(jnp.float32)]
-        + [from_peer(part, turn, devices).astype(jnp.float32) for turn in across]
+        [part]
+        + [from_peer(part, turn, devices) for turn in across]
     )
     part, object_step = lax.optimization_barrier((part, object_step))
     square = [part] + [from_peer(part, turn, devices) for turn in inside]

time: 128 us -> 105 us (0.82); the launches traced: 128 us -> 107 us
  Pallas kernels: 56.3 us -> 29.2 us
  waiting for transfers between devices: 18.4 us -> 43.3 us
  starting transfers between devices: 44.2 us -> 28.2 us
  other arithmetic: 6.31 us -> 0.93 us
  local copies, waits for them, and re-layouts: 2.26 us -> 4.34 us
    pallas_call x3 -> x6, Pallas kernels: 52.2 us -> 25 us  [the longest x3 22.1 us: step(): pl.pallas_call(functools.partial(step_kernel, count, capacity, scale, not...]
    ppermute x7, waiting for transfers between devices: 3.63 us -> 22.5 us  [on_device(): lax.ppermute(block, 'tile', [(i, i ^ hop) for i in range(tile_count)])]
    ppermute x9, starting transfers between devices: 27.4 us -> 15.7 us  [from_peer(): return lax.ppermute(array, ('tile', 'pos'), pairs)]
    ppermute x9, waiting for transfers between devices: 14.8 us -> 20.8 us  [from_peer(): return lax.ppermute(array, ('tile', 'pos'), pairs)]
    add x1 -> x0, other arithmetic: 4.47 us -> none  [on_device(): object_step = object_step + lax.ppermute(send, 'pos', other)]
    ppermute x7, starting transfers between devices: 15 us -> 12.4 us  [on_device(): lax.ppermute(block, 'tile', [(i, i ^ hop) for i in range(tile_count)])]
    unnamed x20 -> x16, local copies, waits for them, and re-layouts: 2.26 us -> 4.34 us
    ppermute x3 -> x1, starting transfers between devices: 1.8 us -> 0.08 us  [on_device(): object_step = halves(total, lax.ppermute(send, 'pos', [(0, 1), (1, 0)]))]
  transfers between devices with their start and end apart: 19 -> 17, of which waited for: 6 -> 11; matrix products, arithmetic and copies ran while one was open for 1% -> 0% of each run, Pallas kernels for 29% -> 15%
where the time goes in v3:
time: 105 us; the launch traced here: 107 us
  waiting for transfers between devices  43.3 us (41%)
  Pallas kernels  29.2 us (28%)
  starting transfers between devices  28.2 us (27%)
  local copies, waits for them, and re-layouts  4.34 us (4%)
    ppermute x7, waiting for transfers between devices, on_device(): lax.ppermute(block, 'tile', [(i, i ^ hop) for i in range(tile_count)])  22.5 us
    pallas_call x3, Pallas kernels, step(): pl.pallas_call(functools.partial(step_kernel, count, capacity, scale, not...  22.1 us
    ppermute x9, waiting for transfers between devices, from_peer(): return lax.ppermute(array, ('tile', 'pos'), pairs)  20.8 us
    ppermute x9, starting transfers between devices, from_peer(): return lax.ppermute(array, ('tile', 'pos'), pairs)  15.7 us
    ppermute x7, starting transfers between devices, on_device(): lax.ppermute(block, 'tile', [(i, i ^ hop) for i in range(tile_count)])  12.4 us
    unnamed x16, local copies, waits for them, and re-layouts  4.34 us
    pallas_call x1, Pallas kernels, pack(): pl.pallas_call(functools.partial(pack_kernel, tile_count, capacity), out_...  4.16 us
  transfers between devices with their start and end apart: 17, of which 11 were waited for; matrix products, arithmetic and copies ran while one was open for 0% of the time, Pallas kernels for 15%

profile of v3, /device:TPU:0, one launch (start us, length us, event | category | flops | bytes accessed | tf_op | source)
XLA Modules:
  0.0 106.7 jit_solution(3304283734509200247)
XLA Ops:
  0.7 4.2 %pack_patterns.1 = (bf16[1040,128]{1,0:T(8,128)(2,1)}, bf16[1040,128]{1,0:T(8,128)(2,1)}, bf16[1040,128]{1,0:T(8,128)(2,1)}, bf16[1040,128]{1,0:T(8,128)(2,1)}, ...) custom-call(s32[32]{0:T(128)} %bitcast.3, ...), custom_call_target="tpu_custom_call" | custom-call | tf_op jit(solution)/shard_map/pack_patterns/pallas_call | solution.py:89
  4.8 3.0 %collective-permute-start = (bf16[1040,128]{1,0:T(8,128)(2,1)}, bf16[1040,128]{1,0:T(8,128)(2,1)S(1)}, u32[]{:S(2)}, u32[]{:S(2)}) collective-permute-start(bf16[1040,128]{1,0:T(8,128)(2,1)} %get-tuple-element.30), channel_id=1, source_target_pairs={{0,2},{2,0},{4,6},{6,4},{8,10},{10,8},{12,14},{14,12},{1,3},{3,1},... | collective-permute-start | bytes 798728 | tf_op jit(solution)/shard_map/ppermute | solution.py:548
  7.8 1.6 %collective-permute-start.5 = (bf16[1040,128]{1,0:T(8,128)(2,1)}, bf16[1040,128]{1,0:T(8,128)(2,1)S(1)}, u32[]{:S(2)}, u32[]{:S(2)}) collective-permute-start(bf16[1040,128]{1,0:T(8,128)(2,1)} %get-tuple-element.37), channel_id=1, source_target_pairs={{0,4},{2,6},{4,0},{6,2},{8,12},{10,14},{12,8},{14,10},{1,5},{3,7},... | collective-permute-start | bytes 798728 | tf_op jit(solution)/shard_map/ppermute | solution.py:548
  9.4 4.0 %collective-permute-start.3 = (bf16[1040,128]{1,0:T(8,128)(2,1)}, bf16[1040,128]{1,0:T(8,128)(2,1)S(1)}, u32[]{:S(2)}, u32[]{:S(2)}) collective-permute-start(bf16[1040,128]{1,0:T(8,128)(2,1)} %get-tuple-element.34), channel_id=1, source_target_pairs={{0,12},{2,14},{4,8},{6,10},{8,4},{10,6},{12,0},{14,2},{1,13},{3,15... | collective-permute-start | bytes 798728 | tf_op jit(solution)/shard_map/ppermute | solution.py:548
  13.4 1.2 %collective-permute-start.4 = (bf16[1040,128]{1,0:T(8,128)(2,1)}, bf16[1040,128]{1,0:T(8,128)(2,1)S(1)}, u32[]{:S(2)}, u32[]{:S(2)}) collective-permute-start(bf16[1040,128]{1,0:T(8,128)(2,1)} %get-tuple-element.35), channel_id=1, source_target_pairs={{0,14},{2,12},{4,10},{6,8},{8,6},{10,4},{12,2},{14,0},{1,15},{3,13... | collective-permute-start | bytes 798728 | tf_op jit(solution)/shard_map/ppermute | solution.py:548
  14.5 2.2 %copy-done = f32[2,512,1024]{2,1,0:T(8,128)S(1)} copy-done((f32[2,512,1024]{2,1,0:T(8,128)S(1)}, f32[2,512,1024]{2,1,0:T(8,128)}, u32[]{:S(2)}) %copy-start) | copy-done | bytes 4194328
  16.7 1.0 copy-done.1
  17.8 0.9 copy-done.2
  18.7 0.7 prepare_strip.1
  19.6 0.8 collective-permute-start.1
  20.4 1.9 %collective-permute-start.2 = (bf16[1040,128]{1,0:T(8,128)(2,1)S(1)}, bf16[1040,128]{1,0:T(8,128)(2,1)S(1)}, u32[]{:S(2)}, u32[]{:S(2)}) collective-permute-start(bf16[1040,128]{1,0:T(8,128)(2,1)S(1)} %copy-done.6), channel_id=1, source_target_pairs={{0,10},{2,8},{4,14},{6,12},{8,2},{10,0},{12,6},{14,4},{1,11},{3,9}... | collective-permute-start | bytes 798728 | tf_op jit(solution)/shard_map/ppermute | solution.py:548
  22.3 1.1 %collective-permute-done.6.rest_3_ = bf16[1040,128]{1,0:T(8,128)(2,1)S(1)} collective-permute-done((bf16[1040,128]{1,0:T(8,128)(2,1)}, bf16[1040,128]{1,0:T(8,128)(2,1)S(1)}, u32[]{:S(2)}, u32[]{:S(2)}) %collective-permute-start.6) | collective-permute-done | bytes 266272 | tf_op jit(solution)/shard_map/ppermute | solution.py:548
  23.5 9.7 %gradient_step.3 = (f32[2,9,520,128]{3,2,1,0:T(8,128)S(1)}, f32[1024,128]{1,0:T(8,128)S(1)}) custom-call(f32[2,9,520,128]{3,2,1,0:T(8,128)S(1)} %get-tuple-element.27.field, f32[4,2,128,128]{3,2,1,0:T(8,128)S(1)} %get-tuple-element.28.lit, bf16[2,256,256]{2,1,0:T(8,128)(2,1)S(1)} %copy-done.5, f32[2,128,128]{2,1,0:T(8,128)S(1)} %copy-done.3, ...), custom_call_target="tpu_custom_call" | custom-call | flops 8589934592 | bytes 16777216 | tf_op jit(solution)/shard_map/gradient_step/pallas_call | solution.py:429
  33.1 4.5 %collective-permute-done.4.rest_1_ = bf16[1040,128]{1,0:T(8,128)(2,1)S(1)} collective-permute-done((bf16[1040,128]{1,0:T(8,128)(2,1)}, bf16[1040,128]{1,0:T(8,128)(2,1)S(1)}, u32[]{:S(2)}, u32[]{:S(2)}) %collective-permute-start.4) | collective-permute-done | bytes 266272 | tf_op jit(solution)/shard_map/ppermute | solution.py:548
  37.6 5.4 %gradient_step.4 = (f32[2,9,520,128]{3,2,1,0:T(8,128)S(1)}, f32[1024,128]{1,0:T(8,128)S(1)}) custom-call(f32[2,9,520,128]{3,2,1,0:T(8,128)S(1)} %get-tuple-element.27.field, f32[4,2,128,128]{3,2,1,0:T(8,128)S(1)} %get-tuple-element.28.lit, bf16[2,256,256]{2,1,0:T(8,128)(2,1)S(1)} %copy-done.5, f32[2,128,128]{2,1,0:T(8,128)S(1)} %copy-done.3, ...), custom_call_target="tpu_custom_call" | custom-call | flops 4294967296 | bytes 16777216 | tf_op jit(solution)/shard_map/gradient_step/pallas_call | solution.py:429
  43.0 12.7 %collective-permute-done.1.rest_0_ = bf16[1040,128]{1,0:T(8,128)(2,1)S(1)} collective-permute-done((bf16[1040,128]{1,0:T(8,128)(2,1)S(1)}, bf16[1040,128]{1,0:T(8,128)(2,1)S(1)}, u32[]{:S(2)}, u32[]{:S(2)}) %collective-permute-start.1) | collective-permute-done | bytes 266272 | tf_op jit(solution)/shard_map/ppermute | solution.py:548
  55.8 4.2 %collective-permute-done.2.rest_1_ = bf16[1040,128]{1,0:T(8,128)(2,1)S(1)} collective-permute-done((bf16[1040,128]{1,0:T(8,128)(2,1)S(1)}, bf16[1040,128]{1,0:T(8,128)(2,1)S(1)}, u32[]{:S(2)}, u32[]{:S(2)}) %collective-permute-start.2) | collective-permute-done | bytes 266272 | tf_op jit(solution)/shard_map/ppermute | solution.py:548
  60.0 7.0 %gradient_step.5 = (f32[2,9,520,128]{3,2,1,0:T(8,128)S(1)}, f32[1024,128]{1,0:T(8,128)}, f32[256,128]{1,0:T(8,128)S(1)}, f32[256,128]{1,0:T(8,128)S(1)}, f32[256,128]{1,0:T(8,128)S(1)}, /*index=5*/f32[256,128]{1,0:T(8,128)S(1)}) custom-call(f32[2,9,520,128]{3,2,1,0:T(8,128)S(1)} %get-tuple-element.27.field, f32[4,2,128,128]{3,2,1,0:T(8,128)S(1)} %get-tuple-element.28.lit, ...), custom_call_target="tpu_custom_call" | custom-call | flops 4294967296 | bytes 16777216 | tf_op jit(solution)/shard_map/gradient_step/pallas_call | solution.py:429
  67.0 5.9 %collective-permute-start.8 = (f32[256,128]{1,0:T(8,128)S(1)}, f32[256,128]{1,0:T(8,128)S(1)}, u32[]{:S(2)}, u32[]{:S(2)}) collective-permute-start(f32[256,128]{1,0:T(8,128)S(1)} %get-tuple-element.46), channel_id=1, source_target_pairs={{0,2},{1,3},{2,0},{3,1},{4,6},{5,7},{6,4},{7,5},{8,10},{9,11},{10,... | collective-permute-start | bytes 393224 | tf_op jit(solution)/shard_map/ppermute | solution.py:523
  73.4 2.9 %collective-permute-done.8 = f32[256,128]{1,0:T(8,128)S(1)} collective-permute-done((f32[256,128]{1,0:T(8,128)S(1)}, f32[256,128]{1,0:T(8,128)S(1)}, u32[]{:S(2)}, u32[]{:S(2)}) %collective-permute-start.8) | collective-permute-done | bytes 131104 | tf_op jit(solution)/shard_map/ppermute | solution.py:523
  76.3 2.4 %collective-permute-done.9 = f32[256,128]{1,0:T(8,128)S(1)} collective-permute-done((f32[256,128]{1,0:T(8,128)S(1)}, f32[256,128]{1,0:T(8,128)S(1)}, u32[]{:S(2)}, u32[]{:S(2)}) %collective-permute-start.9) | collective-permute-done | bytes 131104 | tf_op jit(solution)/shard_map/ppermute | solution.py:523
  78.7 7.2 %collective-permute-start.11 = (f32[256,128]{1,0:T(8,128)S(1)}, f32[256,128]{1,0:T(8,128)S(1)}, u32[]{:S(2)}, u32[]{:S(2)}) collective-permute-start(f32[256,128]{1,0:T(8,128)S(1)} %add_add_fusion.1), channel_id=1, source_target_pairs={{0,8},{1,9},{2,10},{3,11},{4,12},{5,13},{6,14},{7,15},{8,0},{9,1},... | collective-permute-start | bytes 393224 | tf_op jit(solution)/shard_map/ppermute | solution.py:523
  86.0 0.6 collective-permute-start.10
  86.6 3.7 %collective-permute-done.11 = f32[256,128]{1,0:T(8,128)S(1)} collective-permute-done((f32[256,128]{1,0:T(8,128)S(1)}, f32[256,128]{1,0:T(8,128)S(1)}, u32[]{:S(2)}, u32[]{:S(2)}) %collective-permute-start.11) | collective-permute-done | bytes 131104 | tf_op jit(solution)/shard_map/ppermute | solution.py:523
  90.3 3.9 %collective-permute-done.12 = f32[256,128]{1,0:T(8,128)S(1)} collective-permute-done((f32[256,128]{1,0:T(8,128)S(1)}, f32[256,128]{1,0:T(8,128)S(1)}, u32[]{:S(2)}, u32[]{:S(2)}) %collective-permute-start.12) | collective-permute-done | bytes 131104 | tf_op jit(solution)/shard_map/ppermute | solution.py:523
  94.2 1.2 %collective-permute-done.10 = f32[256,128]{1,0:T(8,128)S(1)} collective-permute-done((f32[256,128]{1,0:T(8,128)S(1)}, f32[256,128]{1,0:T(8,128)S(1)}, u32[]{:S(2)}, u32[]{:S(2)}) %collective-permute-start.10) | collective-permute-done | bytes 131104 | tf_op jit(solution)/shard_map/ppermute | solution.py:523
  95.4 1.8 %add_half.1 = f32[2,512,512]{2,1,0:T(8,128)} custom-call(f32[2,9,520,128]{3,2,1,0:T(8,128)S(1)} %get-tuple-element.43.total, f32[2,512,512]{2,1,0:T(8,128)S(1)} %collective-permute-done.13.received), custom_call_target="tpu_custom_call" | custom-call | flops 1048576 | bytes 4194304 | tf_op jit(solution)/shard_map/add_half/pallas_call | solution.py:510
  97.2 0.8 collective-permute-start.14
  97.9 0.8 collective-permute-start.15
  99.1 3.8 %collective-permute-done.14 = f32[256,128]{1,0:T(8,128)S(1)} collective-permute-done((f32[256,128]{1,0:T(8,128)S(1)}, f32[256,128]{1,0:T(8,128)S(1)}, u32[]{:S(2)}, u32[]{:S(2)}) %collective-permute-start.14) | collective-permute-done | bytes 131104 | tf_op jit(solution)/shard_map/ppermute | solution.py:523
  102.9 2.9 %collective-permute-done.15 = f32[256,128]{1,0:T(8,128)S(1)} collective-permute-done((f32[256,128]{1,0:T(8,128)S(1)}, f32[256,128]{1,0:T(8,128)S(1)}, u32[]{:S(2)}, u32[]{:S(2)}) %collective-permute-start.15) | collective-permute-done | bytes 131104 | tf_op jit(solution)/shard_map/ppermute | solution.py:523
  105.8 0.8 pad_maximum_fusion
  (29 shorter events, 1.3 us)
Async XLA Ops:
  0.6 22.8 %copy-start.3 = (f32[2,128,128]{2,1,0:T(8,128)S(1)}, f32[2,128,128]{2,1,0:T(8,128)}, u32[]{:S(2)}) copy-start(f32[2,128,128]{2,1,0:T(8,128)} %constant.19.clone.chirp_ref) | copy-start | bytes 393220
  0.6 22.8 %copy-start.5 = (bf16[2,256,256]{2,1,0:T(8,128)(2,1)S(1)}, bf16[2,256,256]{2,1,0:T(8,128)(2,1)}, u32[]{:S(2)}) copy-start(bf16[2,256,256]{2,1,0:T(8,128)(2,1)} %constant.18.clone.dft_ref) | copy-start | bytes 786436
  4.8 14.6 %collective-permute-start = (bf16[1040,128]{1,0:T(8,128)(2,1)}, bf16[1040,128]{1,0:T(8,128)(2,1)S(1)}, u32[]{:S(2)}, u32[]{:S(2)}) collective-permute-start(bf16[1040,128]{1,0:T(8,128)(2,1)} %get-tuple-element.30), channel_id=1, source_target_pairs={{0,2},{2,0},{4,6},{6,4},{8,10},{10,8},{12,14},{14,12},{1,3},{3,1},... | collective-permute-start | bytes 798728 | tf_op jit(solution)/shard_map/ppermute | solution.py:548
  7.8 12.6 %collective-permute-start.5 = (bf16[1040,128]{1,0:T(8,128)(2,1)}, bf16[1040,128]{1,0:T(8,128)(2,1)S(1)}, u32[]{:S(2)}, u32[]{:S(2)}) collective-permute-start(bf16[1040,128]{1,0:T(8,128)(2,1)} %get-tuple-element.37), channel_id=1, source_target_pairs={{0,4},{2,6},{4,0},{6,2},{8,12},{10,14},{12,8},{14,10},{1,5},{3,7},... | collective-permute-start | bytes 798728 | tf_op jit(solution)/shard_map/ppermute | solution.py:548
  9.4 14.1 %collective-permute-start.6 = (bf16[1040,128]{1,0:T(8,128)(2,1)}, bf16[1040,128]{1,0:T(8,128)(2,1)S(1)}, u32[]{:S(2)}, u32[]{:S(2)}) collective-permute-start(bf16[1040,128]{1,0:T(8,128)(2,1)} %get-tuple-element.38), channel_id=1, source_target_pairs={{0,6},{2,4},{4,2},{6,0},{8,14},{10,12},{12,10},{14,8},{1,7},{3,5},... | collective-permute-start | bytes 798728 | tf_op jit(solution)/shard_map/ppermute | solution.py:548
  9.4 23.8 %collective-permute-start.3 = (bf16[1040,128]{1,0:T(8,128)(2,1)}, bf16[1040,128]{1,0:T(8,128)(2,1)S(1)}, u32[]{:S(2)}, u32[]{:S(2)}) collective-permute-start(bf16[1040,128]{1,0:T(8,128)(2,1)} %get-tuple-element.34), channel_id=1, source_target_pairs={{0,12},{2,14},{4,8},{6,10},{8,4},{10,6},{12,0},{14,2},{1,13},{3,15... | collective-permute-start | bytes 798728 | tf_op jit(solution)/shard_map/ppermute | solution.py:548
  13.4 24.3 %collective-permute-start.4 = (bf16[1040,128]{1,0:T(8,128)(2,1)}, bf16[1040,128]{1,0:T(8,128)(2,1)S(1)}, u32[]{:S(2)}, u32[]{:S(2)}) collective-permute-start(bf16[1040,128]{1,0:T(8,128)(2,1)} %get-tuple-element.35), channel_id=1, source_target_pairs={{0,14},{2,12},{4,10},{6,8},{8,6},{10,4},{12,2},{14,0},{1,15},{3,13... | collective-permute-start | bytes 798728 | tf_op jit(solution)/shard_map/ppermute | solution.py:548
  14.5 2.2 %copy-start = (f32[2,512,1024]{2,1,0:T(8,128)S(1)}, f32[2,512,1024]{2,1,0:T(8,128)}, u32[]{:S(2)}) copy-start(f32[2,512,1024]{2,1,0:T(8,128)} %object_hbm.1) | copy-start | bytes 12582916
  16.7 1.0 copy-start.1
  17.8 0.9 copy-start.2
  18.7 1.0 copy-start.7
  18.7 1.7 %copy-start.6 = (bf16[1040,128]{1,0:T(8,128)(2,1)S(1)}, bf16[1040,128]{1,0:T(8,128)(2,1)}, u32[]{:S(2)}) copy-start(bf16[1040,128]{1,0:T(8,128)(2,1)} %get-tuple-element.33) | copy-start | bytes 798724
  18.7 4.8 %copy-start.4 = (bf16[1040,128]{1,0:T(8,128)(2,1)S(1)}, bf16[1040,128]{1,0:T(8,128)(2,1)}, u32[]{:S(2)}) copy-start(bf16[1040,128]{1,0:T(8,128)(2,1)} %get-tuple-element.36.rest_0_) | copy-start | bytes 798724
  19.6 36.1 %collective-permute-start.1 = (bf16[1040,128]{1,0:T(8,128)(2,1)S(1)}, bf16[1040,128]{1,0:T(8,128)(2,1)S(1)}, u32[]{:S(2)}, u32[]{:S(2)}) collective-permute-start(bf16[1040,128]{1,0:T(8,128)(2,1)S(1)} %copy-done.7), channel_id=1, source_target_pairs={{0,8},{2,10},{4,12},{6,14},{8,0},{10,2},{12,4},{14,6},{1,9},{3,11}... | collective-permute-start | bytes 798728 | tf_op jit(solution)/shard_map/ppermute | solution.py:548
  20.4 39.5 %collective-permute-start.2 = (bf16[1040,128]{1,0:T(8,128)(2,1)S(1)}, bf16[1040,128]{1,0:T(8,128)(2,1)S(1)}, u32[]{:S(2)}, u32[]{:S(2)}) collective-permute-start(bf16[1040,128]{1,0:T(8,128)(2,1)S(1)} %copy-done.6), channel_id=1, source_target_pairs={{0,10},{2,8},{4,14},{6,12},{8,2},{10,0},{12,6},{14,4},{1,11},{3,9}... | collective-permute-start | bytes 798728 | tf_op jit(solution)/shard_map/ppermute | solution.py:548
  67.0 9.2 %collective-permute-start.8 = (f32[256,128]{1,0:T(8,128)S(1)}, f32[256,128]{1,0:T(8,128)S(1)}, u32[]{:S(2)}, u32[]{:S(2)}) collective-permute-start(f32[256,128]{1,0:T(8,128)S(1)} %get-tuple-element.46), channel_id=1, source_target_pairs={{0,2},{1,3},{2,0},{3,1},{4,6},{5,7},{6,4},{7,5},{8,10},{9,11},{10,... | collective-permute-start | bytes 393224 | tf_op jit(solution)/shard_map/ppermute | solution.py:523
  72.9 5.8 %collective-permute-start.9 = (f32[256,128]{1,0:T(8,128)S(1)}, f32[256,128]{1,0:T(8,128)S(1)}, u32[]{:S(2)}, u32[]{:S(2)}) collective-permute-start(f32[256,128]{1,0:T(8,128)S(1)} %get-tuple-element.47), channel_id=1, source_target_pairs={{0,3},{1,2},{2,1},{3,0},{4,7},{5,6},{6,5},{7,4},{8,11},{9,10},{10,... | collective-permute-start | bytes 393224 | tf_op jit(solution)/shard_map/ppermute | solution.py:523
  72.9 5.8 %collective-permute-start.7 = (f32[256,128]{1,0:T(8,128)S(1)}, f32[256,128]{1,0:T(8,128)S(1)}, u32[]{:S(2)}, u32[]{:S(2)}) collective-permute-start(f32[256,128]{1,0:T(8,128)S(1)} %get-tuple-element.45), channel_id=1, source_target_pairs={{0,1},{1,0},{2,3},{3,2},{4,5},{5,4},{6,7},{7,6},{8,9},{9,8},{10,11... | collective-permute-start | bytes 393224 | tf_op jit(solution)/shard_map/ppermute | solution.py:523
  78.7 16.7 %collective-permute-start.13 = (f32[2,512,512]{2,1,0:T(8,128)S(1)}, f32[2,512,512]{2,1,0:T(8,128)S(1)}, u32[]{:S(2)}, u32[]{:S(2)}) collective-permute-start(f32[2,512,512]{2,1,0:T(8,128)S(1)} %give_half.1), channel_id=1, source_target_pairs={{0,1},{1,0},{2,3},{3,2},{4,5},{5,4},{6,7},{7,6},{8,9},{9,8},{10,11... | collective-permute-start | bytes 6291464 | tf_op jit(solution)/shard_map/ppermute | solution.py:559
  78.7 11.6 %collective-permute-start.11 = (f32[256,128]{1,0:T(8,128)S(1)}, f32[256,128]{1,0:T(8,128)S(1)}, u32[]{:S(2)}, u32[]{:S(2)}) collective-permute-start(f32[256,128]{1,0:T(8,128)S(1)} %add_add_fusion.1), channel_id=1, source_target_pairs={{0,8},{1,9},{2,10},{3,11},{4,12},{5,13},{6,14},{7,15},{8,0},{9,1},... | collective-permute-start | bytes 393224 | tf_op jit(solution)/shard_map/ppermute | solution.py:523
  86.0 8.2 %collective-permute-start.12 = (f32[256,128]{1,0:T(8,128)S(1)}, f32[256,128]{1,0:T(8,128)S(1)}, u32[]{:S(2)}, u32[]{:S(2)}) collective-permute-start(f32[256,128]{1,0:T(8,128)S(1)} %add_add_fusion.1), channel_id=1, source_target_pairs={{0,12},{1,13},{2,14},{3,15},{4,8},{5,9},{6,10},{7,11},{8,4},{9,5},... | collective-permute-start | bytes 393224 | tf_op jit(solution)/shard_map/ppermute | solution.py:523
  86.0 9.4 %collective-permute-start.10 = (f32[256,128]{1,0:T(8,128)S(1)}, f32[256,128]{1,0:T(8,128)S(1)}, u32[]{:S(2)}, u32[]{:S(2)}) collective-permute-start(f32[256,128]{1,0:T(8,128)S(1)} %add_add_fusion.1), channel_id=1, source_target_pairs={{0,4},{1,5},{2,6},{3,7},{4,0},{5,1},{6,2},{7,3},{8,12},{9,13},{10,... | collective-permute-start | bytes 393224 | tf_op jit(solution)/shard_map/ppermute | solution.py:523
  97.2 5.7 %collective-permute-start.14 = (f32[256,128]{1,0:T(8,128)S(1)}, f32[256,128]{1,0:T(8,128)S(1)}, u32[]{:S(2)}, u32[]{:S(2)}) collective-permute-start(f32[256,128]{1,0:T(8,128)S(1)} %add_add_fusion), channel_id=1, source_target_pairs={{0,3},{1,2},{2,1},{3,0},{4,7},{5,6},{6,5},{7,4},{8,11},{9,10},{10,... | collective-permute-start | bytes 393224 | tf_op jit(solution)/shard_map/ppermute | solution.py:523
  97.9 7.9 %collective-permute-start.15 = (f32[256,128]{1,0:T(8,128)S(1)}, f32[256,128]{1,0:T(8,128)S(1)}, u32[]{:S(2)}, u32[]{:S(2)}) collective-permute-start(f32[256,128]{1,0:T(8,128)S(1)} %add_add_fusion), channel_id=1, source_target_pairs={{0,2},{1,3},{2,0},{3,1},{4,6},{5,7},{6,4},{7,5},{8,10},{9,11},{10,... | collective-permute-start | bytes 393224 | tf_op jit(solution)/shard_map/ppermute | solution.py:523
  98.7 7.1 %collective-permute-start.16 = (f32[256,128]{1,0:T(8,128)S(1)}, f32[256,128]{1,0:T(8,128)S(1)}, u32[]{:S(2)}, u32[]{:S(2)}) collective-permute-start(f32[256,128]{1,0:T(8,128)S(1)} %add_add_fusion), channel_id=1, source_target_pairs={{0,1},{1,0},{2,3},{3,2},{4,5},{5,4},{6,7},{7,6},{8,9},{9,8},{10,11... | collective-permute-start | bytes 393224 | tf_op jit(solution)/shard_map/ppermute | solution.py:523

commit v4 on v3

--- a/solution.py
+++ b/solution.py
@@ -58,27 +58,20 @@
     line = lax.broadcasted_iota(jnp.int32, (HEAD, LANES), 0)
     for hop in range(tile_count):
         count = count_ref[hop]
-        head = jnp.where(line == 4, count, 0)
+        corner = jnp.zeros((HEAD, LANES), jnp.int32)
         for rank in range(capacity):
             valid = rank < count
             index = jnp.where(valid, source_ref[hop * capacity + rank], 0)
-            row, col = row_ref[index], col_ref[index]
+            value = jnp.where(line < 2, row_ref[index], col_ref[index])
+            corner = jnp.where((lane == rank) & valid, value, corner)
 
             @pl.when(valid)
             def _(hop=hop, rank=rank, index=index):
                 blocks[hop][rank * length : (rank + 1) * length, :] = pat_ref[index]
 
-            digits = jnp.where(
-                line == 0,
-                row // DIGIT,
-                jnp.where(
-                    line == 1,
-                    row % DIGIT,
-                    jnp.where(line == 2, col // DIGIT, jnp.where(line == 3, col % DIGIT, 0)),
-                ),
-            )
-            head = head + jnp.where((lane == rank) & valid, digits, 0)
-        blocks[hop][capacity * length :, :] = head.astype(jnp.float32).astype(jnp.bfloat16)
+        digits = jnp.where(line % 2 == 0, corner // DIGIT, corner % DIGIT)
+        digits = jnp.where(line < 4, digits, jnp.where(line == 4, count, 0))
+        blocks[hop][capacity * length :, :] = digits.astype(jnp.float32).astype(jnp.bfloat16)
 
 
 def pack(patterns, tile_ids, rows, cols, tile_count, capacity):
@@ -380,7 +373,11 @@
         patch[1][1] = jnp.zeros(patch[1].shape[1:], jnp.float32)
         run(exit_chunks(jnp.int32(0), 0))
         run(column_chunks(0, 0, 0), exit_chunks(jnp.int32(1), 1))
-        lax.fori_loop(0, number // 2 + 1, visit, 0)
+        lax.fori_loop(0, (number + 1) // 2, visit, 0)
+
+        @pl.when(number % 2 == 0)
+        def _():
+            run(step_chunks(number - 1, 1))
 
     if not last:
         return
@@ -557,11 +554,9 @@
     part = tree_sum([grads[0]] + [from_peer(grads[turn], turn, devices) for turn in inside])
     send, part = lax.optimization_barrier((halves(total), part))
     object_step = halves(total, lax.ppermute(send, "pos", [(0, 1), (1, 0)]))
-    part = tree_sum(
-        [part]
-        + [from_peer(part, turn, devices) for turn in across]
-    )
-    part, object_step = lax.optimization_barrier((part, object_step))
+    received = [from_peer(part, turn, devices) for turn in across]
+    object_step, *received = lax.optimization_barrier([object_step] + received)
+    part = tree_sum([part] + received)
     square = [part] + [from_peer(part, turn, devices) for turn in inside]
     me = lax.axis_index(("tile", "pos"))
     for bit in (1, 2):

time: 105 us -> 105 us (level); the launches traced: 107 us -> 104 us
  Pallas kernels: 29.2 us -> 25.7 us
    pallas_call x3, Pallas kernels: 22.1 us -> 19.2 us  [step(): pl.pallas_call(functools.partial(step_kernel, count, capacity, scale, not...]
    ppermute x9, waiting for transfers between devices: 20.8 us -> 18.3 us  [from_peer(): return lax.ppermute(array, ('tile', 'pos'), pairs)]
    ppermute x7, waiting for transfers between devices: 22.5 us -> 24.7 us  [on_device(): lax.ppermute(block, 'tile', [(i, i ^ hop) for i in range(tile_count)])]
where the time goes in v4:
time: 105 us; the launch traced here: 104 us
  waiting for transfers between devices  42.9 us (41%)
  starting transfers between devices  29.1 us (28%)
  Pallas kernels  25.7 us (24%)
  local copies, waits for them, and re-layouts  4.34 us (4%)
    ppermute x7, waiting for transfers between devices, on_device(): lax.ppermute(block, 'tile', [(i, i ^ hop) for i in range(tile_count)])  24.7 us
    pallas_call x3, Pallas kernels, step(): pl.pallas_call(functools.partial(step_kernel, count, capacity, scale, not...  19.2 us
    ppermute x9, waiting for transfers between devices, from_peer(): return lax.ppermute(array, ('tile', 'pos'), pairs)  18.3 us
    ppermute x9, starting transfers between devices, from_peer(): return lax.ppermute(array, ('tile', 'pos'), pairs)  15.7 us
    ppermute x7, starting transfers between devices, on_device(): lax.ppermute(block, 'tile', [(i, i ^ hop) for i in range(tile_count)])  12.4 us
    unnamed x16, local copies, waits for them, and re-layouts  4.34 us
    pallas_call x1, Pallas kernels, pack(): pl.pallas_call(functools.partial(pack_kernel, tile_count, capacity), out_...  3.64 us
  transfers between devices with their start and end apart: 17, of which 11 were waited for; matrix products, arithmetic and copies ran while one was open for 0% of the time, Pallas kernels for 15%

profile of v4, /device:TPU:0, one launch (start us, length us, event | category | flops | bytes accessed | tf_op | source)
XLA Modules:
  0.0 103.7 jit_solution(13107954450294157750)
XLA Ops:
  0.7 3.6 %pack_patterns.1 = (bf16[1040,128]{1,0:T(8,128)(2,1)}, bf16[1040,128]{1,0:T(8,128)(2,1)}, bf16[1040,128]{1,0:T(8,128)(2,1)}, bf16[1040,128]{1,0:T(8,128)(2,1)}, ...) custom-call(s32[32]{0:T(128)} %bitcast.3, ...), custom_call_target="tpu_custom_call" | custom-call | tf_op jit(solution)/shard_map/pack_patterns/pallas_call | solution.py:82
  4.3 3.0 %collective-permute-start = (bf16[1040,128]{1,0:T(8,128)(2,1)}, bf16[1040,128]{1,0:T(8,128)(2,1)S(1)}, u32[]{:S(2)}, u32[]{:S(2)}) collective-permute-start(bf16[1040,128]{1,0:T(8,128)(2,1)} %get-tuple-element.32), channel_id=1, source_target_pairs={{0,2},{2,0},{4,6},{6,4},{8,10},{10,8},{12,14},{14,12},{1,3},{3,1},... | collective-permute-start | bytes 798728 | tf_op jit(solution)/shard_map/ppermute | solution.py:545
  7.3 1.6 %collective-permute-start.5 = (bf16[1040,128]{1,0:T(8,128)(2,1)}, bf16[1040,128]{1,0:T(8,128)(2,1)S(1)}, u32[]{:S(2)}, u32[]{:S(2)}) collective-permute-start(bf16[1040,128]{1,0:T(8,128)(2,1)} %get-tuple-element.39), channel_id=1, source_target_pairs={{0,4},{2,6},{4,0},{6,2},{8,12},{10,14},{12,8},{14,10},{1,5},{3,7},... | collective-permute-start | bytes 798728 | tf_op jit(solution)/shard_map/ppermute | solution.py:545
  8.8 4.0 %collective-permute-start.3 = (bf16[1040,128]{1,0:T(8,128)(2,1)}, bf16[1040,128]{1,0:T(8,128)(2,1)S(1)}, u32[]{:S(2)}, u32[]{:S(2)}) collective-permute-start(bf16[1040,128]{1,0:T(8,128)(2,1)} %get-tuple-element.36), channel_id=1, source_target_pairs={{0,12},{2,14},{4,8},{6,10},{8,4},{10,6},{12,0},{14,2},{1,13},{3,15... | collective-permute-start | bytes 798728 | tf_op jit(solution)/shard_map/ppermute | solution.py:545
  12.8 1.2 %collective-permute-start.4 = (bf16[1040,128]{1,0:T(8,128)(2,1)}, bf16[1040,128]{1,0:T(8,128)(2,1)S(1)}, u32[]{:S(2)}, u32[]{:S(2)}) collective-permute-start(bf16[1040,128]{1,0:T(8,128)(2,1)} %get-tuple-element.37), channel_id=1, source_target_pairs={{0,14},{2,12},{4,10},{6,8},{8,6},{10,4},{12,2},{14,0},{1,15},{3,13... | collective-permute-start | bytes 798728 | tf_op jit(solution)/shard_map/ppermute | solution.py:545
  14.0 2.2 %copy-done = f32[2,512,1024]{2,1,0:T(8,128)S(1)} copy-done((f32[2,512,1024]{2,1,0:T(8,128)S(1)}, f32[2,512,1024]{2,1,0:T(8,128)}, u32[]{:S(2)}) %copy-start) | copy-done | bytes 4194328
  16.2 1.0 %copy-done.1 = f32[4,2,128,128]{3,2,1,0:T(8,128)S(1)} copy-done((f32[4,2,128,128]{3,2,1,0:T(8,128)S(1)}, f32[4,2,128,128]{3,2,1,0:T(8,128)}, u32[]{:S(2)}) %copy-start.1) | copy-done | bytes 524312
  17.2 0.9 copy-done.2
  19.1 0.8 collective-permute-start.1
  19.9 1.9 %collective-permute-start.2 = (bf16[1040,128]{1,0:T(8,128)(2,1)S(1)}, bf16[1040,128]{1,0:T(8,128)(2,1)S(1)}, u32[]{:S(2)}, u32[]{:S(2)}) collective-permute-start(bf16[1040,128]{1,0:T(8,128)(2,1)S(1)} %copy-done.6), channel_id=1, source_target_pairs={{0,10},{2,8},{4,14},{6,12},{8,2},{10,0},{12,6},{14,4},{1,11},{3,9}... | collective-permute-start | bytes 798728 | tf_op jit(solution)/shard_map/ppermute | solution.py:545
  21.8 1.1 %collective-permute-done.6.rest_3_ = bf16[1040,128]{1,0:T(8,128)(2,1)S(1)} collective-permute-done((bf16[1040,128]{1,0:T(8,128)(2,1)}, bf16[1040,128]{1,0:T(8,128)(2,1)S(1)}, u32[]{:S(2)}, u32[]{:S(2)}) %collective-permute-start.6) | collective-permute-done | bytes 266272 | tf_op jit(solution)/shard_map/ppermute | solution.py:545
  22.9 7.5 %gradient_step.3 = (f32[2,9,520,128]{3,2,1,0:T(8,128)S(1)}, f32[1024,128]{1,0:T(8,128)S(1)}) custom-call(f32[2,9,520,128]{3,2,1,0:T(8,128)S(1)} %get-tuple-element.29.field, f32[4,2,128,128]{3,2,1,0:T(8,128)S(1)} %get-tuple-element.30.lit, bf16[2,256,256]{2,1,0:T(8,128)(2,1)S(1)} %copy-done.5, f32[2,128,128]{2,1,0:T(8,128)S(1)} %copy-done.3, ...), custom_call_target="tpu_custom_call" | custom-call | flops 8589934592 | bytes 16777216 | tf_op jit(solution)/shard_map/gradient_step/pallas_call | solution.py:426
  30.5 1.1 %collective-permute-done.3.rest_0_ = bf16[1040,128]{1,0:T(8,128)(2,1)S(1)} collective-permute-done((bf16[1040,128]{1,0:T(8,128)(2,1)}, bf16[1040,128]{1,0:T(8,128)(2,1)S(1)}, u32[]{:S(2)}, u32[]{:S(2)}) %collective-permute-start.3) | collective-permute-done | bytes 266272 | tf_op jit(solution)/shard_map/ppermute | solution.py:545
  31.6 5.5 %collective-permute-done.4.rest_1_ = bf16[1040,128]{1,0:T(8,128)(2,1)S(1)} collective-permute-done((bf16[1040,128]{1,0:T(8,128)(2,1)}, bf16[1040,128]{1,0:T(8,128)(2,1)S(1)}, u32[]{:S(2)}, u32[]{:S(2)}) %collective-permute-start.4) | collective-permute-done | bytes 266272 | tf_op jit(solution)/shard_map/ppermute | solution.py:545
  37.1 5.4 %gradient_step.4 = (f32[2,9,520,128]{3,2,1,0:T(8,128)S(1)}, f32[1024,128]{1,0:T(8,128)S(1)}) custom-call(f32[2,9,520,128]{3,2,1,0:T(8,128)S(1)} %get-tuple-element.29.field, f32[4,2,128,128]{3,2,1,0:T(8,128)S(1)} %get-tuple-element.30.lit, bf16[2,256,256]{2,1,0:T(8,128)(2,1)S(1)} %copy-done.5, f32[2,128,128]{2,1,0:T(8,128)S(1)} %copy-done.3, ...), custom_call_target="tpu_custom_call" | custom-call | flops 4294967296 | bytes 16777216 | tf_op jit(solution)/shard_map/gradient_step/pallas_call | solution.py:426
  42.5 12.7 %collective-permute-done.1.rest_0_ = bf16[1040,128]{1,0:T(8,128)(2,1)S(1)} collective-permute-done((bf16[1040,128]{1,0:T(8,128)(2,1)S(1)}, bf16[1040,128]{1,0:T(8,128)(2,1)S(1)}, u32[]{:S(2)}, u32[]{:S(2)}) %collective-permute-start.1) | collective-permute-done | bytes 266272 | tf_op jit(solution)/shard_map/ppermute | solution.py:545
  55.2 4.2 %collective-permute-done.2.rest_1_ = bf16[1040,128]{1,0:T(8,128)(2,1)S(1)} collective-permute-done((bf16[1040,128]{1,0:T(8,128)(2,1)S(1)}, bf16[1040,128]{1,0:T(8,128)(2,1)S(1)}, u32[]{:S(2)}, u32[]{:S(2)}) %collective-permute-start.2) | collective-permute-done | bytes 266272 | tf_op jit(solution)/shard_map/ppermute | solution.py:545
  59.4 6.3 %gradient_step.5 = (f32[2,9,520,128]{3,2,1,0:T(8,128)S(1)}, f32[1024,128]{1,0:T(8,128)}, f32[256,128]{1,0:T(8,128)S(1)}, f32[256,128]{1,0:T(8,128)S(1)}, f32[256,128]{1,0:T(8,128)S(1)}, /*index=5*/f32[256,128]{1,0:T(8,128)S(1)}) custom-call(f32[2,9,520,128]{3,2,1,0:T(8,128)S(1)} %get-tuple-element.29.field, f32[4,2,128,128]{3,2,1,0:T(8,128)S(1)} %get-tuple-element.30.lit, ...), custom_call_target="tpu_custom_call" | custom-call | flops 4294967296 | bytes 16777216 | tf_op jit(solution)/shard_map/gradient_step/pallas_call | solution.py:426
  65.7 1.0 collective-permute-start.8
  66.7 1.2 %collective-permute-start.7 = (f32[256,128]{1,0:T(8,128)S(1)}, f32[256,128]{1,0:T(8,128)S(1)}, u32[]{:S(2)}, u32[]{:S(2)}) collective-permute-start(f32[256,128]{1,0:T(8,128)S(1)} %get-tuple-element.47), channel_id=1, source_target_pairs={{0,1},{1,0},{2,3},{3,2},{4,5},{5,4},{6,7},{7,6},{8,9},{9,8},{10,11... | collective-permute-start | bytes 393224 | tf_op jit(solution)/shard_map/ppermute | solution.py:520
  68.3 3.5 %collective-permute-done.8 = f32[256,128]{1,0:T(8,128)S(1)} collective-permute-done((f32[256,128]{1,0:T(8,128)S(1)}, f32[256,128]{1,0:T(8,128)S(1)}, u32[]{:S(2)}, u32[]{:S(2)}) %collective-permute-start.8) | collective-permute-done | bytes 131104 | tf_op jit(solution)/shard_map/ppermute | solution.py:520
  72.5 0.9 collective-permute-start.10
  73.5 1.1 %collective-permute-start.11 = (f32[256,128]{1,0:T(8,128)S(1)}, f32[256,128]{1,0:T(8,128)S(1)}, u32[]{:S(2)}, u32[]{:S(2)}) collective-permute-start(f32[256,128]{1,0:T(8,128)S(1)} %add_add_fusion.1), channel_id=1, source_target_pairs={{0,4},{1,5},{2,6},{3,7},{4,0},{5,1},{6,2},{7,3},{8,12},{9,13},{10,... | collective-permute-start | bytes 393224 | tf_op jit(solution)/shard_map/ppermute | solution.py:520
  74.6 9.1 %collective-permute-start.12 = (f32[256,128]{1,0:T(8,128)S(1)}, f32[256,128]{1,0:T(8,128)S(1)}, u32[]{:S(2)}, u32[]{:S(2)}) collective-permute-start(f32[256,128]{1,0:T(8,128)S(1)} %add_add_fusion.1), channel_id=1, source_target_pairs={{0,8},{1,9},{2,10},{3,11},{4,12},{5,13},{6,14},{7,15},{8,0},{9,1},... | collective-permute-start | bytes 393224 | tf_op jit(solution)/shard_map/ppermute | solution.py:520
  83.7 1.4 %collective-permute-start.13 = (f32[256,128]{1,0:T(8,128)S(1)}, f32[256,128]{1,0:T(8,128)S(1)}, u32[]{:S(2)}, u32[]{:S(2)}) collective-permute-start(f32[256,128]{1,0:T(8,128)S(1)} %add_add_fusion.1), channel_id=1, source_target_pairs={{0,12},{1,13},{2,14},{3,15},{4,8},{5,9},{6,10},{7,11},{8,4},{9,5},... | collective-permute-start | bytes 393224 | tf_op jit(solution)/shard_map/ppermute | solution.py:520
  85.1 1.8 %add_half.1 = f32[2,512,512]{2,1,0:T(8,128)} custom-call(f32[2,9,520,128]{3,2,1,0:T(8,128)S(1)} %get-tuple-element.45.total, f32[2,512,512]{2,1,0:T(8,128)S(1)} %collective-permute-done.10.received), custom_call_target="tpu_custom_call" | custom-call | flops 1048576 | bytes 4194304 | tf_op jit(solution)/shard_map/add_half/pallas_call | solution.py:507
  86.8 0.9 collective-permute-done.12
  87.8 6.8 %collective-permute-done.13 = f32[256,128]{1,0:T(8,128)S(1)} collective-permute-done((f32[256,128]{1,0:T(8,128)S(1)}, f32[256,128]{1,0:T(8,128)S(1)}, u32[]{:S(2)}, u32[]{:S(2)}) %collective-permute-start.13) | collective-permute-done | bytes 131104 | tf_op jit(solution)/shard_map/ppermute | solution.py:520
  94.7 1.2 %collective-permute-start.15 = (f32[256,128]{1,0:T(8,128)S(1)}, f32[256,128]{1,0:T(8,128)S(1)}, u32[]{:S(2)}, u32[]{:S(2)}) collective-permute-start(f32[256,128]{1,0:T(8,128)S(1)} %add_add_fusion), channel_id=1, source_target_pairs={{0,2},{1,3},{2,0},{3,1},{4,6},{5,7},{6,4},{7,5},{8,10},{9,11},{10,... | collective-permute-start | bytes 393224 | tf_op jit(solution)/shard_map/ppermute | solution.py:520
  96.6 3.9 %collective-permute-done.14 = f32[256,128]{1,0:T(8,128)S(1)} collective-permute-done((f32[256,128]{1,0:T(8,128)S(1)}, f32[256,128]{1,0:T(8,128)S(1)}, u32[]{:S(2)}, u32[]{:S(2)}) %collective-permute-start.14) | collective-permute-done | bytes 131104 | tf_op jit(solution)/shard_map/ppermute | solution.py:520
  100.5 2.4 %collective-permute-done.15 = f32[256,128]{1,0:T(8,128)S(1)} collective-permute-done((f32[256,128]{1,0:T(8,128)S(1)}, f32[256,128]{1,0:T(8,128)S(1)}, u32[]{:S(2)}, u32[]{:S(2)}) %collective-permute-start.15) | collective-permute-done | bytes 131104 | tf_op jit(solution)/shard_map/ppermute | solution.py:520
  102.9 0.8 pad_maximum_fusion
  (29 shorter events, 2.8 us)
Async XLA Ops:
  0.6 22.3 %copy-start.3 = (f32[2,128,128]{2,1,0:T(8,128)S(1)}, f32[2,128,128]{2,1,0:T(8,128)}, u32[]{:S(2)}) copy-start(f32[2,128,128]{2,1,0:T(8,128)} %constant.19.clone.chirp_ref) | copy-start | bytes 393220
  0.6 22.3 %copy-start.5 = (bf16[2,256,256]{2,1,0:T(8,128)(2,1)S(1)}, bf16[2,256,256]{2,1,0:T(8,128)(2,1)}, u32[]{:S(2)}) copy-start(bf16[2,256,256]{2,1,0:T(8,128)(2,1)} %constant.18.clone.dft_ref) | copy-start | bytes 786436
  4.3 14.6 %collective-permute-start = (bf16[1040,128]{1,0:T(8,128)(2,1)}, bf16[1040,128]{1,0:T(8,128)(2,1)S(1)}, u32[]{:S(2)}, u32[]{:S(2)}) collective-permute-start(bf16[1040,128]{1,0:T(8,128)(2,1)} %get-tuple-element.32), channel_id=1, source_target_pairs={{0,2},{2,0},{4,6},{6,4},{8,10},{10,8},{12,14},{14,12},{1,3},{3,1},... | collective-permute-start | bytes 798728 | tf_op jit(solution)/shard_map/ppermute | solution.py:545
  7.3 12.6 %collective-permute-start.5 = (bf16[1040,128]{1,0:T(8,128)(2,1)}, bf16[1040,128]{1,0:T(8,128)(2,1)S(1)}, u32[]{:S(2)}, u32[]{:S(2)}) collective-permute-start(bf16[1040,128]{1,0:T(8,128)(2,1)} %get-tuple-element.39), channel_id=1, source_target_pairs={{0,4},{2,6},{4,0},{6,2},{8,12},{10,14},{12,8},{14,10},{1,5},{3,7},... | collective-permute-start | bytes 798728 | tf_op jit(solution)/shard_map/ppermute | solution.py:545
  8.8 14.1 %collective-permute-start.6 = (bf16[1040,128]{1,0:T(8,128)(2,1)}, bf16[1040,128]{1,0:T(8,128)(2,1)S(1)}, u32[]{:S(2)}, u32[]{:S(2)}) collective-permute-start(bf16[1040,128]{1,0:T(8,128)(2,1)} %get-tuple-element.40), channel_id=1, source_target_pairs={{0,6},{2,4},{4,2},{6,0},{8,14},{10,12},{12,10},{14,8},{1,7},{3,5},... | collective-permute-start | bytes 798728 | tf_op jit(solution)/shard_map/ppermute | solution.py:545
  8.8 22.7 %collective-permute-start.3 = (bf16[1040,128]{1,0:T(8,128)(2,1)}, bf16[1040,128]{1,0:T(8,128)(2,1)S(1)}, u32[]{:S(2)}, u32[]{:S(2)}) collective-permute-start(bf16[1040,128]{1,0:T(8,128)(2,1)} %get-tuple-element.36), channel_id=1, source_target_pairs={{0,12},{2,14},{4,8},{6,10},{8,4},{10,6},{12,0},{14,2},{1,13},{3,15... | collective-permute-start | bytes 798728 | tf_op jit(solution)/shard_map/ppermute | solution.py:545
  12.8 24.3 %collective-permute-start.4 = (bf16[1040,128]{1,0:T(8,128)(2,1)}, bf16[1040,128]{1,0:T(8,128)(2,1)S(1)}, u32[]{:S(2)}, u32[]{:S(2)}) collective-permute-start(bf16[1040,128]{1,0:T(8,128)(2,1)} %get-tuple-element.37), channel_id=1, source_target_pairs={{0,14},{2,12},{4,10},{6,8},{8,6},{10,4},{12,2},{14,0},{1,15},{3,13... | collective-permute-start | bytes 798728 | tf_op jit(solution)/shard_map/ppermute | solution.py:545
  14.0 2.2 %copy-start = (f32[2,512,1024]{2,1,0:T(8,128)S(1)}, f32[2,512,1024]{2,1,0:T(8,128)}, u32[]{:S(2)}) copy-start(f32[2,512,1024]{2,1,0:T(8,128)} %object_hbm.1) | copy-start | bytes 12582916
  16.2 1.0 %copy-start.1 = (f32[4,2,128,128]{3,2,1,0:T(8,128)S(1)}, f32[4,2,128,128]{3,2,1,0:T(8,128)}, u32[]{:S(2)}) copy-start(f32[4,2,128,128]{3,2,1,0:T(8,128)} %probe_ref.1) | copy-start | bytes 1572868
  17.2 0.9 copy-start.2
  18.2 1.0 copy-start.7
  18.2 1.7 %copy-start.6 = (bf16[1040,128]{1,0:T(8,128)(2,1)S(1)}, bf16[1040,128]{1,0:T(8,128)(2,1)}, u32[]{:S(2)}) copy-start(bf16[1040,128]{1,0:T(8,128)(2,1)} %get-tuple-element.35) | copy-start | bytes 798724
  18.2 4.8 %copy-start.4 = (bf16[1040,128]{1,0:T(8,128)(2,1)S(1)}, bf16[1040,128]{1,0:T(8,128)(2,1)}, u32[]{:S(2)}) copy-start(bf16[1040,128]{1,0:T(8,128)(2,1)} %get-tuple-element.38.rest_0_) | copy-start | bytes 798724
  19.1 36.1 %collective-permute-start.1 = (bf16[1040,128]{1,0:T(8,128)(2,1)S(1)}, bf16[1040,128]{1,0:T(8,128)(2,1)S(1)}, u32[]{:S(2)}, u32[]{:S(2)}) collective-permute-start(bf16[1040,128]{1,0:T(8,128)(2,1)S(1)} %copy-done.7), channel_id=1, source_target_pairs={{0,8},{2,10},{4,12},{6,14},{8,0},{10,2},{12,4},{14,6},{1,9},{3,11}... | collective-permute-start | bytes 798728 | tf_op jit(solution)/shard_map/ppermute | solution.py:545
  19.9 39.5 %collective-permute-start.2 = (bf16[1040,128]{1,0:T(8,128)(2,1)S(1)}, bf16[1040,128]{1,0:T(8,128)(2,1)S(1)}, u32[]{:S(2)}, u32[]{:S(2)}) collective-permute-start(bf16[1040,128]{1,0:T(8,128)(2,1)S(1)} %copy-done.6), channel_id=1, source_target_pairs={{0,10},{2,8},{4,14},{6,12},{8,2},{10,0},{12,6},{14,4},{1,11},{3,9}... | collective-permute-start | bytes 798728 | tf_op jit(solution)/shard_map/ppermute | solution.py:545
  65.7 6.1 %collective-permute-start.8 = (f32[256,128]{1,0:T(8,128)S(1)}, f32[256,128]{1,0:T(8,128)S(1)}, u32[]{:S(2)}, u32[]{:S(2)}) collective-permute-start(f32[256,128]{1,0:T(8,128)S(1)} %get-tuple-element.48), channel_id=1, source_target_pairs={{0,2},{1,3},{2,0},{3,1},{4,6},{5,7},{6,4},{7,5},{8,10},{9,11},{10,... | collective-permute-start | bytes 393224 | tf_op jit(solution)/shard_map/ppermute | solution.py:520
  66.7 5.8 %collective-permute-start.9 = (f32[256,128]{1,0:T(8,128)S(1)}, f32[256,128]{1,0:T(8,128)S(1)}, u32[]{:S(2)}, u32[]{:S(2)}) collective-permute-start(f32[256,128]{1,0:T(8,128)S(1)} %get-tuple-element.49), channel_id=1, source_target_pairs={{0,3},{1,2},{2,1},{3,0},{4,7},{5,6},{6,5},{7,4},{8,11},{9,10},{10,... | collective-permute-start | bytes 393224 | tf_op jit(solution)/shard_map/ppermute | solution.py:520
  66.7 5.8 %collective-permute-start.7 = (f32[256,128]{1,0:T(8,128)S(1)}, f32[256,128]{1,0:T(8,128)S(1)}, u32[]{:S(2)}, u32[]{:S(2)}) collective-permute-start(f32[256,128]{1,0:T(8,128)S(1)} %get-tuple-element.47), channel_id=1, source_target_pairs={{0,1},{1,0},{2,3},{3,2},{4,5},{5,4},{6,7},{7,6},{8,9},{9,8},{10,11... | collective-permute-start | bytes 393224 | tf_op jit(solution)/shard_map/ppermute | solution.py:520
  72.5 12.5 %collective-permute-start.10 = (f32[2,512,512]{2,1,0:T(8,128)S(1)}, f32[2,512,512]{2,1,0:T(8,128)S(1)}, u32[]{:S(2)}, u32[]{:S(2)}) collective-permute-start(f32[2,512,512]{2,1,0:T(8,128)S(1)} %give_half.1), channel_id=1, source_target_pairs={{0,1},{1,0},{2,3},{3,2},{4,5},{5,4},{6,7},{7,6},{8,9},{9,8},{10,11... | collective-permute-start | bytes 6291464 | tf_op jit(solution)/shard_map/ppermute | solution.py:556
  73.5 13.4 %collective-permute-start.11 = (f32[256,128]{1,0:T(8,128)S(1)}, f32[256,128]{1,0:T(8,128)S(1)}, u32[]{:S(2)}, u32[]{:S(2)}) collective-permute-start(f32[256,128]{1,0:T(8,128)S(1)} %add_add_fusion.1), channel_id=1, source_target_pairs={{0,4},{1,5},{2,6},{3,7},{4,0},{5,1},{6,2},{7,3},{8,12},{9,13},{10,... | collective-permute-start | bytes 393224 | tf_op jit(solution)/shard_map/ppermute | solution.py:520
  74.6 13.2 %collective-permute-start.12 = (f32[256,128]{1,0:T(8,128)S(1)}, f32[256,128]{1,0:T(8,128)S(1)}, u32[]{:S(2)}, u32[]{:S(2)}) collective-permute-start(f32[256,128]{1,0:T(8,128)S(1)} %add_add_fusion.1), channel_id=1, source_target_pairs={{0,8},{1,9},{2,10},{3,11},{4,12},{5,13},{6,14},{7,15},{8,0},{9,1},... | collective-permute-start | bytes 393224 | tf_op jit(solution)/shard_map/ppermute | solution.py:520
  83.7 10.9 %collective-permute-start.13 = (f32[256,128]{1,0:T(8,128)S(1)}, f32[256,128]{1,0:T(8,128)S(1)}, u32[]{:S(2)}, u32[]{:S(2)}) collective-permute-start(f32[256,128]{1,0:T(8,128)S(1)} %add_add_fusion.1), channel_id=1, source_target_pairs={{0,12},{1,13},{2,14},{3,15},{4,8},{5,9},{6,10},{7,11},{8,4},{9,5},... | collective-permute-start | bytes 393224 | tf_op jit(solution)/shard_map/ppermute | solution.py:520
  94.6 5.9 %collective-permute-start.14 = (f32[256,128]{1,0:T(8,128)S(1)}, f32[256,128]{1,0:T(8,128)S(1)}, u32[]{:S(2)}, u32[]{:S(2)}) collective-permute-start(f32[256,128]{1,0:T(8,128)S(1)} %add_add_fusion), channel_id=1, source_target_pairs={{0,3},{1,2},{2,1},{3,0},{4,7},{5,6},{6,5},{7,4},{8,11},{9,10},{10,... | collective-permute-start | bytes 393224 | tf_op jit(solution)/shard_map/ppermute | solution.py:520
  94.7 8.1 %collective-permute-start.15 = (f32[256,128]{1,0:T(8,128)S(1)}, f32[256,128]{1,0:T(8,128)S(1)}, u32[]{:S(2)}, u32[]{:S(2)}) collective-permute-start(f32[256,128]{1,0:T(8,128)S(1)} %add_add_fusion), channel_id=1, source_target_pairs={{0,2},{1,3},{2,0},{3,1},{4,6},{5,7},{6,4},{7,5},{8,10},{9,11},{10,... | collective-permute-start | bytes 393224 | tf_op jit(solution)/shard_map/ppermute | solution.py:520
  95.9 6.9 %collective-permute-start.16 = (f32[256,128]{1,0:T(8,128)S(1)}, f32[256,128]{1,0:T(8,128)S(1)}, u32[]{:S(2)}, u32[]{:S(2)}) collective-permute-start(f32[256,128]{1,0:T(8,128)S(1)} %add_add_fusion), channel_id=1, source_target_pairs={{0,1},{1,0},{2,3},{3,2},{4,5},{5,4},{6,7},{7,6},{8,9},{9,8},{10,11... | collective-permute-start | bytes 393224 | tf_op jit(solution)/shard_map/ppermute | solution.py:520

commit v5 on v4

--- a/solution.py
+++ b/solution.py
@@ -554,9 +554,10 @@
     part = tree_sum([grads[0]] + [from_peer(grads[turn], turn, devices) for turn in inside])
     send, part = lax.optimization_barrier((halves(total), part))
     object_step = halves(total, lax.ppermute(send, "pos", [(0, 1), (1, 0)]))
+    part = part.astype(jnp.bfloat16)
     received = [from_peer(part, turn, devices) for turn in across]
     object_step, *received = lax.optimization_barrier([object_step] + received)
-    part = tree_sum([part] + received)
+    part = tree_sum([piece.astype(jnp.float32) for piece in [part] + received])
     square = [part] + [from_peer(part, turn, devices) for turn in inside]
     me = lax.axis_index(("tile", "pos"))
     for bit in (1, 2):

time: 105 us -> 97.7 us (0.930); the launches traced: 104 us -> 97.6 us
  waiting for transfers between devices: 42.9 us -> 38.1 us
  starting transfers between devices: 29.1 us -> 27.3 us
    ppermute x9, waiting for transfers between devices: 18.3 us -> 13.9 us  [from_peer(): return lax.ppermute(array, ('tile', 'pos'), pairs)]
  transfers between devices with their start and end apart: 17 -> 17, of which waited for: 11 -> 9; matrix products, arithmetic and copies ran while one was open for 0% -> 0% of each run, Pallas kernels for 15% -> 17%
where the time goes in v5:
time: 97.7 us; the launch traced here: 97.6 us
  waiting for transfers between devices  38.1 us (39%)
  starting transfers between devices  27.3 us (28%)
  Pallas kernels  26.1 us (27%)
  local copies, waits for them, and re-layouts  4.34 us (4%)
    ppermute x7, waiting for transfers between devices, on_device(): lax.ppermute(block, 'tile', [(i, i ^ hop) for i in range(tile_count)])  24.2 us
    pallas_call x3, Pallas kernels, step(): pl.pallas_call(functools.partial(step_kernel, count, capacity, scale, not...  19.6 us
    ppermute x9, starting transfers between devices, from_peer(): return lax.ppermute(array, ('tile', 'pos'), pairs)  14.8 us
    ppermute x9, waiting for transfers between devices, from_peer(): return lax.ppermute(array, ('tile', 'pos'), pairs)  13.9 us
    ppermute x7, starting transfers between devices, on_device(): lax.ppermute(block, 'tile', [(i, i ^ hop) for i in range(tile_count)])  12.4 us
    unnamed x16, local copies, waits for them, and re-layouts  4.34 us
    pallas_call x1, Pallas kernels, pack(): pl.pallas_call(functools.partial(pack_kernel, tile_count, capacity), out_...  3.64 us
  transfers between devices with their start and end apart: 17, of which 9 were waited for; matrix products, arithmetic and copies ran while one was open for 0% of the time, Pallas kernels for 17%

profile of v5, /device:TPU:0, one launch (start us, length us, event | category | flops | bytes accessed | tf_op | source)
XLA Modules:
  0.0 97.6 jit_solution(17569343384361811785)
XLA Ops:
  0.7 3.6 %pack_patterns.1 = (bf16[1040,128]{1,0:T(8,128)(2,1)}, bf16[1040,128]{1,0:T(8,128)(2,1)}, bf16[1040,128]{1,0:T(8,128)(2,1)}, bf16[1040,128]{1,0:T(8,128)(2,1)}, ...) custom-call(s32[32]{0:T(128)} %bitcast.3, ...), custom_call_target="tpu_custom_call" | custom-call | tf_op jit(solution)/shard_map/pack_patterns/pallas_call | solution.py:82
  4.3 3.0 %collective-permute-start = (bf16[1040,128]{1,0:T(8,128)(2,1)}, bf16[1040,128]{1,0:T(8,128)(2,1)S(1)}, u32[]{:S(2)}, u32[]{:S(2)}) collective-permute-start(bf16[1040,128]{1,0:T(8,128)(2,1)} %get-tuple-element.32), channel_id=1, source_target_pairs={{0,2},{2,0},{4,6},{6,4},{8,10},{10,8},{12,14},{14,12},{1,3},{3,1},... | collective-permute-start | bytes 798728 | tf_op jit(solution)/shard_map/ppermute | solution.py:545
  7.3 1.6 %collective-permute-start.5 = (bf16[1040,128]{1,0:T(8,128)(2,1)}, bf16[1040,128]{1,0:T(8,128)(2,1)S(1)}, u32[]{:S(2)}, u32[]{:S(2)}) collective-permute-start(bf16[1040,128]{1,0:T(8,128)(2,1)} %get-tuple-element.39), channel_id=1, source_target_pairs={{0,4},{2,6},{4,0},{6,2},{8,12},{10,14},{12,8},{14,10},{1,5},{3,7},... | collective-permute-start | bytes 798728 | tf_op jit(solution)/shard_map/ppermute | solution.py:545
  8.8 4.0 %collective-permute-start.3 = (bf16[1040,128]{1,0:T(8,128)(2,1)}, bf16[1040,128]{1,0:T(8,128)(2,1)S(1)}, u32[]{:S(2)}, u32[]{:S(2)}) collective-permute-start(bf16[1040,128]{1,0:T(8,128)(2,1)} %get-tuple-element.36), channel_id=1, source_target_pairs={{0,12},{2,14},{4,8},{6,10},{8,4},{10,6},{12,0},{14,2},{1,13},{3,15... | collective-permute-start | bytes 798728 | tf_op jit(solution)/shard_map/ppermute | solution.py:545
  12.8 1.2 %collective-permute-start.4 = (bf16[1040,128]{1,0:T(8,128)(2,1)}, bf16[1040,128]{1,0:T(8,128)(2,1)S(1)}, u32[]{:S(2)}, u32[]{:S(2)}) collective-permute-start(bf16[1040,128]{1,0:T(8,128)(2,1)} %get-tuple-element.37), channel_id=1, source_target_pairs={{0,14},{2,12},{4,10},{6,8},{8,6},{10,4},{12,2},{14,0},{1,15},{3,13... | collective-permute-start | bytes 798728 | tf_op jit(solution)/shard_map/ppermute | solution.py:545
  14.0 2.2 %copy-done = f32[2,512,1024]{2,1,0:T(8,128)S(1)} copy-done((f32[2,512,1024]{2,1,0:T(8,128)S(1)}, f32[2,512,1024]{2,1,0:T(8,128)}, u32[]{:S(2)}) %copy-start) | copy-done | bytes 4194328
  16.2 1.0 %copy-done.1 = f32[4,2,128,128]{3,2,1,0:T(8,128)S(1)} copy-done((f32[4,2,128,128]{3,2,1,0:T(8,128)S(1)}, f32[4,2,128,128]{3,2,1,0:T(8,128)}, u32[]{:S(2)}) %copy-start.1) | copy-done | bytes 524312
  17.2 0.9 copy-done.2
  18.2 0.7 prepare_strip.1
  18.9 0.2 copy-done.7
  19.1 0.8 collective-permute-start.1
  19.9 1.9 %collective-permute-start.2 = (bf16[1040,128]{1,0:T(8,128)(2,1)S(1)}, bf16[1040,128]{1,0:T(8,128)(2,1)S(1)}, u32[]{:S(2)}, u32[]{:S(2)}) collective-permute-start(bf16[1040,128]{1,0:T(8,128)(2,1)S(1)} %copy-done.6), channel_id=1, source_target_pairs={{0,10},{2,8},{4,14},{6,12},{8,2},{10,0},{12,6},{14,4},{1,11},{3,9}... | collective-permute-start | bytes 798728 | tf_op jit(solution)/shard_map/ppermute | solution.py:545
  21.8 1.1 %collective-permute-done.6.rest_3_ = bf16[1040,128]{1,0:T(8,128)(2,1)S(1)} collective-permute-done((bf16[1040,128]{1,0:T(8,128)(2,1)}, bf16[1040,128]{1,0:T(8,128)(2,1)S(1)}, u32[]{:S(2)}, u32[]{:S(2)}) %collective-permute-start.6) | collective-permute-done | bytes 266272 | tf_op jit(solution)/shard_map/ppermute | solution.py:545
  22.9 8.8 %gradient_step.3 = (f32[2,9,520,128]{3,2,1,0:T(8,128)S(1)}, f32[1024,128]{1,0:T(8,128)S(1)}) custom-call(f32[2,9,520,128]{3,2,1,0:T(8,128)S(1)} %get-tuple-element.29.field, f32[4,2,128,128]{3,2,1,0:T(8,128)S(1)} %get-tuple-element.30.lit, bf16[2,256,256]{2,1,0:T(8,128)(2,1)S(1)} %copy-done.5, f32[2,128,128]{2,1,0:T(8,128)S(1)} %copy-done.3, ...), custom_call_target="tpu_custom_call" | custom-call | flops 8589934592 | bytes 16777216 | tf_op jit(solution)/shard_map/gradient_step/pallas_call | solution.py:426
  31.8 5.3 %collective-permute-done.4.rest_1_ = bf16[1040,128]{1,0:T(8,128)(2,1)S(1)} collective-permute-done((bf16[1040,128]{1,0:T(8,128)(2,1)}, bf16[1040,128]{1,0:T(8,128)(2,1)S(1)}, u32[]{:S(2)}, u32[]{:S(2)}) %collective-permute-start.4) | collective-permute-done | bytes 266272 | tf_op jit(solution)/shard_map/ppermute | solution.py:545
  37.1 4.6 %gradient_step.4 = (f32[2,9,520,128]{3,2,1,0:T(8,128)S(1)}, f32[1024,128]{1,0:T(8,128)S(1)}) custom-call(f32[2,9,520,128]{3,2,1,0:T(8,128)S(1)} %get-tuple-element.29.field, f32[4,2,128,128]{3,2,1,0:T(8,128)S(1)} %get-tuple-element.30.lit, bf16[2,256,256]{2,1,0:T(8,128)(2,1)S(1)} %copy-done.5, f32[2,128,128]{2,1,0:T(8,128)S(1)} %copy-done.3, ...), custom_call_target="tpu_custom_call" | custom-call | flops 4294967296 | bytes 16777216 | tf_op jit(solution)/shard_map/gradient_step/pallas_call | solution.py:426
  41.7 13.5 %collective-permute-done.1.rest_0_ = bf16[1040,128]{1,0:T(8,128)(2,1)S(1)} collective-permute-done((bf16[1040,128]{1,0:T(8,128)(2,1)S(1)}, bf16[1040,128]{1,0:T(8,128)(2,1)S(1)}, u32[]{:S(2)}, u32[]{:S(2)}) %collective-permute-start.1) | collective-permute-done | bytes 266272 | tf_op jit(solution)/shard_map/ppermute | solution.py:545
  55.2 4.2 %collective-permute-done.2.rest_1_ = bf16[1040,128]{1,0:T(8,128)(2,1)S(1)} collective-permute-done((bf16[1040,128]{1,0:T(8,128)(2,1)S(1)}, bf16[1040,128]{1,0:T(8,128)(2,1)S(1)}, u32[]{:S(2)}, u32[]{:S(2)}) %collective-permute-start.2) | collective-permute-done | bytes 266272 | tf_op jit(solution)/shard_map/ppermute | solution.py:545
  59.4 6.2 %gradient_step.5 = (f32[2,9,520,128]{3,2,1,0:T(8,128)S(1)}, f32[1024,128]{1,0:T(8,128)}, f32[256,128]{1,0:T(8,128)S(1)}, f32[256,128]{1,0:T(8,128)S(1)}, f32[256,128]{1,0:T(8,128)S(1)}, /*index=5*/f32[256,128]{1,0:T(8,128)S(1)}) custom-call(f32[2,9,520,128]{3,2,1,0:T(8,128)S(1)} %get-tuple-element.29.field, f32[4,2,128,128]{3,2,1,0:T(8,128)S(1)} %get-tuple-element.30.lit, ...), custom_call_target="tpu_custom_call" | custom-call | flops 4294967296 | bytes 16777216 | tf_op jit(solution)/shard_map/gradient_step/pallas_call | solution.py:426
  65.7 8.3 %collective-permute-start.8 = (f32[256,128]{1,0:T(8,128)S(1)}, f32[256,128]{1,0:T(8,128)S(1)}, u32[]{:S(2)}, u32[]{:S(2)}) collective-permute-start(f32[256,128]{1,0:T(8,128)S(1)} %get-tuple-element.48), channel_id=1, source_target_pairs={{0,2},{1,3},{2,0},{3,1},{4,6},{5,7},{6,4},{7,5},{8,10},{9,11},{10,... | collective-permute-start | bytes 393224 | tf_op jit(solution)/shard_map/ppermute | solution.py:520
  74.0 0.2 collective-permute-start.7
  74.2 0.3 give_half.1
  74.5 2.9 %collective-permute-done.8 = f32[256,128]{1,0:T(8,128)S(1)} collective-permute-done((f32[256,128]{1,0:T(8,128)S(1)}, f32[256,128]{1,0:T(8,128)S(1)}, u32[]{:S(2)}, u32[]{:S(2)}) %collective-permute-start.8) | collective-permute-done | bytes 131104 | tf_op jit(solution)/shard_map/ppermute | solution.py:520
  77.4 2.4 %collective-permute-done.9 = f32[256,128]{1,0:T(8,128)S(1)} collective-permute-done((f32[256,128]{1,0:T(8,128)S(1)}, f32[256,128]{1,0:T(8,128)S(1)}, u32[]{:S(2)}, u32[]{:S(2)}) %collective-permute-start.9) | collective-permute-done | bytes 131104 | tf_op jit(solution)/shard_map/ppermute | solution.py:520
  80.0 4.3 %collective-permute-start.13 = (bf16[256,128]{1,0:T(8,128)(2,1)S(1)}, bf16[256,128]{1,0:T(8,128)(2,1)S(1)}, u32[]{:S(2)}, u32[]{:S(2)}) collective-permute-start(bf16[256,128]{1,0:T(8,128)(2,1)S(1)} %add_add_fusion.1), channel_id=1, source_target_pairs={{0,12},{1,13},{2,14},{3,15},{4,8},{5,9},{6,10},{7,11},{8,4},{9,5},... | collective-permute-start | bytes 196616 | tf_op jit(solution)/shard_map/ppermute | solution.py:520
  84.3 1.8 %add_half.1 = f32[2,512,512]{2,1,0:T(8,128)} custom-call(f32[2,9,520,128]{3,2,1,0:T(8,128)S(1)} %get-tuple-element.45.total, f32[2,512,512]{2,1,0:T(8,128)S(1)} %collective-permute-done.10.received), custom_call_target="tpu_custom_call" | custom-call | flops 1048576 | bytes 4194304 | tf_op jit(solution)/shard_map/add_half/pallas_call | solution.py:507
  86.1 2.5 %collective-permute-done.12 = bf16[256,128]{1,0:T(8,128)(2,1)S(1)} collective-permute-done((bf16[256,128]{1,0:T(8,128)(2,1)S(1)}, bf16[256,128]{1,0:T(8,128)(2,1)S(1)}, u32[]{:S(2)}, u32[]{:S(2)}) %collective-permute-start.12) | collective-permute-done | bytes 65568 | tf_op jit(solution)/shard_map/ppermute | solution.py:520
  88.7 1.2 %collective-permute-start.15 = (f32[256,128]{1,0:T(8,128)S(1)}, f32[256,128]{1,0:T(8,128)S(1)}, u32[]{:S(2)}, u32[]{:S(2)}) collective-permute-start(f32[256,128]{1,0:T(8,128)S(1)} %add_add_fusion), channel_id=1, source_target_pairs={{0,2},{1,3},{2,0},{3,1},{4,6},{5,7},{6,4},{7,5},{8,10},{9,11},{10,... | collective-permute-start | bytes 393224 | tf_op jit(solution)/shard_map/ppermute | solution.py:520
  89.9 0.6 collective-permute-start.16
  90.6 3.9 %collective-permute-done.14 = f32[256,128]{1,0:T(8,128)S(1)} collective-permute-done((f32[256,128]{1,0:T(8,128)S(1)}, f32[256,128]{1,0:T(8,128)S(1)}, u32[]{:S(2)}, u32[]{:S(2)}) %collective-permute-start.14) | collective-permute-done | bytes 131104 | tf_op jit(solution)/shard_map/ppermute | solution.py:520
  94.5 2.2 %collective-permute-done.15 = f32[256,128]{1,0:T(8,128)S(1)} collective-permute-done((f32[256,128]{1,0:T(8,128)S(1)}, f32[256,128]{1,0:T(8,128)S(1)}, u32[]{:S(2)}, u32[]{:S(2)}) %collective-permute-start.15) | collective-permute-done | bytes 131104 | tf_op jit(solution)/shard_map/ppermute | solution.py:520
  96.7 0.8 pad_maximum_fusion
  (29 shorter events, 0.4 us)
Async XLA Ops:
  0.6 22.3 %copy-start.3 = (f32[2,128,128]{2,1,0:T(8,128)S(1)}, f32[2,128,128]{2,1,0:T(8,128)}, u32[]{:S(2)}) copy-start(f32[2,128,128]{2,1,0:T(8,128)} %constant.19.clone.chirp_ref) | copy-start | bytes 393220
  0.6 22.3 %copy-start.5 = (bf16[2,256,256]{2,1,0:T(8,128)(2,1)S(1)}, bf16[2,256,256]{2,1,0:T(8,128)(2,1)}, u32[]{:S(2)}) copy-start(bf16[2,256,256]{2,1,0:T(8,128)(2,1)} %constant.18.clone.dft_ref) | copy-start | bytes 786436
  4.3 14.6 %collective-permute-start = (bf16[1040,128]{1,0:T(8,128)(2,1)}, bf16[1040,128]{1,0:T(8,128)(2,1)S(1)}, u32[]{:S(2)}, u32[]{:S(2)}) collective-permute-start(bf16[1040,128]{1,0:T(8,128)(2,1)} %get-tuple-element.32), channel_id=1, source_target_pairs={{0,2},{2,0},{4,6},{6,4},{8,10},{10,8},{12,14},{14,12},{1,3},{3,1},... | collective-permute-start | bytes 798728 | tf_op jit(solution)/shard_map/ppermute | solution.py:545
  7.3 12.6 %collective-permute-start.5 = (bf16[1040,128]{1,0:T(8,128)(2,1)}, bf16[1040,128]{1,0:T(8,128)(2,1)S(1)}, u32[]{:S(2)}, u32[]{:S(2)}) collective-permute-start(bf16[1040,128]{1,0:T(8,128)(2,1)} %get-tuple-element.39), channel_id=1, source_target_pairs={{0,4},{2,6},{4,0},{6,2},{8,12},{10,14},{12,8},{14,10},{1,5},{3,7},... | collective-permute-start | bytes 798728 | tf_op jit(solution)/shard_map/ppermute | solution.py:545
  8.8 14.1 %collective-permute-start.6 = (bf16[1040,128]{1,0:T(8,128)(2,1)}, bf16[1040,128]{1,0:T(8,128)(2,1)S(1)}, u32[]{:S(2)}, u32[]{:S(2)}) collective-permute-start(bf16[1040,128]{1,0:T(8,128)(2,1)} %get-tuple-element.40), channel_id=1, source_target_pairs={{0,6},{2,4},{4,2},{6,0},{8,14},{10,12},{12,10},{14,8},{1,7},{3,5},... | collective-permute-start | bytes 798728 | tf_op jit(solution)/shard_map/ppermute | solution.py:545
  8.8 22.9 %collective-permute-start.3 = (bf16[1040,128]{1,0:T(8,128)(2,1)}, bf16[1040,128]{1,0:T(8,128)(2,1)S(1)}, u32[]{:S(2)}, u32[]{:S(2)}) collective-permute-start(bf16[1040,128]{1,0:T(8,128)(2,1)} %get-tuple-element.36), channel_id=1, source_target_pairs={{0,12},{2,14},{4,8},{6,10},{8,4},{10,6},{12,0},{14,2},{1,13},{3,15... | collective-permute-start | bytes 798728 | tf_op jit(solution)/shard_map/ppermute | solution.py:545
  12.8 24.3 %collective-permute-start.4 = (bf16[1040,128]{1,0:T(8,128)(2,1)}, bf16[1040,128]{1,0:T(8,128)(2,1)S(1)}, u32[]{:S(2)}, u32[]{:S(2)}) collective-permute-start(bf16[1040,128]{1,0:T(8,128)(2,1)} %get-tuple-element.37), channel_id=1, source_target_pairs={{0,14},{2,12},{4,10},{6,8},{8,6},{10,4},{12,2},{14,0},{1,15},{3,13... | collective-permute-start | bytes 798728 | tf_op jit(solution)/shard_map/ppermute | solution.py:545
  14.0 2.2 %copy-start = (f32[2,512,1024]{2,1,0:T(8,128)S(1)}, f32[2,512,1024]{2,1,0:T(8,128)}, u32[]{:S(2)}) copy-start(f32[2,512,1024]{2,1,0:T(8,128)} %object_hbm.1) | copy-start | bytes 12582916
  16.2 1.0 %copy-start.1 = (f32[4,2,128,128]{3,2,1,0:T(8,128)S(1)}, f32[4,2,128,128]{3,2,1,0:T(8,128)}, u32[]{:S(2)}) copy-start(f32[4,2,128,128]{3,2,1,0:T(8,128)} %probe_ref.1) | copy-start | bytes 1572868
  17.2 0.9 copy-start.2
  18.2 1.0 copy-start.7
  18.2 1.7 %copy-start.6 = (bf16[1040,128]{1,0:T(8,128)(2,1)S(1)}, bf16[1040,128]{1,0:T(8,128)(2,1)}, u32[]{:S(2)}) copy-start(bf16[1040,128]{1,0:T(8,128)(2,1)} %get-tuple-element.35) | copy-start | bytes 798724
  18.2 4.8 %copy-start.4 = (bf16[1040,128]{1,0:T(8,128)(2,1)S(1)}, bf16[1040,128]{1,0:T(8,128)(2,1)}, u32[]{:S(2)}) copy-start(bf16[1040,128]{1,0:T(8,128)(2,1)} %get-tuple-element.38.rest_0_) | copy-start | bytes 798724
  19.1 36.1 %collective-permute-start.1 = (bf16[1040,128]{1,0:T(8,128)(2,1)S(1)}, bf16[1040,128]{1,0:T(8,128)(2,1)S(1)}, u32[]{:S(2)}, u32[]{:S(2)}) collective-permute-start(bf16[1040,128]{1,0:T(8,128)(2,1)S(1)} %copy-done.7), channel_id=1, source_target_pairs={{0,8},{2,10},{4,12},{6,14},{8,0},{10,2},{12,4},{14,6},{1,9},{3,11}... | collective-permute-start | bytes 798728 | tf_op jit(solution)/shard_map/ppermute | solution.py:545
  19.9 39.5 %collective-permute-start.2 = (bf16[1040,128]{1,0:T(8,128)(2,1)S(1)}, bf16[1040,128]{1,0:T(8,128)(2,1)S(1)}, u32[]{:S(2)}, u32[]{:S(2)}) collective-permute-start(bf16[1040,128]{1,0:T(8,128)(2,1)S(1)} %copy-done.6), channel_id=1, source_target_pairs={{0,10},{2,8},{4,14},{6,12},{8,2},{10,0},{12,6},{14,4},{1,11},{3,9}... | collective-permute-start | bytes 798728 | tf_op jit(solution)/shard_map/ppermute | solution.py:545
  65.7 11.7 %collective-permute-start.8 = (f32[256,128]{1,0:T(8,128)S(1)}, f32[256,128]{1,0:T(8,128)S(1)}, u32[]{:S(2)}, u32[]{:S(2)}) collective-permute-start(f32[256,128]{1,0:T(8,128)S(1)} %get-tuple-element.48), channel_id=1, source_target_pairs={{0,2},{1,3},{2,0},{3,1},{4,6},{5,7},{6,4},{7,5},{8,10},{9,11},{10,... | collective-permute-start | bytes 393224 | tf_op jit(solution)/shard_map/ppermute | solution.py:520
  74.0 5.8 %collective-permute-start.9 = (f32[256,128]{1,0:T(8,128)S(1)}, f32[256,128]{1,0:T(8,128)S(1)}, u32[]{:S(2)}, u32[]{:S(2)}) collective-permute-start(f32[256,128]{1,0:T(8,128)S(1)} %get-tuple-element.49), channel_id=1, source_target_pairs={{0,3},{1,2},{2,1},{3,0},{4,7},{5,6},{6,5},{7,4},{8,11},{9,10},{10,... | collective-permute-start | bytes 393224 | tf_op jit(solution)/shard_map/ppermute | solution.py:520
  74.0 5.8 %collective-permute-start.7 = (f32[256,128]{1,0:T(8,128)S(1)}, f32[256,128]{1,0:T(8,128)S(1)}, u32[]{:S(2)}, u32[]{:S(2)}) collective-permute-start(f32[256,128]{1,0:T(8,128)S(1)} %get-tuple-element.47), channel_id=1, source_target_pairs={{0,1},{1,0},{2,3},{3,2},{4,5},{5,4},{6,7},{7,6},{8,9},{9,8},{10,11... | collective-permute-start | bytes 393224 | tf_op jit(solution)/shard_map/ppermute | solution.py:520
  79.8 4.5 %collective-permute-start.10 = (f32[2,512,512]{2,1,0:T(8,128)S(1)}, f32[2,512,512]{2,1,0:T(8,128)S(1)}, u32[]{:S(2)}, u32[]{:S(2)}) collective-permute-start(f32[2,512,512]{2,1,0:T(8,128)S(1)} %give_half.1), channel_id=1, source_target_pairs={{0,1},{1,0},{2,3},{3,2},{4,5},{5,4},{6,7},{7,6},{8,9},{9,8},{10,11... | collective-permute-start | bytes 6291464 | tf_op jit(solution)/shard_map/ppermute | solution.py:556
  79.8 6.2 %collective-permute-start.11 = (bf16[256,128]{1,0:T(8,128)(2,1)S(1)}, bf16[256,128]{1,0:T(8,128)(2,1)S(1)}, u32[]{:S(2)}, u32[]{:S(2)}) collective-permute-start(bf16[256,128]{1,0:T(8,128)(2,1)S(1)} %add_add_fusion.1), channel_id=1, source_target_pairs={{0,4},{1,5},{2,6},{3,7},{4,0},{5,1},{6,2},{7,3},{8,12},{9,13},{10,... | collective-permute-start | bytes 196616 | tf_op jit(solution)/shard_map/ppermute | solution.py:520
  79.9 8.7 %collective-permute-start.12 = (bf16[256,128]{1,0:T(8,128)(2,1)S(1)}, bf16[256,128]{1,0:T(8,128)(2,1)S(1)}, u32[]{:S(2)}, u32[]{:S(2)}) collective-permute-start(bf16[256,128]{1,0:T(8,128)(2,1)S(1)} %add_add_fusion.1), channel_id=1, source_target_pairs={{0,8},{1,9},{2,10},{3,11},{4,12},{5,13},{6,14},{7,15},{8,0},{9,1},... | collective-permute-start | bytes 196616 | tf_op jit(solution)/shard_map/ppermute | solution.py:520
  80.0 8.6 %collective-permute-start.13 = (bf16[256,128]{1,0:T(8,128)(2,1)S(1)}, bf16[256,128]{1,0:T(8,128)(2,1)S(1)}, u32[]{:S(2)}, u32[]{:S(2)}) collective-permute-start(bf16[256,128]{1,0:T(8,128)(2,1)S(1)} %add_add_fusion.1), channel_id=1, source_target_pairs={{0,12},{1,13},{2,14},{3,15},{4,8},{5,9},{6,10},{7,11},{8,4},{9,5},... | collective-permute-start | bytes 196616 | tf_op jit(solution)/shard_map/ppermute | solution.py:520
  88.6 5.9 %collective-permute-start.14 = (f32[256,128]{1,0:T(8,128)S(1)}, f32[256,128]{1,0:T(8,128)S(1)}, u32[]{:S(2)}, u32[]{:S(2)}) collective-permute-start(f32[256,128]{1,0:T(8,128)S(1)} %add_add_fusion), channel_id=1, source_target_pairs={{0,3},{1,2},{2,1},{3,0},{4,7},{5,6},{6,5},{7,4},{8,11},{9,10},{10,... | collective-permute-start | bytes 393224 | tf_op jit(solution)/shard_map/ppermute | solution.py:520
  88.7 8.0 %collective-permute-start.15 = (f32[256,128]{1,0:T(8,128)S(1)}, f32[256,128]{1,0:T(8,128)S(1)}, u32[]{:S(2)}, u32[]{:S(2)}) collective-permute-start(f32[256,128]{1,0:T(8,128)S(1)} %add_add_fusion), channel_id=1, source_target_pairs={{0,2},{1,3},{2,0},{3,1},{4,6},{5,7},{6,4},{7,5},{8,10},{9,11},{10,... | collective-permute-start | bytes 393224 | tf_op jit(solution)/shard_map/ppermute | solution.py:520
  89.9 6.8 %collective-permute-start.16 = (f32[256,128]{1,0:T(8,128)S(1)}, f32[256,128]{1,0:T(8,128)S(1)}, u32[]{:S(2)}, u32[]{:S(2)}) collective-permute-start(f32[256,128]{1,0:T(8,128)S(1)} %add_add_fusion), channel_id=1, source_target_pairs={{0,1},{1,0},{2,3},{3,2},{4,5},{5,4},{6,7},{7,6},{8,9},{9,8},{10,11... | collective-permute-start | bytes 393224 | tf_op jit(solution)/shard_map/ppermute | solution.py:520

commit v6 on v5

--- a/solution.py
+++ b/solution.py
@@ -550,15 +550,18 @@
     total, grads = sums[0], sums[2:]
 
     devices = tile_count * pos_count
-    inside, across = range(1, SQUARE), range(SQUARE, devices, SQUARE)
-    part = tree_sum([grads[0]] + [from_peer(grads[turn], turn, devices) for turn in inside])
+    across = range(SQUARE, devices, SQUARE)
+    near = grads[0] + from_peer(grads[1], 1, devices)
+    part = near + from_peer(grads[2] + from_peer(grads[3], 1, devices), 2, devices)
     send, part = lax.optimization_barrier((halves(total), part))
     object_step = halves(total, lax.ppermute(send, "pos", [(0, 1), (1, 0)]))
     part = part.astype(jnp.bfloat16)
     received = [from_peer(part, turn, devices) for turn in across]
     object_step, *received = lax.optimization_barrier([object_step] + received)
     part = tree_sum([piece.astype(jnp.float32) for piece in [part] + received])
-    square = [part] + [from_peer(part, turn, devices) for turn in inside]
+    square = [part, from_peer(part, 1, devices)]
+    square += [from_peer(part, 2, devices)]
+    square += [from_peer(square[2], 1, devices)]
     me = lax.axis_index(("tile", "pos"))
     for bit in (1, 2):
         swapped = (me & bit) != 0

time: 97.7 us -> 97.6 us (level)
  the two profiles are of different devices: /device:TPU:0 before, /device:TPU:11 now
where the time goes in v6:
time: 97.6 us; the launch traced here: 97.2 us
  Pallas kernels  44 us (45%)
  starting transfers between devices  27.8 us (28%)
  waiting for transfers between devices  19.3 us (20%)
  local copies, waits for them, and re-layouts  4.34 us (4%)
    pallas_call x3, Pallas kernels, step(): pl.pallas_call(functools.partial(step_kernel, count, capacity, scale, not...  37.5 us
    ppermute x9, starting transfers between devices, from_peer(): return lax.ppermute(array, ('tile', 'pos'), pairs)  17.7 us
    ppermute x9, waiting for transfers between devices, from_peer(): return lax.ppermute(array, ('tile', 'pos'), pairs)  11.1 us
    ppermute x7, starting transfers between devices, on_device(): lax.ppermute(block, 'tile', [(i, i ^ hop) for i in range(tile_count)])  9.19 us
    ppermute x7, waiting for transfers between devices, on_device(): lax.ppermute(block, 'tile', [(i, i ^ hop) for i in range(tile_count)])  7.11 us
    unnamed x16, local copies, waits for them, and re-layouts  4.34 us
    pallas_call x1, Pallas kernels, pack(): pl.pallas_call(functools.partial(pack_kernel, tile_count, capacity), out_...  3.64 us
  transfers between devices with their start and end apart: 17, of which 8 were waited for; matrix products, arithmetic and copies ran while one was open for 0% of the time, Pallas kernels for 31%

profile of v6, /device:TPU:11, one launch (start us, length us, event | category | flops | bytes accessed | tf_op | source)
XLA Modules:
  0.0 97.2 jit_solution(2909924934698608598)
XLA Ops:
  0.7 3.6 %pack_patterns.1 = (bf16[1040,128]{1,0:T(8,128)(2,1)}, bf16[1040,128]{1,0:T(8,128)(2,1)}, bf16[1040,128]{1,0:T(8,128)(2,1)}, bf16[1040,128]{1,0:T(8,128)(2,1)}, ...) custom-call(s32[32]{0:T(128)} %bitcast.3, ...), custom_call_target="tpu_custom_call" | custom-call | tf_op jit(solution)/shard_map/pack_patterns/pallas_call | solution.py:82
  4.3 1.2 %collective-permute-start = (bf16[1040,128]{1,0:T(8,128)(2,1)}, bf16[1040,128]{1,0:T(8,128)(2,1)S(1)}, u32[]{:S(2)}, u32[]{:S(2)}) collective-permute-start(bf16[1040,128]{1,0:T(8,128)(2,1)} %get-tuple-element.32), channel_id=1, source_target_pairs={{0,2},{2,0},{4,6},{6,4},{8,10},{10,8},{12,14},{14,12},{1,3},{3,1},... | collective-permute-start | bytes 798728 | tf_op jit(solution)/shard_map/ppermute | solution.py:545
  5.7 1.2 %collective-permute-start.6 = (bf16[1040,128]{1,0:T(8,128)(2,1)}, bf16[1040,128]{1,0:T(8,128)(2,1)S(1)}, u32[]{:S(2)}, u32[]{:S(2)}) collective-permute-start(bf16[1040,128]{1,0:T(8,128)(2,1)} %get-tuple-element.40), channel_id=1, source_target_pairs={{0,6},{2,4},{4,2},{6,0},{8,14},{10,12},{12,10},{14,8},{1,7},{3,5},... | collective-permute-start | bytes 798728 | tf_op jit(solution)/shard_map/ppermute | solution.py:545
  6.9 1.3 %collective-permute-start.3 = (bf16[1040,128]{1,0:T(8,128)(2,1)}, bf16[1040,128]{1,0:T(8,128)(2,1)S(1)}, u32[]{:S(2)}, u32[]{:S(2)}) collective-permute-start(bf16[1040,128]{1,0:T(8,128)(2,1)} %get-tuple-element.36), channel_id=1, source_target_pairs={{0,12},{2,14},{4,8},{6,10},{8,4},{10,6},{12,0},{14,2},{1,13},{3,15... | collective-permute-start | bytes 798728 | tf_op jit(solution)/shard_map/ppermute | solution.py:545
  8.2 1.1 %collective-permute-start.4 = (bf16[1040,128]{1,0:T(8,128)(2,1)}, bf16[1040,128]{1,0:T(8,128)(2,1)S(1)}, u32[]{:S(2)}, u32[]{:S(2)}) collective-permute-start(bf16[1040,128]{1,0:T(8,128)(2,1)} %get-tuple-element.37), channel_id=1, source_target_pairs={{0,14},{2,12},{4,10},{6,8},{8,6},{10,4},{12,2},{14,0},{1,15},{3,13... | collective-permute-start | bytes 798728 | tf_op jit(solution)/shard_map/ppermute | solution.py:545
  9.4 2.2 %copy-done = f32[2,512,1024]{2,1,0:T(8,128)S(1)} copy-done((f32[2,512,1024]{2,1,0:T(8,128)S(1)}, f32[2,512,1024]{2,1,0:T(8,128)}, u32[]{:S(2)}) %copy-start) | copy-done | bytes 4194328
  11.6 1.0 %copy-done.1 = f32[4,2,128,128]{3,2,1,0:T(8,128)S(1)} copy-done((f32[4,2,128,128]{3,2,1,0:T(8,128)S(1)}, f32[4,2,128,128]{3,2,1,0:T(8,128)}, u32[]{:S(2)}) %copy-start.1) | copy-done | bytes 524312
  12.6 0.9 copy-done.2
  13.5 0.7 prepare_strip.1
  14.3 0.2 copy-done.7
  14.5 4.1 %collective-permute-start.1 = (bf16[1040,128]{1,0:T(8,128)(2,1)S(1)}, bf16[1040,128]{1,0:T(8,128)(2,1)S(1)}, u32[]{:S(2)}, u32[]{:S(2)}) collective-permute-start(bf16[1040,128]{1,0:T(8,128)(2,1)S(1)} %copy-done.7), channel_id=1, source_target_pairs={{0,8},{2,10},{4,12},{6,14},{8,0},{10,2},{12,4},{14,6},{1,9},{3,11}... | collective-permute-start | bytes 798728 | tf_op jit(solution)/shard_map/ppermute | solution.py:545
  18.6 1.5 %collective-permute-done.6.rest_3_ = bf16[1040,128]{1,0:T(8,128)(2,1)S(1)} collective-permute-done((bf16[1040,128]{1,0:T(8,128)(2,1)}, bf16[1040,128]{1,0:T(8,128)(2,1)S(1)}, u32[]{:S(2)}, u32[]{:S(2)}) %collective-permute-start.6) | collective-permute-done | bytes 266272 | tf_op jit(solution)/shard_map/ppermute | solution.py:545
  20.1 17.2 %gradient_step.3 = (f32[2,9,520,128]{3,2,1,0:T(8,128)S(1)}, f32[1024,128]{1,0:T(8,128)S(1)}) custom-call(f32[2,9,520,128]{3,2,1,0:T(8,128)S(1)} %get-tuple-element.29.field, f32[4,2,128,128]{3,2,1,0:T(8,128)S(1)} %get-tuple-element.30.lit, bf16[2,256,256]{2,1,0:T(8,128)(2,1)S(1)} %copy-done.5, f32[2,128,128]{2,1,0:T(8,128)S(1)} %copy-done.3, ...), custom_call_target="tpu_custom_call" | custom-call | flops 8589934592 | bytes 16777216 | tf_op jit(solution)/shard_map/gradient_step/pallas_call | solution.py:426
  37.4 10.3 %gradient_step.4 = (f32[2,9,520,128]{3,2,1,0:T(8,128)S(1)}, f32[1024,128]{1,0:T(8,128)S(1)}) custom-call(f32[2,9,520,128]{3,2,1,0:T(8,128)S(1)} %get-tuple-element.29.field, f32[4,2,128,128]{3,2,1,0:T(8,128)S(1)} %get-tuple-element.30.lit, bf16[2,256,256]{2,1,0:T(8,128)(2,1)S(1)} %copy-done.5, f32[2,128,128]{2,1,0:T(8,128)S(1)} %copy-done.3, ...), custom_call_target="tpu_custom_call" | custom-call | flops 4294967296 | bytes 16777216 | tf_op jit(solution)/shard_map/gradient_step/pallas_call | solution.py:426
  47.7 5.6 %collective-permute-done.2.rest_1_ = bf16[1040,128]{1,0:T(8,128)(2,1)S(1)} collective-permute-done((bf16[1040,128]{1,0:T(8,128)(2,1)S(1)}, bf16[1040,128]{1,0:T(8,128)(2,1)S(1)}, u32[]{:S(2)}, u32[]{:S(2)}) %collective-permute-start.2) | collective-permute-done | bytes 266272 | tf_op jit(solution)/shard_map/ppermute | solution.py:545
  53.3 9.9 %gradient_step.5 = (f32[2,9,520,128]{3,2,1,0:T(8,128)S(1)}, f32[1024,128]{1,0:T(8,128)}, f32[256,128]{1,0:T(8,128)S(1)}, f32[256,128]{1,0:T(8,128)S(1)}, f32[256,128]{1,0:T(8,128)S(1)}, /*index=5*/f32[256,128]{1,0:T(8,128)S(1)}) custom-call(f32[2,9,520,128]{3,2,1,0:T(8,128)S(1)} %get-tuple-element.29.field, f32[4,2,128,128]{3,2,1,0:T(8,128)S(1)} %get-tuple-element.30.lit, ...), custom_call_target="tpu_custom_call" | custom-call | flops 4294967296 | bytes 16777216 | tf_op jit(solution)/shard_map/gradient_step/pallas_call | solution.py:426
  63.2 6.6 %collective-permute-start.8 = (f32[256,128]{1,0:T(8,128)S(1)}, f32[256,128]{1,0:T(8,128)S(1)}, u32[]{:S(2)}, u32[]{:S(2)}) collective-permute-start(f32[256,128]{1,0:T(8,128)S(1)} %get-tuple-element.49), channel_id=1, source_target_pairs={{0,1},{1,0},{2,3},{3,2},{4,5},{5,4},{6,7},{7,6},{8,9},{9,8},{10,11... | collective-permute-start | bytes 393224 | tf_op jit(solution)/shard_map/ppermute | solution.py:520
  69.9 0.9 collective-permute-done.8
  70.8 4.7 %collective-permute-start.9 = (f32[256,128]{1,0:T(8,128)S(1)}, f32[256,128]{1,0:T(8,128)S(1)}, u32[]{:S(2)}, u32[]{:S(2)}) collective-permute-start(f32[256,128]{1,0:T(8,128)S(1)} %add.22), channel_id=1, source_target_pairs={{0,2},{1,3},{2,0},{3,1},{4,6},{5,7},{6,4},{7,5},{8,10},{9,11},{10,... | collective-permute-start | bytes 393224 | tf_op jit(solution)/shard_map/ppermute | solution.py:520
  75.6 0.3 give_half.1
  75.9 3.2 %collective-permute-done.9 = f32[256,128]{1,0:T(8,128)S(1)} collective-permute-done((f32[256,128]{1,0:T(8,128)S(1)}, f32[256,128]{1,0:T(8,128)S(1)}, u32[]{:S(2)}, u32[]{:S(2)}) %collective-permute-start.9) | collective-permute-done | bytes 131104 | tf_op jit(solution)/shard_map/ppermute | solution.py:520
  79.2 0.9 collective-permute-start.10
  80.1 2.7 %collective-permute-start.13 = (bf16[256,128]{1,0:T(8,128)(2,1)S(1)}, bf16[256,128]{1,0:T(8,128)(2,1)S(1)}, u32[]{:S(2)}, u32[]{:S(2)}) collective-permute-start(bf16[256,128]{1,0:T(8,128)(2,1)S(1)} %add_add_fusion.1), channel_id=1, source_target_pairs={{0,12},{1,13},{2,14},{3,15},{4,8},{5,9},{6,10},{7,11},{8,4},{9,5},... | collective-permute-start | bytes 196616 | tf_op jit(solution)/shard_map/ppermute | solution.py:520
  82.8 1.1 %collective-permute-done.10.received = f32[2,512,512]{2,1,0:T(8,128)S(1)} collective-permute-done((f32[2,512,512]{2,1,0:T(8,128)S(1)}, f32[2,512,512]{2,1,0:T(8,128)S(1)}, u32[]{:S(2)}, u32[]{:S(2)}) %collective-permute-start.10) | collective-permute-done | bytes 2097184 | tf_op jit(solution)/shard_map/ppermute | solution.py:557
  83.9 1.8 %add_half.1 = f32[2,512,512]{2,1,0:T(8,128)} custom-call(f32[2,9,520,128]{3,2,1,0:T(8,128)S(1)} %get-tuple-element.45.total, f32[2,512,512]{2,1,0:T(8,128)S(1)} %collective-permute-done.10.received), custom_call_target="tpu_custom_call" | custom-call | flops 1048576 | bytes 4194304 | tf_op jit(solution)/shard_map/add_half/pallas_call | solution.py:507
  85.7 3.6 %collective-permute-done.13 = bf16[256,128]{1,0:T(8,128)(2,1)S(1)} collective-permute-done((bf16[256,128]{1,0:T(8,128)(2,1)S(1)}, bf16[256,128]{1,0:T(8,128)(2,1)S(1)}, u32[]{:S(2)}, u32[]{:S(2)}) %collective-permute-start.13) | collective-permute-done | bytes 65568 | tf_op jit(solution)/shard_map/ppermute | solution.py:520
  89.3 1.5 %collective-permute-start.14 = (f32[256,128]{1,0:T(8,128)S(1)}, f32[256,128]{1,0:T(8,128)S(1)}, u32[]{:S(2)}, u32[]{:S(2)}) collective-permute-start(f32[256,128]{1,0:T(8,128)S(1)} %add_add_fusion), channel_id=1, source_target_pairs={{0,2},{1,3},{2,0},{3,1},{4,6},{5,7},{6,4},{7,5},{8,10},{9,11},{10,... | collective-permute-start | bytes 393224 | tf_op jit(solution)/shard_map/ppermute | solution.py:520
  90.8 0.8 collective-permute-start.16
  91.6 2.4 %collective-permute-done.14 = f32[256,128]{1,0:T(8,128)S(1)} collective-permute-done((f32[256,128]{1,0:T(8,128)S(1)}, f32[256,128]{1,0:T(8,128)S(1)}, u32[]{:S(2)}, u32[]{:S(2)}) %collective-permute-start.14) | collective-permute-done | bytes 131104 | tf_op jit(solution)/shard_map/ppermute | solution.py:520
  94.0 1.3 %collective-permute-start.15 = (f32[256,128]{1,0:T(8,128)S(1)}, f32[256,128]{1,0:T(8,128)S(1)}, u32[]{:S(2)}, u32[]{:S(2)}) collective-permute-start(f32[256,128]{1,0:T(8,128)S(1)} %collective-permute-done.14), channel_id=1, source_target_pairs={{0,1},{1,0},{2,3},{3,2},{4,5},{5,4},{6,7},{7,6},{8,9},{9,8},{10,11... | collective-permute-start | bytes 393224 | tf_op jit(solution)/shard_map/ppermute | solution.py:520
  95.3 1.0 %collective-permute-done.15 = f32[256,128]{1,0:T(8,128)S(1)} collective-permute-done((f32[256,128]{1,0:T(8,128)S(1)}, f32[256,128]{1,0:T(8,128)S(1)}, u32[]{:S(2)}, u32[]{:S(2)}) %collective-permute-start.15) | collective-permute-done | bytes 131104 | tf_op jit(solution)/shard_map/ppermute | solution.py:520
  96.3 0.8 pad_maximum_fusion
  (30 shorter events, 0.4 us)
Async XLA Ops:
  0.6 19.5 %copy-start.3 = (f32[2,128,128]{2,1,0:T(8,128)S(1)}, f32[2,128,128]{2,1,0:T(8,128)}, u32[]{:S(2)}) copy-start(f32[2,128,128]{2,1,0:T(8,128)} %constant.19.clone.chirp_ref) | copy-start | bytes 393220
  0.6 19.5 %copy-start.5 = (bf16[2,256,256]{2,1,0:T(8,128)(2,1)S(1)}, bf16[2,256,256]{2,1,0:T(8,128)(2,1)}, u32[]{:S(2)}) copy-start(bf16[2,256,256]{2,1,0:T(8,128)(2,1)} %constant.18.clone.dft_ref) | copy-start | bytes 786436
  4.3 10.0 %collective-permute-start = (bf16[1040,128]{1,0:T(8,128)(2,1)}, bf16[1040,128]{1,0:T(8,128)(2,1)S(1)}, u32[]{:S(2)}, u32[]{:S(2)}) collective-permute-start(bf16[1040,128]{1,0:T(8,128)(2,1)} %get-tuple-element.32), channel_id=1, source_target_pairs={{0,2},{2,0},{4,6},{6,4},{8,10},{10,8},{12,14},{14,12},{1,3},{3,1},... | collective-permute-start | bytes 798728 | tf_op jit(solution)/shard_map/ppermute | solution.py:545
  5.5 13.0 %collective-permute-start.5 = (bf16[1040,128]{1,0:T(8,128)(2,1)}, bf16[1040,128]{1,0:T(8,128)(2,1)S(1)}, u32[]{:S(2)}, u32[]{:S(2)}) collective-permute-start(bf16[1040,128]{1,0:T(8,128)(2,1)} %get-tuple-element.39), channel_id=1, source_target_pairs={{0,4},{2,6},{4,0},{6,2},{8,12},{10,14},{12,8},{14,10},{1,5},{3,7},... | collective-permute-start | bytes 798728 | tf_op jit(solution)/shard_map/ppermute | solution.py:545
  5.7 14.4 %collective-permute-start.6 = (bf16[1040,128]{1,0:T(8,128)(2,1)}, bf16[1040,128]{1,0:T(8,128)(2,1)S(1)}, u32[]{:S(2)}, u32[]{:S(2)}) collective-permute-start(bf16[1040,128]{1,0:T(8,128)(2,1)} %get-tuple-element.40), channel_id=1, source_target_pairs={{0,6},{2,4},{4,2},{6,0},{8,14},{10,12},{12,10},{14,8},{1,7},{3,5},... | collective-permute-start | bytes 798728 | tf_op jit(solution)/shard_map/ppermute | solution.py:545
  6.9 30.4 %collective-permute-start.3 = (bf16[1040,128]{1,0:T(8,128)(2,1)}, bf16[1040,128]{1,0:T(8,128)(2,1)S(1)}, u32[]{:S(2)}, u32[]{:S(2)}) collective-permute-start(bf16[1040,128]{1,0:T(8,128)(2,1)} %get-tuple-element.36), channel_id=1, source_target_pairs={{0,12},{2,14},{4,8},{6,10},{8,4},{10,6},{12,0},{14,2},{1,13},{3,15... | collective-permute-start | bytes 798728 | tf_op jit(solution)/shard_map/ppermute | solution.py:545
  8.2 29.1 %collective-permute-start.4 = (bf16[1040,128]{1,0:T(8,128)(2,1)}, bf16[1040,128]{1,0:T(8,128)(2,1)S(1)}, u32[]{:S(2)}, u32[]{:S(2)}) collective-permute-start(bf16[1040,128]{1,0:T(8,128)(2,1)} %get-tuple-element.37), channel_id=1, source_target_pairs={{0,14},{2,12},{4,10},{6,8},{8,6},{10,4},{12,2},{14,0},{1,15},{3,13... | collective-permute-start | bytes 798728 | tf_op jit(solution)/shard_map/ppermute | solution.py:545
  9.4 2.2 %copy-start = (f32[2,512,1024]{2,1,0:T(8,128)S(1)}, f32[2,512,1024]{2,1,0:T(8,128)}, u32[]{:S(2)}) copy-start(f32[2,512,1024]{2,1,0:T(8,128)} %object_hbm.1) | copy-start | bytes 12582916
  11.6 1.0 %copy-start.1 = (f32[4,2,128,128]{3,2,1,0:T(8,128)S(1)}, f32[4,2,128,128]{3,2,1,0:T(8,128)}, u32[]{:S(2)}) copy-start(f32[4,2,128,128]{3,2,1,0:T(8,128)} %probe_ref.1) | copy-start | bytes 1572868
  12.6 0.9 copy-start.2
  13.5 1.0 copy-start.7
  13.5 5.1 %copy-start.6 = (bf16[1040,128]{1,0:T(8,128)(2,1)S(1)}, bf16[1040,128]{1,0:T(8,128)(2,1)}, u32[]{:S(2)}) copy-start(bf16[1040,128]{1,0:T(8,128)(2,1)} %get-tuple-element.35) | copy-start | bytes 798724
  13.5 6.6 %copy-start.4 = (bf16[1040,128]{1,0:T(8,128)(2,1)S(1)}, bf16[1040,128]{1,0:T(8,128)(2,1)}, u32[]{:S(2)}) copy-start(bf16[1040,128]{1,0:T(8,128)(2,1)} %get-tuple-element.38.rest_0_) | copy-start | bytes 798724
  14.5 33.2 %collective-permute-start.1 = (bf16[1040,128]{1,0:T(8,128)(2,1)S(1)}, bf16[1040,128]{1,0:T(8,128)(2,1)S(1)}, u32[]{:S(2)}, u32[]{:S(2)}) collective-permute-start(bf16[1040,128]{1,0:T(8,128)(2,1)S(1)} %copy-done.7), channel_id=1, source_target_pairs={{0,8},{2,10},{4,12},{6,14},{8,0},{10,2},{12,4},{14,6},{1,9},{3,11}... | collective-permute-start | bytes 798728 | tf_op jit(solution)/shard_map/ppermute | solution.py:545
  18.6 34.7 %collective-permute-start.2 = (bf16[1040,128]{1,0:T(8,128)(2,1)S(1)}, bf16[1040,128]{1,0:T(8,128)(2,1)S(1)}, u32[]{:S(2)}, u32[]{:S(2)}) collective-permute-start(bf16[1040,128]{1,0:T(8,128)(2,1)S(1)} %copy-done.6), channel_id=1, source_target_pairs={{0,10},{2,8},{4,14},{6,12},{8,2},{10,0},{12,6},{14,4},{1,11},{3,9}... | collective-permute-start | bytes 798728 | tf_op jit(solution)/shard_map/ppermute | solution.py:545
  63.2 7.6 %collective-permute-start.8 = (f32[256,128]{1,0:T(8,128)S(1)}, f32[256,128]{1,0:T(8,128)S(1)}, u32[]{:S(2)}, u32[]{:S(2)}) collective-permute-start(f32[256,128]{1,0:T(8,128)S(1)} %get-tuple-element.49), channel_id=1, source_target_pairs={{0,1},{1,0},{2,3},{3,2},{4,5},{5,4},{6,7},{7,6},{8,9},{9,8},{10,11... | collective-permute-start | bytes 393224 | tf_op jit(solution)/shard_map/ppermute | solution.py:520
  69.8 6.1 %collective-permute-start.7 = (f32[256,128]{1,0:T(8,128)S(1)}, f32[256,128]{1,0:T(8,128)S(1)}, u32[]{:S(2)}, u32[]{:S(2)}) collective-permute-start(f32[256,128]{1,0:T(8,128)S(1)} %get-tuple-element.47), channel_id=1, source_target_pairs={{0,1},{1,0},{2,3},{3,2},{4,5},{5,4},{6,7},{7,6},{8,9},{9,8},{10,11... | collective-permute-start | bytes 393224 | tf_op jit(solution)/shard_map/ppermute | solution.py:520
  70.8 8.3 %collective-permute-start.9 = (f32[256,128]{1,0:T(8,128)S(1)}, f32[256,128]{1,0:T(8,128)S(1)}, u32[]{:S(2)}, u32[]{:S(2)}) collective-permute-start(f32[256,128]{1,0:T(8,128)S(1)} %add.22), channel_id=1, source_target_pairs={{0,2},{1,3},{2,0},{3,1},{4,6},{5,7},{6,4},{7,5},{8,10},{9,11},{10,... | collective-permute-start | bytes 393224 | tf_op jit(solution)/shard_map/ppermute | solution.py:520
  79.2 4.7 %collective-permute-start.10 = (f32[2,512,512]{2,1,0:T(8,128)S(1)}, f32[2,512,512]{2,1,0:T(8,128)S(1)}, u32[]{:S(2)}, u32[]{:S(2)}) collective-permute-start(f32[2,512,512]{2,1,0:T(8,128)S(1)} %give_half.1), channel_id=1, source_target_pairs={{0,1},{1,0},{2,3},{3,2},{4,5},{5,4},{6,7},{7,6},{8,9},{9,8},{10,11... | collective-permute-start | bytes 6291464 | tf_op jit(solution)/shard_map/ppermute | solution.py:557
  80.1 5.6 %collective-permute-start.11 = (bf16[256,128]{1,0:T(8,128)(2,1)S(1)}, bf16[256,128]{1,0:T(8,128)(2,1)S(1)}, u32[]{:S(2)}, u32[]{:S(2)}) collective-permute-start(bf16[256,128]{1,0:T(8,128)(2,1)S(1)} %add_add_fusion.1), channel_id=1, source_target_pairs={{0,4},{1,5},{2,6},{3,7},{4,0},{5,1},{6,2},{7,3},{8,12},{9,13},{10,... | collective-permute-start | bytes 196616 | tf_op jit(solution)/shard_map/ppermute | solution.py:520
  80.1 5.6 %collective-permute-start.12 = (bf16[256,128]{1,0:T(8,128)(2,1)S(1)}, bf16[256,128]{1,0:T(8,128)(2,1)S(1)}, u32[]{:S(2)}, u32[]{:S(2)}) collective-permute-start(bf16[256,128]{1,0:T(8,128)(2,1)S(1)} %add_add_fusion.1), channel_id=1, source_target_pairs={{0,8},{1,9},{2,10},{3,11},{4,12},{5,13},{6,14},{7,15},{8,0},{9,1},... | collective-permute-start | bytes 196616 | tf_op jit(solution)/shard_map/ppermute | solution.py:520
  80.1 9.1 %collective-permute-start.13 = (bf16[256,128]{1,0:T(8,128)(2,1)S(1)}, bf16[256,128]{1,0:T(8,128)(2,1)S(1)}, u32[]{:S(2)}, u32[]{:S(2)}) collective-permute-start(bf16[256,128]{1,0:T(8,128)(2,1)S(1)} %add_add_fusion.1), channel_id=1, source_target_pairs={{0,12},{1,13},{2,14},{3,15},{4,8},{5,9},{6,10},{7,11},{8,4},{9,5},... | collective-permute-start | bytes 196616 | tf_op jit(solution)/shard_map/ppermute | solution.py:520
  89.3 4.7 %collective-permute-start.14 = (f32[256,128]{1,0:T(8,128)S(1)}, f32[256,128]{1,0:T(8,128)S(1)}, u32[]{:S(2)}, u32[]{:S(2)}) collective-permute-start(f32[256,128]{1,0:T(8,128)S(1)} %add_add_fusion), channel_id=1, source_target_pairs={{0,2},{1,3},{2,0},{3,1},{4,6},{5,7},{6,4},{7,5},{8,10},{9,11},{10,... | collective-permute-start | bytes 393224 | tf_op jit(solution)/shard_map/ppermute | solution.py:520
  90.8 4.5 %collective-permute-start.16 = (f32[256,128]{1,0:T(8,128)S(1)}, f32[256,128]{1,0:T(8,128)S(1)}, u32[]{:S(2)}, u32[]{:S(2)}) collective-permute-start(f32[256,128]{1,0:T(8,128)S(1)} %add_add_fusion), channel_id=1, source_target_pairs={{0,1},{1,0},{2,3},{3,2},{4,5},{5,4},{6,7},{7,6},{8,9},{9,8},{10,11... | collective-permute-start | bytes 393224 | tf_op jit(solution)/shard_map/ppermute | solution.py:520
  94.0 2.3 %collective-permute-start.15 = (f32[256,128]{1,0:T(8,128)S(1)}, f32[256,128]{1,0:T(8,128)S(1)}, u32[]{:S(2)}, u32[]{:S(2)}) collective-permute-start(f32[256,128]{1,0:T(8,128)S(1)} %collective-permute-done.14), channel_id=1, source_target_pairs={{0,1},{1,0},{2,3},{3,2},{4,5},{5,4},{6,7},{7,6},{8,9},{9,8},{10,11... | collective-permute-start | bytes 393224 | tf_op jit(solution)/shard_map/ppermute | solution.py:520
